TPU v7x, 32 devices: a whole 2x2x4 slice. The times are simulated.
32 devices in a mesh: head: 2 (over x), blk: 16 (over z, y, core).
Axes of the slice: x: 2, y: 2, z: 4, core: 2. Of those that a mesh axis runs over, the one named last changes fastest.
Arguments:
- states: bfloat16 [16, 2, 128, 1536], P('blk', 'head'), may hold values from -6 to 6
- teacher: bfloat16 [16, 2, 128, 1536], P('blk', 'head'), may hold values from -6 to 6
- valid: int32 [16, 2, 128], P('blk', 'head'), may hold values from 0 to 1
- routes: int32 [16, 2, 128, 4], P('blk', 'head'), may hold values from 0 to 7, all different within a row; in each aligned block of 128 rows (0 to 127, 128 to 255, ..., all dimensions but the last counted through in order) at most 96 rows name the same one
- gates: float32 [16, 2, 128, 4], P('blk', 'head'), may hold values from 0.1 to 0.4
- doc_starts: int32 [3], replicated, may hold values from 0 to 4095, as said below
- norm_one: bfloat16 [1536], P(('head', 'blk')), may hold values from 0.5 to 1.5
- w_query: bfloat16 [1536, 1536], P(('head', 'blk')), may hold values from -0.15625 to 0.15625
- key_weight: bfloat16 [1536, 256], P(('head', 'blk')), may hold values from -0.15625 to 0.15625
- value_weight: bfloat16 [1536, 256], P(('head', 'blk')), may hold values from -0.15625 to 0.15625
- w_output: bfloat16 [1536, 1536], P(('head', 'blk')), may hold values from -1.25 to 1.25
- norm_two: bfloat16 [1536], P(('head', 'blk')), may hold values from 0.5 to 1.5
- expert_in: bfloat16 [8, 1536, 1536], P(None, ('head', 'blk')), may hold values from -0.15625 to 0.15625
- expert_out: bfloat16 [8, 768, 1536], P(None, ('head', 'blk')), may hold values from -0.625 to 0.625
Outputs:
- final_states: bfloat16 [16, 2, 128, 1536], P('blk', 'head')
- loss: float32 [], replicated
- grad_states: float32 [16, 2, 128, 1536], P('blk', 'head')
- grad_norm_one: float32 [1536], P(('head', 'blk'))
- grad_query: float32 [1536, 1536], P(('head', 'blk'))
- grad_key: float32 [1536, 256], P(('head', 'blk'))
- grad_value: float32 [1536, 256], P(('head', 'blk'))
- grad_output: float32 [1536, 1536], P(('head', 'blk'))
- grad_norm_two: float32 [1536], P(('head', 'blk'))
- grad_expert_in: float32 [8, 1536, 1536], P(None, ('head', 'blk'))
- grad_expert_out: float32 [8, 768, 1536], P(None, ('head', 'blk'))
Inputs may be any that keep to these rules, and one draw needn't show every extreme that they name: `routes`: at most 96 of one device's rows name one expert, and some expert reaches 96. `doc_starts`: strictly rising, the first is 0.
All inputs are finite; a program needn't handle non-finite values.
Results may differ from a plain program's by a relative error of at most 0.019.
Values may be sent and summed in bfloat16 or wider, within the bound.
A program may use at most 448 MiB of HBM per device.

v0:
```python
import jax
import jax.numpy as jnp
from jax import lax
from jax.sharding import PartitionSpec as P

QUERY_HEADS = 12
KEY_VALUE_HEADS = 2
HEAD_SIZE = 128
TOP = 4
E = 8
CAP = 96


ROTARY_BASE = 10000.0
FLOOR_SCORE = -1e30


def product(left, right):
    return jnp.dot(left, right, preferred_element_type=jnp.float32)


def rms_norm(values, gain):
    scale = lax.rsqrt(jnp.mean(values * values, axis=-1, keepdims=True) + 1e-06)
    return values * scale * gain


def rotary_apply(values, where, sign):
    half = values.shape[-1] // 2
    freq = ROTARY_BASE ** (-jnp.arange(half).astype(jnp.float32) / half)
    angle = where.astype(jnp.float32)[:, None] * freq[None, :]
    cosine = jnp.cos(angle)[:, None, :]
    sine = jnp.sin(angle)[:, None, :] * sign
    first = values[..., :half]
    second = values[..., half:]
    return jnp.concatenate(
        [first * cosine - second * sine, second * cosine + first * sine], axis=-1
    )


def doc_layout(position_index, doc_starts):
    inside = (position_index[:, None] >= doc_starts[None, :]).astype(jnp.int32)
    document_segment = jnp.sum(inside, axis=-1) - 1
    begin = jnp.max(jnp.where(inside > 0, doc_starts[None, :], 0), axis=-1)
    return (document_segment, position_index - begin)


def gated(pair):
    half = pair.shape[-1] // 2
    return jax.nn.gelu(pair[..., :half], approximate=True) * pair[..., half:]


def in_blocks(step_fn, carry, piece, rows):
    count_blocks = piece[0].shape[0] // rows

    def turn(number, state):
        part = tuple((lax.dynamic_slice_in_dim(item, number * rows, rows, 0) for item in piece))
        return step_fn(state, part, number * rows)

    return lax.fori_loop(0, count_blocks, turn, carry)


def per_device(
    states,
    teacher,
    valid,
    routes,
    gates,
    doc_starts,
    norm_one,
    w_query,
    key_weight,
    value_weight,
    w_output,
    norm_two,
    expert_in,
    expert_out,
):
    count_per_token = states.shape[2]
    width = states.shape[3]
    pairs = lax.axis_size("head")
    blocks = lax.axis_size("blk")
    rows = count_per_token * pairs
    span = rows * blocks
    head_group = QUERY_HEADS // KEY_VALUE_HEADS
    scale = HEAD_SIZE ** (-0.5)
    highest = lax.Precision.HIGHEST
    block_index = lax.axis_index("blk")
    pair_index = lax.axis_index("head")
    token_index = (block_index * pairs + pair_index) * count_per_token + jnp.arange(
        count_per_token, dtype=jnp.int32
    )
    unused_segment, token_position = doc_layout(token_index, doc_starts)
    query_index = block_index * rows + jnp.arange(rows, dtype=jnp.int32)
    query_segment, query_where = doc_layout(query_index, doc_starts)
    last_query = block_index * rows + rows - 1
    inputs = states.reshape(count_per_token, width).astype(jnp.float32)
    target = teacher.reshape(count_per_token, width).astype(jnp.float32)
    keep_mask = valid.reshape(count_per_token).astype(jnp.float32)
    route_rows = routes.reshape(count_per_token, TOP)
    gate_rows = gates.reshape(count_per_token, TOP)
    query_w, key_w, value_w, out_w, gain_low_one, gain_low_two = (
        lax.all_gather(w_query, ("head", "blk"), axis=0, tiled=True),
        lax.all_gather(key_weight, ("head", "blk"), axis=0, tiled=True),
        lax.all_gather(value_weight, ("head", "blk"), axis=0, tiled=True),
        lax.all_gather(w_output, ("head", "blk"), axis=0, tiled=True),
        lax.all_gather(norm_one, ("head", "blk"), axis=0, tiled=True),
        lax.all_gather(norm_two, ("head", "blk"), axis=0, tiled=True),
    )
    gain_one = gain_low_one.astype(jnp.float32)
    gain_two = gain_low_two.astype(jnp.float32)
    normed_one = rms_norm(inputs, gain_one)
    normed_low = normed_one.astype(jnp.bfloat16)
    query_lin = product(normed_low, query_w)
    key_linear = product(normed_low, key_w)
    value_linear = product(normed_low, value_w)
    query_rotated = rotary_apply(
        query_lin.reshape(count_per_token, QUERY_HEADS, HEAD_SIZE), token_position, 1.0
    )
    key_rotated = rotary_apply(
        key_linear.reshape(count_per_token, KEY_VALUE_HEADS, HEAD_SIZE), token_position, 1.0
    )
    query_outgoing = query_rotated.astype(jnp.bfloat16).reshape(
        count_per_token, KEY_VALUE_HEADS, head_group * HEAD_SIZE
    )
    key_send = key_rotated.astype(jnp.bfloat16)
    value_outgoing = value_linear.astype(jnp.bfloat16).reshape(
        count_per_token, KEY_VALUE_HEADS, HEAD_SIZE
    )
    query_grp, key_grp, value_grp = (
        lax.all_to_all(query_outgoing, "head", split_axis=1, concat_axis=0, tiled=True),
        lax.all_to_all(key_send, "head", split_axis=1, concat_axis=0, tiled=True),
        lax.all_to_all(value_outgoing, "head", split_axis=1, concat_axis=0, tiled=True),
    )
    query_heads = query_grp.reshape(rows, head_group, HEAD_SIZE)
    key_rows = key_grp.reshape(rows, HEAD_SIZE)
    value_rows = value_grp.reshape(rows, HEAD_SIZE)

    def scores_for(keys, start):
        block_size = keys.shape[0]
        key_index = start + jnp.arange(block_size, dtype=jnp.int32)
        key_segment, unused_where = doc_layout(key_index, doc_starts)
        allowed = (key_index[None, :] <= query_index[:, None]) & (
            key_segment[None, :] == query_segment[:, None]
        )
        raw = (
            jnp.einsum("qhd,kd->hqk", query_heads, keys, preferred_element_type=jnp.float32) * scale
        )
        return (raw, allowed[None])

    def attend(carry, piece, start):
        keys, values = piece

        def work(state):
            running, total, accum = state
            raw, allowed = scores_for(keys, start)
            masked = jnp.where(allowed, raw, FLOOR_SCORE)
            newest = jnp.maximum(running, jnp.max(masked, axis=-1))
            factor = jnp.exp(running - newest)
            weights = jnp.where(allowed, jnp.exp(masked - newest[..., None]), 0.0)
            total = total * factor + jnp.sum(weights, axis=-1)
            update = jnp.einsum(
                "hqk,kd->qhd",
                weights.astype(jnp.bfloat16),
                values,
                preferred_element_type=jnp.float32,
            )
            accum = accum * factor.T[:, :, None] + update
            return (newest, total, accum)

        return lax.cond(start <= last_query, work, lambda state: state, carry)

    start_state = (
        jnp.full((head_group, rows), FLOOR_SCORE, jnp.float32),
        jnp.zeros((head_group, rows), jnp.float32),
        jnp.zeros((rows, head_group, HEAD_SIZE), jnp.float32),
    )
    running, total, accum = in_blocks(
        attend,
        start_state,
        (
            lax.all_gather(key_rows, "blk", axis=0, tiled=True),
            lax.all_gather(value_rows, "blk", axis=0, tiled=True),
        ),
        rows,
    )
    attn_full = accum / total.T[:, :, None]
    log_total = running + jnp.log(total)
    out_send = attn_full.astype(jnp.bfloat16).reshape(rows, 1, head_group * HEAD_SIZE)
    out_tok = lax.all_to_all(out_send, "head", split_axis=0, concat_axis=1, tiled=True).reshape(
        count_per_token, QUERY_HEADS * HEAD_SIZE
    )
    residual = inputs + product(out_tok, out_w)
    normed_two = rms_norm(residual, gain_two)
    normed_two_low = normed_two.astype(jnp.bfloat16)
    up_w, down_w = (
        lax.all_gather(expert_in, ("head", "blk"), axis=1, tiled=True),
        lax.all_gather(expert_out, ("head", "blk"), axis=1, tiled=True),
    )
    route_hot = (route_rows[:, :, None] == jnp.arange(E, dtype=jnp.int32)[None, None, :]).astype(
        jnp.int32
    )
    flat_hot = route_hot.reshape(count_per_token * TOP, E)
    before = jnp.cumsum(flat_hot, axis=0) - flat_hot
    slot = jnp.sum(before * flat_hot, axis=-1).reshape(count_per_token, TOP)
    slot_hot = (slot[:, :, None] == jnp.arange(CAP, dtype=jnp.int32)[None, None, :]).astype(
        jnp.float32
    )
    route_float = route_hot.astype(jnp.float32)
    dispatch = jnp.einsum("tje,tjc->ect", route_float, slot_hot, precision=highest)
    combine = jnp.einsum("tje,tjc,tj->ect", route_float, slot_hot, gate_rows, precision=highest)
    expert_rows = jnp.einsum(
        "ect,td->ecd",
        dispatch.astype(jnp.bfloat16),
        normed_two_low,
        preferred_element_type=jnp.float32,
    ).astype(jnp.bfloat16)
    pair = jnp.einsum("ecd,edf->ecf", expert_rows, up_w, preferred_element_type=jnp.float32)
    hidden_low = gated(pair).astype(jnp.bfloat16)
    expert_result = jnp.einsum(
        "ecf,efd->ecd", hidden_low, down_w, preferred_element_type=jnp.float32
    )
    mixture = jnp.einsum("ect,ecd->td", combine, expert_result, precision=highest)
    final = residual + mixture
    diff = final - target
    local_count = jnp.sum(keep_mask)
    local_error = jnp.sum(keep_mask * jnp.sum(diff * diff, axis=-1))
    count_all, error_all = lax.psum((local_count, local_error), ("head", "blk"))
    loss = error_all / (width * count_all)
    grad_final = keep_mask[:, None] * diff * (span * 1.0 / count_all)
    up_back, down_back = (
        lax.all_gather(expert_in, ("head", "blk"), axis=1, tiled=True),
        lax.all_gather(expert_out, ("head", "blk"), axis=1, tiled=True),
    )
    grad_result = jnp.einsum("ect,td->ecd", combine, grad_final, precision=highest).astype(
        jnp.bfloat16
    )
    grad_down = jnp.einsum(
        "ecf,ecd->efd", hidden_low, grad_result, preferred_element_type=jnp.float32
    )
    grad_hidden = jnp.einsum(
        "ecd,efd->ecf", grad_result, down_back, preferred_element_type=jnp.float32
    )
    unused_value, pull_gate = jax.vjp(gated, pair)
    grad_pair = pull_gate(grad_hidden)[0].astype(jnp.bfloat16)
    grad_up = jnp.einsum("ecd,ecf->edf", expert_rows, grad_pair, preferred_element_type=jnp.float32)
    grad_rows = jnp.einsum("ecf,edf->ecd", grad_pair, up_back, preferred_element_type=jnp.float32)
    grad_normed_two = jnp.einsum("ect,ecd->td", dispatch, grad_rows, precision=highest)
    unused_value, pull_two = jax.vjp(rms_norm, residual, gain_two)
    grad_res_norm, grad_gain_two = pull_two(grad_normed_two)
    grad_residual = grad_final + grad_res_norm
    grad_attn_low = grad_residual.astype(jnp.bfloat16)
    grad_out_w = jnp.einsum("tk,td->kd", out_tok, grad_attn_low, preferred_element_type=jnp.float32)
    output_gradient_token = jnp.einsum(
        "td,kd->tk", grad_attn_low, out_w, preferred_element_type=jnp.float32
    ).astype(jnp.bfloat16)
    grad_out_grp = lax.all_to_all(
        output_gradient_token.reshape(count_per_token, KEY_VALUE_HEADS, head_group * HEAD_SIZE),
        "head",
        split_axis=1,
        concat_axis=0,
        tiled=True,
    ).reshape(rows, head_group, HEAD_SIZE)
    delta = jnp.einsum(
        "qhd,qhd->hq", grad_out_grp.astype(jnp.float32), attn_full, precision=highest
    )

    def attend_back(carry, piece, start):
        keys, values = piece

        def work(state):
            grad_query, grad_keys, grad_values = state
            raw, allowed = scores_for(keys, start)
            weights = jnp.where(allowed, jnp.exp(raw - log_total[..., None]), 0.0)
            grad_weights = jnp.einsum(
                "qhd,kd->hqk", grad_out_grp, values, preferred_element_type=jnp.float32
            )
            grad_raw = (weights * (grad_weights - delta[..., None])).astype(jnp.bfloat16)
            grad_query = (
                grad_query
                + jnp.einsum("hqk,kd->qhd", grad_raw, keys, preferred_element_type=jnp.float32)
                * scale
            )
            key_part = (
                jnp.einsum("hqk,qhd->kd", grad_raw, query_heads, preferred_element_type=jnp.float32)
                * scale
            )
            value_part = jnp.einsum(
                "hqk,qhd->kd",
                weights.astype(jnp.bfloat16),
                grad_out_grp,
                preferred_element_type=jnp.float32,
            )
            block_size = keys.shape[0]
            grad_keys = lax.dynamic_update_slice_in_dim(
                grad_keys,
                lax.dynamic_slice_in_dim(grad_keys, start, block_size, 0) + key_part,
                start,
                0,
            )
            grad_values = lax.dynamic_update_slice_in_dim(
                grad_values,
                lax.dynamic_slice_in_dim(grad_values, start, block_size, 0) + value_part,
                start,
                0,
            )
            return (grad_query, grad_keys, grad_values)

        return lax.cond(start <= last_query, work, lambda state: state, carry)

    back_state = (
        jnp.zeros((rows, head_group, HEAD_SIZE), jnp.float32),
        jnp.zeros((span, HEAD_SIZE), jnp.float32),
        jnp.zeros((span, HEAD_SIZE), jnp.float32),
    )
    grad_query, grad_keys_full, grad_values_full = in_blocks(
        attend_back,
        back_state,
        (
            lax.all_gather(key_rows, "blk", axis=0, tiled=True),
            lax.all_gather(value_rows, "blk", axis=0, tiled=True),
        ),
        rows,
    )
    grad_keys, grad_values = (
        lax.psum_scatter(grad_keys_full, "blk", scatter_dimension=0, tiled=True),
        lax.psum_scatter(grad_values_full, "blk", scatter_dimension=0, tiled=True),
    )
    grad_query_lin = (
        rotary_apply(grad_query, query_where, -1.0)
        .astype(jnp.bfloat16)
        .reshape(rows, 1, head_group * HEAD_SIZE)
    )
    grad_key_lin = rotary_apply(grad_keys.reshape(rows, 1, HEAD_SIZE), query_where, -1.0).astype(
        jnp.bfloat16
    )
    grad_value_lin = grad_values.astype(jnp.bfloat16).reshape(rows, 1, HEAD_SIZE)
    back_query, key_backward, value_backward = (
        lax.all_to_all(grad_query_lin, "head", split_axis=0, concat_axis=1, tiled=True),
        lax.all_to_all(grad_key_lin, "head", split_axis=0, concat_axis=1, tiled=True),
        lax.all_to_all(grad_value_lin, "head", split_axis=0, concat_axis=1, tiled=True),
    )
    back_query = back_query.reshape(count_per_token, QUERY_HEADS * HEAD_SIZE)
    key_backward = key_backward.reshape(count_per_token, KEY_VALUE_HEADS * HEAD_SIZE)
    value_backward = value_backward.reshape(count_per_token, KEY_VALUE_HEADS * HEAD_SIZE)
    grad_query_w = jnp.einsum(
        "td,tk->dk", normed_low, back_query, preferred_element_type=jnp.float32
    )
    grad_key_w = jnp.einsum(
        "td,tk->dk", normed_low, key_backward, preferred_element_type=jnp.float32
    )
    grad_value_w = jnp.einsum(
        "td,tk->dk", normed_low, value_backward, preferred_element_type=jnp.float32
    )
    grad_normed_one = jnp.einsum(
        "tk,dk->td", back_query, query_w, preferred_element_type=jnp.float32
    )
    grad_normed_one = grad_normed_one + jnp.einsum(
        "tk,dk->td", key_backward, key_w, preferred_element_type=jnp.float32
    )
    grad_normed_one = grad_normed_one + jnp.einsum(
        "tk,dk->td", value_backward, value_w, preferred_element_type=jnp.float32
    )
    unused_value, pull_one = jax.vjp(rms_norm, inputs, gain_one)
    grad_in_norm, grad_gain_one = pull_one(grad_normed_one)
    grad_inputs = grad_residual + grad_in_norm
    sums = (
        lax.psum_scatter(grad_query_w, ("head", "blk"), scatter_dimension=0, tiled=True),
        lax.psum_scatter(grad_key_w, ("head", "blk"), scatter_dimension=0, tiled=True),
        lax.psum_scatter(grad_value_w, ("head", "blk"), scatter_dimension=0, tiled=True),
        lax.psum_scatter(grad_out_w, ("head", "blk"), scatter_dimension=0, tiled=True),
        lax.psum_scatter(grad_gain_one, ("head", "blk"), scatter_dimension=0, tiled=True),
        lax.psum_scatter(grad_gain_two, ("head", "blk"), scatter_dimension=0, tiled=True),
        lax.psum_scatter(grad_up, ("head", "blk"), scatter_dimension=1, tiled=True),
        lax.psum_scatter(grad_down, ("head", "blk"), scatter_dimension=1, tiled=True),
    )
    shape = states.shape
    return (
        final.astype(jnp.bfloat16).reshape(shape),
        loss,
        grad_inputs.reshape(shape),
        sums[4],
        sums[0],
        sums[1],
        sums[2],
        sums[3],
        sums[5],
        sums[6],
        sums[7],
    )


def solution(mesh):
    in_specs = (
        P("blk", "head", None, None),
        P("blk", "head", None, None),
        P("blk", "head", None),
        P("blk", "head", None, None),
        P("blk", "head", None, None),
        P(),
        P(("head", "blk")),
        P(("head", "blk"), None),
        P(("head", "blk"), None),
        P(("head", "blk"), None),
        P(("head", "blk"), None),
        P(("head", "blk")),
        P(None, ("head", "blk"), None),
        P(None, ("head", "blk"), None),
    )
    out_specs = (
        P("blk", "head", None, None),
        P(),
        P("blk", "head", None, None),
        P(("head", "blk")),
        P(("head", "blk"), None),
        P(("head", "blk"), None),
        P(("head", "blk"), None),
        P(("head", "blk"), None),
        P(("head", "blk")),
        P(None, ("head", "blk"), None),
        P(None, ("head", "blk"), None),
    )
    return jax.shard_map(
        per_device, mesh=mesh, in_specs=in_specs, out_specs=out_specs, check_vma=False
    )
```

profile of v0, /device:TPU:0, one launch (start us, length us, event | category | flops | bytes accessed | tf_op | source)
XLA Modules:
  0.0 2443.2 jit_solution(6555546676234160416)
XLA Ops:
  8.0 46.5 %all_gather.35 = bf16[1536,256]{1,0:T(8,128)(2,1)S(1)} all-gather(bf16[48,256]{1,0:T(8,128)(2,1)} %param.30), channel_id=1, replica_groups=mesh['head'=2,'blk'=16] {'head','blk'}, dimensions={0}, use_global_device_ids=true | all-gather | bytes 811008 | tf_op jit(solution)/shard_map/all_gather | solution.py:103
  55.3 37.9 %all-reduce.7 = (bf16[1536]{0:T(1024)(128)(2,1)S(1)}, bf16[1536]{0:T(1024)(128)(2,1)S(1)}) all-reduce(bf16[1536]{0:T(1024)(128)(2,1)S(1)} %dynamic-update-slice, bf16[1536]{0:T(1024)(128)(2,1)S(1)} %dynamic-update-slice.1), channel_id=1, replica_groups=mesh['head'=2,'blk'=16] {'head','blk'}, use_global_device_ids=true, to_apply=%add.2 | all-reduce | flops 3072 | bytes 12288
  102.9 41.3 %all_gather.38 = bf16[1536,256]{1,0:T(8,128)(2,1)S(1)} all-gather(bf16[48,256]{1,0:T(8,128)(2,1)S(1)} %copy-done.38), channel_id=1, replica_groups=mesh['head'=2,'blk'=16] {'head','blk'}, dimensions={0}, use_global_device_ids=true | all-gather | bytes 811008 | tf_op jit(solution)/shard_map/all_gather | solution.py:104
  155.2 37.3 %psum.15 = f32[]{:T(128)} all-reduce(f32[]{:T(128)} %convert_reduce_fusion.3), channel_id=1, replica_groups=mesh['head'=2,'blk'=16] {'head','blk'}, use_global_device_ids=true, to_apply=%region_18.19 | all-reduce | flops 1 | bytes 8 | tf_op jit(solution)/shard_map/psum | solution.py:227
  215.6 8.8 all-to-all-done.1
  237.3 11.0 all-to-all-done.3
  260.0 212.3 %all-gather.15.cloned.1.call-done = bf16[8,1536,1536]{2,1,0:T(8,128)(2,1)} async-done(((bf16[8,48,1536]{2,1,0:T(8,128)(2,1)}), bf16[8,1536,1536]{2,1,0:T(8,128)(2,1)}) %all-gather.15.cloned.1.call-update) | async-done | bytes 37748752 | tf_op jit(solution)/shard_map/all_gather | solution.py:196
  472.2 17.7 fusion.131
  494.2 103.7 %all-gather.17.cloned.1.call-done = bf16[8,768,1536]{2,1,0:T(8,128)(2,1)} async-done(((bf16[8,24,1536]{2,1,0:T(8,128)(2,1)}), bf16[8,768,1536]{2,1,0:T(8,128)(2,1)}) %all-gather.17.cloned.1.call-update) | async-done | bytes 18874384 | tf_op jit(solution)/shard_map/all_gather | solution.py:197
  597.9 8.4 fusion.132
  614.2 13.0 fusion.54
  627.2 20.3 fusion.87
  674.8 9.0 while.37
  687.5 176.7 %reduce-scatter.9.cloned.1.call-done = f32[256,128]{0,1:T(8,128)} async-done(((f32[4096,128]{0,1:T(8,128)}), f32[256,128]{0,1:T(8,128)}) %reduce-scatter.9.cloned.1.call-update) | async-done | bytes 131088 | tf_op jit(solution)/shard_map/reduce_scatter | solution.py:325
  874.9 54.1 %reduce-scatter.11.cloned.1.call-done = f32[256,128]{1,0:T(8,128)} async-done(((f32[4096,128]{1,0:T(8,128)}), f32[256,128]{1,0:T(8,128)}) %reduce-scatter.11.cloned.1.call-update) | async-done | bytes 131088 | tf_op jit(solution)/shard_map/reduce_scatter | solution.py:326
  946.3 8.3 all_to_all.124
  961.5 16.5 fusion.134
  979.7 30.2 %fusion.86 = f32[8,1536,1536]{2,1,0:T(8,128)} fusion(bf16[8,96,1536]{2,1,0:T(8,128)(2,1)S(1)} %copy-done.2, f32[8,96,768]{2,1,0:T(8,128)} %get-tuple-element.1011, f32[8,96,768]{2,1,0:T(8,128)} %get-tuple-element.1010), kind=kOutput, calls=%fused_computation.137 | convolution fusion | flops 3626237952 | bytes 82575360 | tf_op jit(solution)/shard_map/ecd,ecf->edf/dot_general | solution.py:245
  1016.9 39.4 %all-reduce.6 = (f32[]{:T(128)}, f32[1536]{0:T(1024)S(1)}, f32[1536]{0:T(1024)S(1)}) all-reduce(f32[]{:T(128)} %multiply_reduce_fusion.4, f32[1536]{0:T(1024)S(1)} %get-tuple-element.943, f32[1536]{0:T(1024)S(1)} %copy-done.33), channel_id=1, replica_groups=mesh['head'=2,'blk'=16] {'head','blk'}, use_global_device_ids=true, to_apply=%region_16.17 | all-reduce | flops 3073 | bytes 24584 | tf_op jit(solution)/shard_map/psum | solution.py:227
  1059.3 73.4 %reduce-scatter.17.cloned.1.call-done = f32[48,256]{1,0:T(8,128)} async-done(((f32[1536,256]{1,0:T(8,128)}), f32[48,256]{1,0:T(8,128)}) %reduce-scatter.17.cloned.1.call-update) | async-done | bytes 49168 | tf_op jit(solution)/shard_map/reduce_scatter | solution.py:369
  1132.7 141.2 %reduce-scatter.19.cloned.1.call-done = f32[48,1536]{1,0:T(8,128)} async-done(((f32[1536,1536]{1,0:T(8,128)}), f32[48,1536]{1,0:T(8,128)}) %reduce-scatter.19.cloned.1.call-update) | async-done | bytes 294928 | tf_op jit(solution)/shard_map/reduce_scatter | solution.py:370
  1273.9 142.0 %reduce-scatter.13.cloned.1.call-done = f32[48,1536]{1,0:T(8,128)} async-done(((f32[1536,1536]{1,0:T(8,128)}), f32[48,1536]{1,0:T(8,128)}) %reduce-scatter.13.cloned.1.call-update) | async-done | bytes 294928 | tf_op jit(solution)/shard_map/reduce_scatter | solution.py:367
  1415.9 352.4 %reduce-scatter.23.cloned.1.call-done = f32[8,24,1536]{2,1,0:T(8,128)} async-done(((f32[8,768,1536]{2,1,0:T(8,128)}), f32[8,24,1536]{2,1,0:T(8,128)}) %reduce-scatter.23.cloned.1.call-update) | async-done | bytes 1179664 | tf_op jit(solution)/shard_map/reduce_scatter | solution.py:374
  1768.3 666.8 %reduce-scatter.21.cloned.1.call-done = f32[8,48,1536]{2,1,0:T(8,128)} async-done(((f32[8,1536,1536]{2,1,0:T(8,128)}), f32[8,48,1536]{2,1,0:T(8,128)}) %reduce-scatter.21.cloned.1.call-update) | async-done | bytes 2359312 | tf_op jit(solution)/shard_map/reduce_scatter | solution.py:373
  (360 shorter events, 179.8 us)
Async XLA Ops:
  7.2 193.1 %all-gather.9.cloned.1.call-start = ((), (), s32[]{:S(2)}) async-start(), calls=%async_computation.17 | async-start | bytes 4866048 | tf_op jit(solution)/shard_map/all_gather | solution.py:102
  8.0 217.4 %all-gather.7.cloned.1.call-start = ((), (), s32[]{:S(2)}) async-start(), calls=%async_computation.16 | async-start | bytes 1114112 | tf_op jit(solution)/shard_map/all_gather | solution.py:181
  93.3 113.6 %copy-start.24 = (f32[1536]{0:T(1024)}, f32[1536]{0:T(1024)S(1)}, u32[]{:S(2)}) copy-start(f32[1536]{0:T(1024)S(1)} %convert_element_type.208) | copy-start | bytes 18436
  93.6 113.3 %copy-start.34 = (f32[128]{0:T(128)}, f32[128]{0:T(128)S(1)}, u32[]{:S(2)}) copy-start(f32[128]{0:T(128)S(1)} %fusion.117) | copy-start | bytes 1540
  102.8 122.5 %all-gather.11.cloned.1.call-start = ((), (), s32[]{:S(2)}) async-start(), calls=%async_computation.18 | async-start | bytes 1114112 | tf_op jit(solution)/shard_map/all_gather | solution.py:182
  152.8 102.0 %all-gather.13.cloned.1.call-start = ((), (), s32[]{:S(2)}) async-start(), calls=%async_computation.19 | async-start | bytes 4866048 | tf_op jit(solution)/shard_map/all_gather | solution.py:105
  153.4 318.8 %all-gather.15.cloned.1.call-start = ((), (), s32[]{:S(2)}) async-start(), calls=%async_computation.20 | async-start | bytes 38928384 | tf_op jit(solution)/shard_map/all_gather | solution.py:196
  154.0 443.9 %all-gather.17.cloned.1.call-start = ((), (), s32[]{:S(2)}) async-start(), calls=%async_computation.21 | async-start | bytes 19464192 | tf_op jit(solution)/shard_map/all_gather | solution.py:197
  211.6 12.8 all-to-all-start.1
  233.3 15.0 all-to-all-start.3
  260.0 230.0 %copy-start.1 = (bf16[8,96,1536]{2,1,0:T(8,128)(2,1)}, bf16[8,96,1536]{2,1,0:T(8,128)(2,1)S(1)}, u32[]{:S(2)}) copy-start(bf16[8,96,1536]{2,1,0:T(8,128)(2,1)S(1)} %convolution_convert_fusion.1) | copy-start | bytes 7077892
  494.2 112.1 %copy-start.4 = (f32[128,1536]{1,0:T(8,128)S(1)}, f32[128,1536]{1,0:T(8,128)}, u32[]{:S(2)}) copy-start(f32[128,1536]{1,0:T(8,128)} %copy-done.3) | copy-start | bytes 2359300
  660.0 10.7 all-to-all-start.4
  663.5 200.8 %reduce-scatter.9.cloned.1.call-start = ((), (), s32[]{:S(2)}) async-start(), calls=%async_computation.22 | async-start | bytes 2228224 | tf_op jit(solution)/shard_map/reduce_scatter | solution.py:325
  686.7 177.6 %copy-start.42 = (f32[64]{0:T(128)S(1)}, f32[64]{0:T(128)}, u32[]{:S(2)}) copy-start(f32[64]{0:T(128)} %copy-done.41) | copy-start | bytes 772
  686.7 186.5 %copy-start.25 = (f32[1536]{0:T(1024)S(1)}, f32[1536]{0:T(1024)}, u32[]{:S(2)}) copy-start(f32[1536]{0:T(1024)} %copy-done.24) | copy-start | bytes 18436
  686.7 186.5 %copy-start.35 = (f32[128]{0:T(128)S(1)}, f32[128]{0:T(128)}, u32[]{:S(2)}) copy-start(f32[128]{0:T(128)} %copy-done.34) | copy-start | bytes 1540
  686.7 242.4 %reduce-scatter.11.cloned.1.call-start = ((), (), s32[]{:S(2)}) async-start(), calls=%async_computation.23 | async-start | bytes 2228224 | tf_op jit(solution)/shard_map/reduce_scatter | solution.py:326
  687.4 371.9 %reduce-scatter.15.cloned.1.call-start = ((), (), s32[]{:S(2)}) async-start(), calls=%async_computation.25 | async-start | bytes 1622016 | tf_op jit(solution)/shard_map/reduce_scatter | solution.py:368
  874.9 257.8 %reduce-scatter.17.cloned.1.call-start = ((), (), s32[]{:S(2)}) async-start(), calls=%async_computation.26 | async-start | bytes 1622016 | tf_op jit(solution)/shard_map/reduce_scatter | solution.py:369
  939.2 334.7 %reduce-scatter.19.cloned.1.call-start = ((), (), s32[]{:S(2)}) async-start(), calls=%async_computation.27 | async-start | bytes 9732096 | tf_op jit(solution)/shard_map/reduce_scatter | solution.py:370
  944.3 471.6 %reduce-scatter.13.cloned.1.call-start = ((), (), s32[]{:S(2)}) async-start(), calls=%async_computation.24 | async-start | bytes 9732096 | tf_op jit(solution)/shard_map/reduce_scatter | solution.py:367
  960.3 808.0 %reduce-scatter.23.cloned.1.call-start = ((), (), s32[]{:S(2)}) async-start(), calls=%async_computation.29 | async-start | bytes 38928384 | tf_op jit(solution)/shard_map/reduce_scatter | solution.py:374
  978.0 1457.1 %reduce-scatter.21.cloned.1.call-start = ((), (), s32[]{:S(2)}) async-start(), calls=%async_computation.28 | async-start | bytes 77856768 | tf_op jit(solution)/shard_map/reduce_scatter | solution.py:373
  (52 other events, 992.3 us)
Sparse Core Ops, SparseCore 0:
  11.0 67.9 all-gather.8
  103.0 37.4 all-gather.6
  152.9 33.8 all-gather.10
  189.6 65.1 all-gather.12
  257.6 214.5 all-gather.14
  475.1 122.7 all-gather.16
  686.8 177.3 reduce-scatter.8
  868.5 60.5 reduce-scatter.10
  934.9 96.0 reduce-scatter.14
  1036.6 96.0 reduce-scatter.16
  1139.2 134.7 reduce-scatter.18
  1281.2 134.5 reduce-scatter.12
  1422.9 345.4 reduce-scatter.22
  1776.3 658.7 reduce-scatter.20
where the time goes:
time: 2460 us; the launch traced here: 2440 us
  waiting for transfers between devices  1960 us (80%)
  blocking collectives  239 us (10%)
  matrix products  164 us (7%)
  local copies, waits for them, and re-layouts  30.5 us (1%)
    reduce_scatter x1, waiting for transfers between devices, per_device(): lax.psum_scatter(grad_up, ('head', 'blk'), scatter_dimension=1, tiled=True)  667 us
    reduce_scatter x1, waiting for transfers between devices, per_device(): lax.psum_scatter(grad_down, ('head', 'blk'), scatter_dimension=1, tiled=T...  352 us
    all_gather x1, waiting for transfers between devices, per_device(): lax.all_gather(expert_in, ('head', 'blk'), axis=1, tiled=True)  212 us
    reduce_scatter x1, waiting for transfers between devices, per_device(): lax.psum_scatter(grad_keys_full, 'blk', scatter_dimension=0, tiled=True)  177 us
    reduce_scatter x1, waiting for transfers between devices, per_device(): lax.psum_scatter(grad_query_w, ('head', 'blk'), scatter_dimension=0, tile...  142 us
    reduce_scatter x1, waiting for transfers between devices, per_device(): lax.psum_scatter(grad_out_w, ('head', 'blk'), scatter_dimension=0, tiled=...  141 us
    all_gather x1, waiting for transfers between devices, per_device(): lax.all_gather(expert_out, ('head', 'blk'), axis=1, tiled=True)  104 us
    psum x2, blocking collectives, per_device(): count_all, error_all = lax.psum((local_count, local_error), ('head', 'blk'))  76.6 us
  transfers between devices with their start and end apart: 17, of which 13 were waited for; matrix products, arithmetic and copies ran while one was open for 5% of the time, Pallas kernels for 0%

commit v1 on v0

--- a/solution.py
+++ b/solution.py
@@ -1,6 +1,10 @@
+import functools
+
 import jax
 import jax.numpy as jnp
 from jax import lax
+from jax.experimental import pallas as pl
+from jax.experimental.pallas import tpu as pltpu
 from jax.sharding import PartitionSpec as P
 
 QUERY_HEADS = 12
@@ -10,10 +14,13 @@
 E = 8
 CAP = 96
 
-
 ROTARY_BASE = 10000.0
 FLOOR_SCORE = -1e30
 
+MESH = pl.DeviceIdType.MESH
+NZ = 4
+BF = jnp.bfloat16
+F32 = jnp.float32
 
 def product(left, right):
     return jnp.dot(left, right, preferred_element_type=jnp.float32)
@@ -59,7 +66,7 @@
     return lax.fori_loop(0, count_blocks, turn, carry)
 
 
-def per_device(
+def per_device_plain(
     states,
     teacher,
     valid,
@@ -389,6 +396,1018 @@
     )
 
 
+class Place:
+    def __init__(self):
+        self.x = lax.axis_index("head")
+        self.b = lax.axis_index("blk")
+        self.c = self.b % 2
+        self.y = (self.b // 2) % 2
+        self.z = self.b // 4
+
+    def near(self, kind):
+        x, y, z, c = self.x, self.y, self.z, self.c
+        if kind == "up":
+            z = jnp.minimum(z + 1, NZ - 1)
+        elif kind == "down":
+            z = jnp.maximum(z - 1, 0)
+        elif kind == "y":
+            y = 1 - y
+        elif kind == "x":
+            x = 1 - x
+        elif kind == "c":
+            c = 1 - c
+        return (x, z * 4 + y * 2 + c)
+
+    def blk(self, z, y, c):
+        return z * 4 + y * 2 + c
+
+    def outward(self, j):
+        inner = jnp.where(j < 2, 1 - j, j)
+        order = jnp.where((self.z == 0) | (self.z == NZ - 1), j, inner)
+        return jnp.where(self.z < 2, order, NZ - 1 - order)
+
+    def inward(self, j):
+        inner = jnp.where(j == 0, 3, jnp.where(j == 1, 0, jnp.where(j == 2, 2, 1)))
+        order = jnp.where((self.z == 0) | (self.z == NZ - 1), NZ - 1 - j, inner)
+        return jnp.where(self.z < 2, order, NZ - 1 - order)
+
+
+def greet_all(me):
+    barrier = pltpu.get_barrier_semaphore()
+
+    def one(k, carry):
+        pl.semaphore_signal(
+            barrier, inc=1, device_id=((me.x + k // 16) % 2, (me.b + k) % 16), device_id_type=MESH
+        )
+        return carry
+
+    lax.fori_loop(1, 32, one, 0)
+    pl.semaphore_wait(barrier, 31)
+
+
+def remote(src, dst, send, recv, to):
+    return pltpu.make_async_remote_copy(
+        src_ref=src, dst_ref=dst, send_sem=send, recv_sem=recv, device_id=to, device_id_type=MESH
+    )
+
+
+def arrived(ref, sem, me):
+    remote(ref, ref, sem, sem, me.near("c")).wait_recv()
+
+
+def left(ref, sem, me):
+    remote(ref, ref, sem, sem, me.near("c")).wait_send()
+
+
+def gather_all(me, g, index, send, recv, between=None):
+    x, y, c = me.x, me.y, me.c
+    half = g.shape[2] // 2
+    first, second = pl.ds(0, half), pl.ds(half, half)
+
+    def put(j, kind, n, s, cols=None, slot=0):
+        ref = g.at[s] if cols is None else g.at[s, :, cols]
+        remote(ref, ref, send.at[j, n], recv.at[s, slot], me.near(kind)).start()
+
+    def turn(j, carry):
+        zz = me.outward(j)
+        own = index(x, zz, y, c)
+
+        @pl.when((j > 0) & (j < 4))
+        def _():
+            arrived(g.at[own], recv.at[own, 0], me)
+
+        @pl.when(j < 4)
+        def _():
+            pl.when((zz <= me.z) & (me.z < NZ - 1))(lambda: put(j, "up", 0, own))
+            pl.when((zz >= me.z) & (me.z > 0))(lambda: put(j, "down", 1, own))
+            put(j, "y", 2, own)
+            put(j, "x", 3, own)
+            put(j, "c", 6, own)
+
+        @pl.when((j > 0) & (j < 5))
+        def _():
+            i = j - 1
+            zp = me.outward(i)
+            s = index(x, zp, 1 - y, c)
+            arrived(g.at[s], recv.at[s, 0], me)
+            put(i, "x", 4, s, first, 0)
+            put(i, "c", 7, s)
+            t = index(1 - x, zp, y, c)
+            arrived(g.at[t], recv.at[t, 0], me)
+            put(i, "y", 5, t, second, 1)
+            put(i, "c", 8, t)
+
+        @pl.when(j > 1)
+        def _():
+            i = j - 2
+            s = index(1 - x, me.outward(i), 1 - y, c)
+            arrived(g.at[s, :, first], recv.at[s, 0], me)
+            arrived(g.at[s, :, second], recv.at[s, 1], me)
+            put(i, "c", 9, s)
+
+        if between is not None:
+            between(j)
+        return carry
+
+    lax.fori_loop(0, 6, turn, 0)
+
+    def close(j, carry):
+        zz = me.outward(j)
+        own = index(x, zz, y, c)
+        whole, part = g.at[own], g.at[own, :, first]
+        pl.when((zz <= me.z) & (me.z < NZ - 1))(lambda: left(whole, send.at[j, 0], me))
+        pl.when((zz >= me.z) & (me.z > 0))(lambda: left(whole, send.at[j, 1], me))
+        for n in (2, 3, 6, 7, 8, 9):
+            left(whole, send.at[j, n], me)
+        for n in (4, 5):
+            left(part, send.at[j, n], me)
+        for xx in (x, 1 - x):
+            for yy in (y, 1 - y):
+                s = index(xx, zz, yy, 1 - c)
+                arrived(g.at[s], recv.at[s, 0], me)
+        return carry
+
+    lax.fori_loop(0, 4, close, 0)
+
+
+def sum_all(me, part, index, out, rc, rd, rn, rz, acc, sc, ss, vc, vn, vz, between=None):
+    x, y, z, c = me.x, me.y, me.z, me.c
+    half = part.shape[2] // 2
+    first, second = pl.ds(0, half), pl.ds(half, half)
+
+    def slot(xx, zz, yy):
+        return zz * 4 + xx * 2 + yy
+
+    def lead(j, carry):
+        zz = me.inward(j)
+        for xx in (1 - x, x):
+            for yy in (1 - y, y):
+                k = slot(xx, zz, yy)
+                remote(part.at[index(xx, zz, yy, 1 - c)], rc.at[k], sc.at[k], vc.at[k], me.near("c")).start()
+        return carry
+
+    lax.fori_loop(0, 4, lead, 0)
+
+    def with_core(xx, zz, yy):
+        k = slot(xx, zz, yy)
+        arrived(rc.at[k], vc.at[k], me)
+        return k, part[index(xx, zz, yy, c)].astype(F32) + rc[k].astype(F32)
+
+    def turn(j, carry):
+        @pl.when(j < 4)
+        def _():
+            zz = me.inward(j)
+            k, total = with_core(1 - x, zz, 1 - y)
+            rc[k] = total.astype(BF)
+            remote(rc.at[k, :, first], rd.at[0, zz], ss.at[j, 0], vn.at[zz, 0], me.near("x")).start()
+            remote(rc.at[k, :, second], rd.at[1, zz], ss.at[j, 1], vn.at[zz, 1], me.near("y")).start()
+
+        @pl.when((j > 0) & (j < 5))
+        def _():
+            i = j - 1
+            zz = me.inward(i)
+            k, total = with_core(x, zz, 1 - y)
+            arrived(rd.at[0, zz], vn.at[zz, 0], me)
+            rc[k, :, second] = total[:, half:].astype(BF)
+            rc[k, :, first] = (total[:, :half] + rd[0, zz].astype(F32)).astype(BF)
+            remote(rc.at[k], rn.at[0, zz], ss.at[i, 2], vn.at[zz, 2], me.near("y")).start()
+            k, total = with_core(1 - x, zz, y)
+            arrived(rd.at[1, zz], vn.at[zz, 1], me)
+            rc[k, :, first] = total[:, :half].astype(BF)
+            rc[k, :, second] = (total[:, half:] + rd[1, zz].astype(F32)).astype(BF)
+            remote(rc.at[k], rn.at[1, zz], ss.at[i, 3], vn.at[zz, 3], me.near("x")).start()
+
+        @pl.when(j > 1)
+        def _():
+            i = j - 2
+            zz = me.inward(i)
+            k, total = with_core(x, zz, y)
+            arrived(rn.at[0, zz], vn.at[zz, 2], me)
+            arrived(rn.at[1, zz], vn.at[zz, 3], me)
+            acc[...] = total + rn[0, zz].astype(F32) + rn[1, zz].astype(F32)
+            along_z(me, i, zz, acc, rc.at[k], rz, ss, 4, vz)
+
+        if between is not None:
+            between(j)
+        return carry
+
+    lax.fori_loop(0, 6, turn, 0)
+    out[...] = acc[...]
+
+    def close(j, carry):
+        zz = me.inward(j)
+        whole, piece = rc.at[0], rc.at[0, :, first]
+        for xx in (1 - x, x):
+            for yy in (1 - y, y):
+                left(whole, sc.at[slot(xx, zz, yy)], me)
+        for n in (0, 1):
+            left(piece, ss.at[j, n], me)
+        for n in (2, 3):
+            left(whole, ss.at[j, n], me)
+        pl.when(zz > z)(lambda: left(whole, ss.at[j, 4], me))
+        pl.when(zz < z)(lambda: left(whole, ss.at[j, 5], me))
+        return carry
+
+    lax.fori_loop(0, 4, close, 0)
+
+
+def along_z(me, i, zz, acc, room, rz, ss, n, vz):
+    z = me.z
+
+    def add(slot):
+        arrived(rz.at[slot], vz.at[slot], me)
+        acc[...] += rz[slot].astype(F32)
+
+    pl.when((zz >= z) & (z > 0))(lambda: add(zz))
+    pl.when((zz < z) & (z < NZ - 1))(lambda: add(zz))
+    pl.when((zz == z) & (z < NZ - 1))(lambda: add(4))
+
+    @pl.when(zz > z)
+    def _():
+        room[...] = acc[...].astype(BF)
+        remote(room, rz.at[zz], ss.at[i, n], vz.at[zz], me.near("up")).start()
+
+    @pl.when(zz < z)
+    def _():
+        room[...] = acc[...].astype(BF)
+        there = jnp.where(zz == z - 1, 4, zz)
+        remote(room, rz.at[there], ss.at[i, n + 1], vz.at[there], me.near("down")).start()
+
+
+def by_weight(x, z, y, c):
+    return x * 16 + z * 4 + y * 2 + c
+
+
+def by_token(x, z, y, c):
+    return (z * 4 + y * 2 + c) * 2 + x
+
+
+ANY = pl.BlockSpec(memory_space=pl.ANY)
+VMEM = pl.BlockSpec(memory_space=pltpu.VMEM)
+DMA = pltpu.SemaphoreType.DMA
+
+
+def params(number, mib):
+    return pltpu.CompilerParams(
+        collective_id=number, has_side_effects=True, vmem_limit_bytes=mib << 20
+    )
+
+
+def weights_kernel(
+    dense, up, down, g, win, wout, own_sem, send, recv, asend, arecv, xsend, xrecv, osend, orecv
+):
+    me = Place()
+    x, b, c = me.x, me.b, me.c
+    here = by_weight(x, me.z, me.y, c)
+    mine = pltpu.make_async_copy(dense, g.at[here], own_sem.at[0])
+    mine.start()
+    pieces = []
+    for k in range(2):
+        col = pl.multiple_of(k * 768 + c * 384, 128)
+        pieces.append(
+            pltpu.make_async_copy(
+                up.at[b // 2, :, pl.ds(col, 384)],
+                win.at[x, b, :, pl.ds(k * 384, 384)],
+                own_sem.at[1 + k],
+            )
+        )
+    for piece in pieces:
+        piece.start()
+    held = pltpu.make_async_copy(down.at[b // 2], wout.at[b], own_sem.at[3])
+    pl.when(c == x)(held.start)
+    greet_all(me)
+    mine.wait()
+
+    def deal(k, carry):
+        t = (b + k) % 16
+        for h in range(2):
+            col = pl.multiple_of(h * 768 + (t % 2) * 384, 128)
+            remote(
+                up.at[t // 2, :, pl.ds(col, 384)],
+                win.at[x, b, :, pl.ds(h * 384, 384)],
+                asend.at[k, h],
+                arecv.at[b, h],
+                (x, t),
+            ).start()
+        pl.when(t % 2 == x)(
+            lambda: remote(down.at[t // 2], wout.at[b], osend.at[k], orecv.at[b], (x, t)).start()
+        )
+        return carry
+
+    def pass_on(k, carry):
+        f = (b + 16 - k) % 16
+
+        @pl.when(k > 0)
+        def _():
+            for h in range(2):
+                arrived(win.at[x, f, :, pl.ds(h * 384, 384)], arecv.at[f, h], me)
+
+        remote(win.at[x, f], win.at[x, f], xsend.at[k], xrecv.at[f], me.near("x")).start()
+
+        @pl.when(c == x)
+        def _():
+            pl.when(k > 0)(lambda: arrived(wout.at[f], orecv.at[f], me))
+            remote(wout.at[f], wout.at[f], osend.at[16 + k], orecv.at[f], me.near("x")).start()
+
+        return carry
+
+    def between(j):
+        @pl.when(j == 0)
+        def _():
+            lax.fori_loop(1, 16, deal, 0)
+            for piece in pieces:
+                piece.wait()
+            pl.when(c == x)(held.wait)
+
+        @pl.when(j >= 2)
+        def _():
+            lax.fori_loop((j - 2) * 4, (j - 2) * 4 + 4, pass_on, 0)
+
+    gather_all(me, g, by_weight, send, recv, between)
+
+    def close(k, carry):
+        slab, piece = win.at[x, b], win.at[x, b, :, pl.ds(0, 384)]
+
+        @pl.when(k > 0)
+        def _():
+            for h in range(2):
+                left(piece, asend.at[k, h], me)
+            pl.when((b + k) % 2 == x)(lambda: left(wout.at[b], osend.at[k], me))
+
+        left(slab, xsend.at[k], me)
+        pl.when(c == x)(lambda: left(wout.at[b], osend.at[16 + k], me))
+        arrived(win.at[1 - x, k], xrecv.at[k], me)
+        pl.when(c != x)(lambda: arrived(wout.at[k], orecv.at[k], me))
+        return carry
+
+    lax.fori_loop(0, 16, close, 0)
+
+
+def bring_weights(dense, up, down):
+    columns = dense.shape[1]
+    return pl.pallas_call(
+        weights_kernel,
+        out_shape=(
+            jax.ShapeDtypeStruct((32, 48, columns), BF),
+            jax.ShapeDtypeStruct((2, 16, 48, 768), BF),
+            jax.ShapeDtypeStruct((16, 48, 768), BF),
+        ),
+        in_specs=[ANY] * 3,
+        out_specs=(ANY,) * 3,
+        scratch_shapes=[
+            DMA((4,)),
+            DMA((4, 10)),
+            DMA((32, 2)),
+            DMA((16, 2)),
+            DMA((16, 2)),
+            DMA((16,)),
+            DMA((16,)),
+            DMA((32,)),
+            DMA((16,)),
+        ],
+        compiler_params=params(1, 8),
+        name="bring_weights",
+    )(dense, up, down)
+
+
+NT = (((1,), (1,)), ((), ()))
+TN = (((0,), (0,)), ((), ()))
+GELU_A = 0.7978845608028654
+GELU_B = 0.044715
+
+
+def experts_kernel(
+    n2, h, teacher, weight, gate, win, wout,
+    final, err, dn2, dy_out, dwin, dwout,
+    nall, dyall, pairs, zg, dpairs, part, rc, ry, rz, acc, errs,
+    gsend, grecv, csend, crecv, ysend, yrecv, zsend, zrecv, esend, erecv,
+):
+    me = Place()
+    x, y, z, b, c = me.x, me.y, me.z, me.b, me.c
+    greet_all(me)
+
+    def gather(buf, way, chunk):
+        def put(j, kind, n, s):
+            remote(buf.at[s], buf.at[s], gsend.at[way, j, n], grecv.at[way, s], me.near(kind)).start()
+
+        def turn(j, carry):
+            zz = me.outward(j)
+            own = me.blk(zz, y, c)
+
+            @pl.when((j > 0) & (j < 4))
+            def _():
+                arrived(buf.at[own], grecv.at[way, own], me)
+
+            @pl.when(j < 4)
+            def _():
+                pl.when((zz <= z) & (z < NZ - 1))(lambda: put(j, "up", 0, own))
+                pl.when((zz >= z) & (z > 0))(lambda: put(j, "down", 1, own))
+                put(j, "y", 2, own)
+                put(j, "c", 3, own)
+
+            @pl.when(j > 0)
+            def _():
+                i = j - 1
+                zp = me.outward(i)
+                s = me.blk(zp, 1 - y, c)
+                arrived(buf.at[s], grecv.at[way, s], me)
+                put(i, "c", 4, s)
+
+                def both(n, carry):
+                    yy = (y + n) % 2
+                    s = me.blk(zp, yy, 1 - c)
+                    arrived(buf.at[s], grecv.at[way, s], me)
+                    chunk(zp * 2 + yy)
+                    return carry
+
+                lax.fori_loop(0, 2, both, 0)
+
+            return carry
+
+        lax.fori_loop(0, 5, turn, 0)
+
+        def close(j, carry):
+            zz = me.outward(j)
+            whole = buf.at[b]
+            pl.when((zz <= z) & (z < NZ - 1))(lambda: left(whole, gsend.at[way, j, 0], me))
+            pl.when((zz >= z) & (z > 0))(lambda: left(whole, gsend.at[way, j, 1], me))
+            for n in (2, 3, 4):
+                left(whole, gsend.at[way, j, n], me)
+            return carry
+
+        lax.fori_loop(0, 4, close, 0)
+
+    def to_other_core(way, q):
+        remote(part.at[q * 2 + 1 - c], rc.at[way, q], csend.at[way, q], crecv.at[way, q], me.near("c")).start()
+
+    def reduce(way, between):
+        def lead(j, carry):
+            zz = me.inward(j)
+            q = zz * 2 + 1 - y
+            s = q * 2 + c
+            arrived(rc.at[way, q], crecv.at[way, q], me)
+            part[s] = (part[s].astype(F32) + rc[way, q].astype(F32)).astype(BF)
+            remote(part.at[s], ry.at[way, zz], ysend.at[way, j], yrecv.at[way, zz], me.near("y")).start()
+            return carry
+
+        lax.fori_loop(0, 4, lead, 0)
+
+        def turn(j, carry):
+            between(j)
+            zz = me.inward(j)
+            q = zz * 2 + y
+            s = q * 2 + c
+            arrived(rc.at[way, q], crecv.at[way, q], me)
+            arrived(ry.at[way, zz], yrecv.at[way, zz], me)
+            acc[...] = part[s].astype(F32) + rc[way, q].astype(F32) + ry[way, zz].astype(F32)
+            along_z(me, j, zz, acc, part.at[s], rz.at[way], zsend.at[way], 0, zrecv.at[way])
+            return carry
+
+        lax.fori_loop(0, 4, turn, 0)
+
+        def close(j, carry):
+            zz = me.inward(j)
+            whole = part.at[b]
+            left(whole, ysend.at[way, j], me)
+            left(whole, csend.at[way, j], me)
+            left(whole, csend.at[way, j + 4], me)
+            pl.when(zz > z)(lambda: left(whole, zsend.at[way, j, 0], me))
+            pl.when(zz < z)(lambda: left(whole, zsend.at[way, j, 1], me))
+            return carry
+
+        lax.fori_loop(0, 4, close, 0)
+
+    def gelu_parts(g):
+        t = jnp.tanh(GELU_A * (g + GELU_B * g * g * g))
+        return t, 0.5 * g * (1.0 + t)
+
+    def forward(q):
+        rows = nall[pl.ds(q * 2, 2)].reshape(256, 1536)
+        pair = jnp.dot(rows, win[...], preferred_element_type=F32)
+        pairs[q] = pair
+        unused, a = gelu_parts(pair[:, :384])
+        zq = (a * pair[:, 384:] * gate[q]).astype(BF)
+        zg[q] = zq
+        out = jnp.dot(zq, wout[...], preferred_element_type=F32)
+        part[pl.ds(q * 2, 2)] = out.astype(BF).reshape(2, 128, 1536)
+        to_other_core(0, q)
+
+    def backward(q):
+        rows = dyall[pl.ds(q * 2, 2)].reshape(256, 1536)
+        dz = lax.dot_general(rows, wout[...], NT, preferred_element_type=F32) * gate[q]
+        g, u = pairs[q, :, :384], pairs[q, :, 384:]
+        t, a = gelu_parts(g)
+        slope = 0.5 * (1.0 + t) + 0.5 * g * (1.0 - t * t) * (GELU_A * (1.0 + 3.0 * GELU_B * g * g))
+        dpairs[q, :, :384] = (dz * u * slope).astype(BF)
+        dpairs[q, :, 384:] = (dz * a).astype(BF)
+        out = lax.dot_general(dpairs[q], win[...], NT, preferred_element_type=F32)
+        part[pl.ds(q * 2, 2)] = out.astype(BF).reshape(2, 128, 1536)
+        to_other_core(1, q)
+
+    nall[b] = n2[...]
+    gather(nall, 0, forward)
+    reduce(0, lambda j: None)
+
+    done = h[...] + acc[...]
+    final[...] = done.astype(BF)
+    diff = done - teacher[...].astype(F32)
+    scaled = weight[:, 0:1] * diff
+    dy_out[...] = scaled
+    dyall[b] = scaled.astype(BF)
+    kept = jnp.sum(weight[:, 1:2] * diff * diff)
+    me_index = x * 16 + b
+    errs[me_index] = jnp.zeros((8, 128), F32) + kept
+
+    def tell(k, carry):
+        to = ((x + k // 16) % 2, (b + k) % 16)
+        remote(errs.at[me_index], errs.at[me_index], esend.at[k], erecv.at[me_index], to).start()
+        return carry
+
+    lax.fori_loop(1, 32, tell, 0)
+    gather(dyall, 1, backward)
+
+    def weight_part(j):
+        for i in range(2):
+
+            @pl.when(j * 2 + i < 6)
+            def _():
+                col = pl.ds(pl.multiple_of((j * 2 + i) * 256, 256), 256)
+                rows = nall[:, :, col].reshape(2048, 256)
+                both = dpairs[...].reshape(2048, 768)
+                dwin[col, :] = lax.dot_general(rows, both, TN, preferred_element_type=F32).astype(BF)
+                right = dyall[:, :, col].reshape(2048, 256)
+                zall = zg[...].reshape(2048, 384)
+                dwout[:, col] = lax.dot_general(zall, right, TN, preferred_element_type=F32).astype(BF)
+
+    reduce(1, weight_part)
+    dn2[...] = acc[...]
+
+    def hear(k, carry):
+        left(errs.at[0], esend.at[k], me)
+        s = ((x + k // 16) % 2) * 16 + (b + k) % 16
+        arrived(errs.at[s], erecv.at[s], me)
+        return carry
+
+    lax.fori_loop(1, 32, hear, 0)
+    total = errs[0]
+    for s in range(1, 32):
+        total = total + errs[s]
+    err[...] = total
+
+
+def run_experts(n2, h, teacher, weight, gate, win, wout):
+    wide = (128, 1536)
+    shard = (16,) + wide
+    return pl.pallas_call(
+        experts_kernel,
+        out_shape=(
+            jax.ShapeDtypeStruct(wide, BF),
+            jax.ShapeDtypeStruct((8, 128), F32),
+            jax.ShapeDtypeStruct(wide, F32),
+            jax.ShapeDtypeStruct(wide, F32),
+            jax.ShapeDtypeStruct((1536, 768), BF),
+            jax.ShapeDtypeStruct((384, 1536), BF),
+        ),
+        in_specs=[VMEM] * 7,
+        out_specs=(VMEM,) * 6,
+        scratch_shapes=[
+            pltpu.VMEM(shard, BF),
+            pltpu.VMEM(shard, BF),
+            pltpu.VMEM((8, 256, 768), F32),
+            pltpu.VMEM((8, 256, 384), BF),
+            pltpu.VMEM((8, 256, 768), BF),
+            pltpu.VMEM(shard, BF),
+            pltpu.VMEM((2, 8) + wide, BF),
+            pltpu.VMEM((2, 4) + wide, BF),
+            pltpu.VMEM((2, 5) + wide, BF),
+            pltpu.VMEM(wide, F32),
+            pltpu.VMEM((32, 8, 128), F32),
+            DMA((2, 4, 5)),
+            DMA((2, 16)),
+            DMA((2, 8)),
+            DMA((2, 8)),
+            DMA((2, 4)),
+            DMA((2, 4)),
+            DMA((2, 4, 2)),
+            DMA((2, 5)),
+            DMA((32,)),
+            DMA((32,)),
+        ],
+        compiler_params=params(2, 61),
+        name="experts",
+    )(n2, h, teacher, weight, gate, win, wout)
+
+
+def grads_kernel(
+    dense, dwin, dwout, g, gup, gdown,
+    rc, rd, rn, rz, acc, xin, xout,
+    sc, ss, vc, vn, vz, xsend, xrecv, asend, arecv, osend, orecv, own_sem,
+):
+    me = Place()
+    x, b, c = me.x, me.b, me.c
+    greet_all(me)
+
+    def over(k, carry):
+        t = (b + k) % 16
+        remote(dwin.at[1 - x, t], xin.at[t], xsend.at[k], xrecv.at[t], me.near("x")).start()
+        pl.when(c != x)(
+            lambda: remote(dwout.at[t], xout.at[t], osend.at[k], orecv.at[t], me.near("x")).start()
+        )
+        return carry
+
+    lax.fori_loop(0, 16, over, 0)
+
+    def deal(k, carry):
+        t = (b + k) % 16
+        arrived(xin.at[t], xrecv.at[t], me)
+        xin[t] = (xin[t].astype(F32) + dwin[x, t].astype(F32)).astype(BF)
+
+        @pl.when(k > 0)
+        def _():
+            for h in range(2):
+                col = pl.multiple_of(h * 768 + c * 384, 128)
+                remote(
+                    xin.at[t, :, pl.ds(h * 384, 384)],
+                    gup.at[b // 2, :, pl.ds(col, 384)],
+                    asend.at[k, h],
+                    arecv.at[b, h],
+                    (x, t),
+                ).start()
+
+        @pl.when(k == 0)
+        def _():
+            for h in range(2):
+                col = pl.multiple_of(h * 768 + c * 384, 128)
+                pltpu.make_async_copy(
+                    xin.at[t, :, pl.ds(h * 384, 384)],
+                    gup.at[b // 2, :, pl.ds(col, 384)],
+                    own_sem.at[h],
+                ).start()
+
+        @pl.when(c == x)
+        def _():
+            arrived(xout.at[t], orecv.at[t], me)
+            xout[t] = (xout[t].astype(F32) + dwout[t].astype(F32)).astype(BF)
+            pl.when(k > 0)(
+                lambda: remote(
+                    xout.at[t], gdown.at[b // 2], osend.at[16 + k], orecv.at[16 + b // 2], (x, t)
+                ).start()
+            )
+            pl.when(k == 0)(
+                pltpu.make_async_copy(xout.at[t], gdown.at[b // 2], own_sem.at[2]).start
+            )
+
+        return carry
+
+    def between(j):
+        @pl.when(j >= 2)
+        def _():
+            lax.fori_loop((j - 2) * 4, (j - 2) * 4 + 4, deal, 0)
+
+    sum_all(me, dense, by_weight, g, rc, rd, rn, rz, acc, sc, ss, vc, vn, vz, between)
+
+    def close(k, carry):
+        left(xin.at[0], xsend.at[k], me)
+        pl.when(c != x)(lambda: left(xout.at[0], osend.at[k], me))
+
+        @pl.when(k > 0)
+        def _():
+            f = (b + 16 - k) % 16
+            for h in range(2):
+                left(xin.at[0, :, pl.ds(0, 384)], asend.at[k, h], me)
+                col = pl.multiple_of(h * 768 + (f % 2) * 384, 128)
+                arrived(gup.at[f // 2, :, pl.ds(col, 384)], arecv.at[f, h], me)
+            pl.when(c == x)(lambda: left(xout.at[0], osend.at[16 + k], me))
+            pl.when(f % 2 == x)(lambda: arrived(gdown.at[f // 2], orecv.at[16 + f // 2], me))
+
+        @pl.when(k == 0)
+        def _():
+            for h in range(2):
+                col = pl.multiple_of(h * 768 + c * 384, 128)
+                pltpu.make_async_copy(
+                    xin.at[b, :, pl.ds(h * 384, 384)],
+                    gup.at[b // 2, :, pl.ds(col, 384)],
+                    own_sem.at[h],
+                ).wait()
+            pl.when(c == x)(
+                pltpu.make_async_copy(xout.at[b], gdown.at[b // 2], own_sem.at[2]).wait
+            )
+
+        return carry
+
+    lax.fori_loop(0, 16, close, 0)
+
+
+def return_grads(dense, dwin, dwout):
+    rows, columns = dense.shape[1:]
+    shard = (rows, columns)
+    return pl.pallas_call(
+        grads_kernel,
+        out_shape=(
+            jax.ShapeDtypeStruct(shard, F32),
+            jax.ShapeDtypeStruct((8, 48, 1536), BF),
+            jax.ShapeDtypeStruct((8, 48, 768), BF),
+        ),
+        in_specs=[VMEM] * 3,
+        out_specs=(VMEM,) * 3,
+        scratch_shapes=[
+            pltpu.VMEM((16,) + shard, BF),
+            pltpu.VMEM((2, 4, rows, columns // 2), BF),
+            pltpu.VMEM((2, 4) + shard, BF),
+            pltpu.VMEM((5,) + shard, BF),
+            pltpu.VMEM(shard, F32),
+            pltpu.VMEM((16, 48, 768), BF),
+            pltpu.VMEM((16, 48, 768), BF),
+            DMA((16,)),
+            DMA((4, 6)),
+            DMA((16,)),
+            DMA((4, 4)),
+            DMA((5,)),
+            DMA((16,)),
+            DMA((16,)),
+            DMA((16, 2)),
+            DMA((16, 2)),
+            DMA((32,)),
+            DMA((32,)),
+            DMA((3,)),
+        ],
+        compiler_params=params(3, 56),
+        name="return_grads",
+    )(dense, dwin, dwout)
+
+
+def per_device(
+    states, teacher, valid, routes, gates, doc_starts, norm_one,
+    w_query, key_weight, value_weight, w_output, norm_two, expert_in, expert_out,
+):
+    count_per_token = states.shape[2]
+    width = states.shape[3]
+    pairs = lax.axis_size("head")
+    blocks = lax.axis_size("blk")
+    rows = count_per_token * pairs
+    span = rows * blocks
+    head_group = QUERY_HEADS // KEY_VALUE_HEADS
+    scale = HEAD_SIZE ** (-0.5)
+    highest = lax.Precision.HIGHEST
+    block_index = lax.axis_index("blk")
+    pair_index = lax.axis_index("head")
+    token_index = (block_index * pairs + pair_index) * count_per_token + jnp.arange(
+        count_per_token, dtype=jnp.int32
+    )
+    unused_segment, token_position = doc_layout(token_index, doc_starts)
+    query_index = block_index * rows + jnp.arange(rows, dtype=jnp.int32)
+    query_segment, query_where = doc_layout(query_index, doc_starts)
+    last_query = block_index * rows + rows - 1
+    inputs = states.reshape(count_per_token, width).astype(jnp.float32)
+    keep_mask = valid.reshape(count_per_token).astype(jnp.float32)
+    route_rows = routes.reshape(count_per_token, TOP)
+    gate_rows = gates.reshape(count_per_token, TOP)
+
+    table = jnp.sum(
+        jnp.where(route_rows[None] == jnp.arange(E, dtype=jnp.int32)[:, None, None], gate_rows[None], 0.0), axis=-1
+    )
+    high = lax.reduce_precision(table, 8, 7)
+    column = jnp.arange(128)[None, :]
+    gains = jnp.where(
+        column == 0,
+        norm_one[:, None].astype(F32),
+        jnp.where(column == 1, norm_two[:, None].astype(F32), jnp.sum(keep_mask)),
+    ).astype(BF)
+    routed = jnp.concatenate([high, table - high, jnp.zeros((32, 128), F32)], axis=0).astype(BF)
+    dense = jnp.concatenate([w_query, key_weight, value_weight, w_output, gains, routed], axis=1)
+    gathered, win, wout = bring_weights(dense, expert_in, expert_out.reshape(E, 48, 768))
+    flat = gathered.reshape(1536, 3840)
+    query_w, key_w, value_w, out_w = flat[:, :1536], flat[:, 1536:1792], flat[:, 1792:2048], flat[:, 2048:3584]
+    gain_one = flat[:, 3584].astype(F32)
+    gain_two = flat[:, 3585].astype(F32)
+    count_all = jnp.sum(gathered[:, 0, 3586].astype(F32))
+    tables = lax.dynamic_slice_in_dim(gathered[:, :16, 3712:], pair_index * 16, 16, 0).astype(F32)
+    mine = lax.dynamic_slice_in_dim(tables, block_index // 2, 1, 1) + lax.dynamic_slice_in_dim(
+        tables, 8 + block_index // 2, 1, 1
+    )
+    gate_plane = mine.reshape(8, 256, 1)
+
+    normed_one = rms_norm(inputs, gain_one)
+    normed_low = normed_one.astype(jnp.bfloat16)
+    query_lin = product(normed_low, query_w)
+    key_linear = product(normed_low, key_w)
+    value_linear = product(normed_low, value_w)
+    query_rotated = rotary_apply(
+        query_lin.reshape(count_per_token, QUERY_HEADS, HEAD_SIZE), token_position, 1.0
+    )
+    key_rotated = rotary_apply(
+        key_linear.reshape(count_per_token, KEY_VALUE_HEADS, HEAD_SIZE), token_position, 1.0
+    )
+    query_outgoing = query_rotated.astype(jnp.bfloat16).reshape(
+        count_per_token, KEY_VALUE_HEADS, head_group * HEAD_SIZE
+    )
+    key_send = key_rotated.astype(jnp.bfloat16)
+    value_outgoing = value_linear.astype(jnp.bfloat16).reshape(
+        count_per_token, KEY_VALUE_HEADS, HEAD_SIZE
+    )
+    query_grp, key_grp, value_grp = (
+        lax.all_to_all(query_outgoing, "head", split_axis=1, concat_axis=0, tiled=True),
+        lax.all_to_all(key_send, "head", split_axis=1, concat_axis=0, tiled=True),
+        lax.all_to_all(value_outgoing, "head", split_axis=1, concat_axis=0, tiled=True),
+    )
+    query_heads = query_grp.reshape(rows, head_group, HEAD_SIZE)
+    key_rows = key_grp.reshape(rows, HEAD_SIZE)
+    value_rows = value_grp.reshape(rows, HEAD_SIZE)
+
+    def scores_for(keys, start):
+        block_size = keys.shape[0]
+        key_index = start + jnp.arange(block_size, dtype=jnp.int32)
+        key_segment, unused_where = doc_layout(key_index, doc_starts)
+        allowed = (key_index[None, :] <= query_index[:, None]) & (
+            key_segment[None, :] == query_segment[:, None]
+        )
+        raw = (
+            jnp.einsum("qhd,kd->hqk", query_heads, keys, preferred_element_type=jnp.float32) * scale
+        )
+        return (raw, allowed[None])
+
+    def attend(carry, piece, start):
+        keys, values = piece
+
+        def work(state):
+            running, total, accum = state
+            raw, allowed = scores_for(keys, start)
+            masked = jnp.where(allowed, raw, FLOOR_SCORE)
+            newest = jnp.maximum(running, jnp.max(masked, axis=-1))
+            factor = jnp.exp(running - newest)
+            weights = jnp.where(allowed, jnp.exp(masked - newest[..., None]), 0.0)
+            total = total * factor + jnp.sum(weights, axis=-1)
+            update = jnp.einsum(
+                "hqk,kd->qhd",
+                weights.astype(jnp.bfloat16),
+                values,
+                preferred_element_type=jnp.float32,
+            )
+            accum = accum * factor.T[:, :, None] + update
+            return (newest, total, accum)
+
+        return lax.cond(start <= last_query, work, lambda state: state, carry)
+
+    start_state = (
+        jnp.full((head_group, rows), FLOOR_SCORE, jnp.float32),
+        jnp.zeros((head_group, rows), jnp.float32),
+        jnp.zeros((rows, head_group, HEAD_SIZE), jnp.float32),
+    )
+    running, total, accum = in_blocks(
+        attend,
+        start_state,
+        (
+            lax.all_gather(key_rows, "blk", axis=0, tiled=True),
+            lax.all_gather(value_rows, "blk", axis=0, tiled=True),
+        ),
+        rows,
+    )
+    attn_full = accum / total.T[:, :, None]
+    log_total = running + jnp.log(total)
+    out_send = attn_full.astype(jnp.bfloat16).reshape(rows, 1, head_group * HEAD_SIZE)
+    out_tok = lax.all_to_all(out_send, "head", split_axis=0, concat_axis=1, tiled=True).reshape(
+        count_per_token, QUERY_HEADS * HEAD_SIZE
+    )
+    residual = inputs + product(out_tok, out_w)
+    normed_two_low = rms_norm(residual, gain_two).astype(jnp.bfloat16)
+    weight = jnp.stack([keep_mask * (span * 1.0 / count_all), keep_mask], axis=1)
+    final, error, grad_normed_two, grad_final, dwin, dwout = run_experts(
+        normed_two_low,
+        residual,
+        teacher.reshape(count_per_token, width),
+        weight,
+        gate_plane,
+        win.reshape(1536, 768),
+        wout.reshape(384, 1536),
+    )
+    loss = error[0, 0] / (width * count_all)
+    unused_value, pull_two = jax.vjp(rms_norm, residual, gain_two)
+    grad_res_norm, grad_gain_two = pull_two(grad_normed_two)
+    grad_residual = grad_final + grad_res_norm
+    grad_attn_low = grad_residual.astype(jnp.bfloat16)
+    grad_out_w = jnp.einsum("tk,td->kd", out_tok, grad_attn_low, preferred_element_type=jnp.float32)
+    output_gradient_token = jnp.einsum(
+        "td,kd->tk", grad_attn_low, out_w, preferred_element_type=jnp.float32
+    ).astype(jnp.bfloat16)
+    grad_out_grp = lax.all_to_all(
+        output_gradient_token.reshape(count_per_token, KEY_VALUE_HEADS, head_group * HEAD_SIZE),
+        "head",
+        split_axis=1,
+        concat_axis=0,
+        tiled=True,
+    ).reshape(rows, head_group, HEAD_SIZE)
+    delta = jnp.einsum(
+        "qhd,qhd->hq", grad_out_grp.astype(jnp.float32), attn_full, precision=highest
+    )
+
+    def attend_back(carry, piece, start):
+        keys, values = piece
+
+        def work(state):
+            grad_query, grad_keys, grad_values = state
+            raw, allowed = scores_for(keys, start)
+            weights = jnp.where(allowed, jnp.exp(raw - log_total[..., None]), 0.0)
+            grad_weights = jnp.einsum(
+                "qhd,kd->hqk", grad_out_grp, values, preferred_element_type=jnp.float32
+            )
+            grad_raw = (weights * (grad_weights - delta[..., None])).astype(jnp.bfloat16)
+            grad_query = (
+                grad_query
+                + jnp.einsum("hqk,kd->qhd", grad_raw, keys, preferred_element_type=jnp.float32)
+                * scale
+            )
+            key_part = (
+                jnp.einsum("hqk,qhd->kd", grad_raw, query_heads, preferred_element_type=jnp.float32)
+                * scale
+            )
+            value_part = jnp.einsum(
+                "hqk,qhd->kd",
+                weights.astype(jnp.bfloat16),
+                grad_out_grp,
+                preferred_element_type=jnp.float32,
+            )
+            block_size = keys.shape[0]
+            grad_keys = lax.dynamic_update_slice_in_dim(
+                grad_keys,
+                lax.dynamic_slice_in_dim(grad_keys, start, block_size, 0) + key_part,
+                start,
+                0,
+            )
+            grad_values = lax.dynamic_update_slice_in_dim(
+                grad_values,
+                lax.dynamic_slice_in_dim(grad_values, start, block_size, 0) + value_part,
+                start,
+                0,
+            )
+            return (grad_query, grad_keys, grad_values)
+
+        return lax.cond(start <= last_query, work, lambda state: state, carry)
+
+    back_state = (
+        jnp.zeros((rows, head_group, HEAD_SIZE), jnp.float32),
+        jnp.zeros((span, HEAD_SIZE), jnp.float32),
+        jnp.zeros((span, HEAD_SIZE), jnp.float32),
+    )
+    grad_query, grad_keys_full, grad_values_full = in_blocks(
+        attend_back,
+        back_state,
+        (
+            lax.all_gather(key_rows, "blk", axis=0, tiled=True),
+            lax.all_gather(value_rows, "blk", axis=0, tiled=True),
+        ),
+        rows,
+    )
+    grad_keys, grad_values = (
+        lax.psum_scatter(grad_keys_full, "blk", scatter_dimension=0, tiled=True),
+        lax.psum_scatter(grad_values_full, "blk", scatter_dimension=0, tiled=True),
+    )
+    grad_query_lin = (
+        rotary_apply(grad_query, query_where, -1.0)
+        .astype(jnp.bfloat16)
+        .reshape(rows, 1, head_group * HEAD_SIZE)
+    )
+    grad_key_lin = rotary_apply(grad_keys.reshape(rows, 1, HEAD_SIZE), query_where, -1.0).astype(
+        jnp.bfloat16
+    )
+    grad_value_lin = grad_values.astype(jnp.bfloat16).reshape(rows, 1, HEAD_SIZE)
+    back_query, key_backward, value_backward = (
+        lax.all_to_all(grad_query_lin, "head", split_axis=0, concat_axis=1, tiled=True),
+        lax.all_to_all(grad_key_lin, "head", split_axis=0, concat_axis=1, tiled=True),
+        lax.all_to_all(grad_value_lin, "head", split_axis=0, concat_axis=1, tiled=True),
+    )
+    back_query = back_query.reshape(count_per_token, QUERY_HEADS * HEAD_SIZE)
+    key_backward = key_backward.reshape(count_per_token, KEY_VALUE_HEADS * HEAD_SIZE)
+    value_backward = value_backward.reshape(count_per_token, KEY_VALUE_HEADS * HEAD_SIZE)
+    back = jnp.concatenate([back_query, key_backward, value_backward], axis=1)
+    grad_qkv = jnp.einsum("td,tk->dk", normed_low, back, preferred_element_type=jnp.float32)
+    grad_normed_one = jnp.einsum(
+        "tk,dk->td", back, flat[:, :2048], preferred_element_type=jnp.float32
+    )
+    unused_value, pull_one = jax.vjp(rms_norm, inputs, gain_one)
+    grad_in_norm, grad_gain_one = pull_one(grad_normed_one)
+    grad_inputs = grad_residual + grad_in_norm
+    tail = jnp.where(
+        column == 0, grad_gain_one[:, None], jnp.where(column == 1, grad_gain_two[:, None], 0.0)
+    )
+    packed = jnp.concatenate([grad_qkv, grad_out_w, tail], axis=1).astype(BF).reshape(32, 48, 3712)
+    packed = jnp.pad(packed, ((0, 0), (0, 0), (0, 128)))
+    sums, gup, gdown = return_grads(packed, dwin.reshape(2, 16, 48, 768), dwout.reshape(16, 48, 768))
+    shape = states.shape
+    return (
+        final.reshape(shape),
+        loss,
+        grad_inputs.reshape(shape),
+        sums[:, 3584],
+        sums[:, :1536],
+        sums[:, 1536:1792],
+        sums[:, 1792:2048],
+        sums[:, 2048:3584],
+        sums[:, 3585],
+        gup.astype(F32),
+        gdown.astype(F32).reshape(E, 24, 1536),
+    )
+
+
 def solution(mesh):
     in_specs = (
         P("blk", "head", None, None),
@@ -419,6 +1438,8 @@
         P(None, ("head", "blk"), None),
         P(None, ("head", "blk"), None),
     )
+    sizes = dict(mesh.shape)
+    plan = per_device if sizes == {"head": 2, "blk": 4 * NZ} else per_device_plain
     return jax.shard_map(
-        per_device, mesh=mesh, in_specs=in_specs, out_specs=out_specs, check_vma=False
-    )
+        plan, mesh=mesh, in_specs=in_specs, out_specs=out_specs, check_vma=False
+    )

time: 2460 us -> 943 us (0.38)
  waiting for transfers between devices: 1960 us -> 266 us
  Pallas kernels: 0 us -> 488 us
  blocking collectives: 239 us -> 15.1 us
  matrix products: 164 us -> 35.9 us
  local copies, waits for them, and re-layouts: 30.5 us -> 58.6 us
    reduce_scatter x6 -> x0, waiting for transfers between devices: 1380 us -> none  [the longest x1 667 us: per_device(): lax.psum_scatter(grad_up, ('head', 'blk'), scatter_dimension=1, tiled=True)]
    pallas_call x0 -> x3, Pallas kernels: none -> 488 us  [the longest x1 237 us: run_experts(): pl.pallas_call(experts_kernel, out_shape=(jax.ShapeDtypeStruct(wide, BF),...]
    all_gather x4 -> x0, waiting for transfers between devices: 322 us -> none  [the longest x1 212 us: per_device(): lax.all_gather(expert_in, ('head', 'blk'), axis=1, tiled=True)]
    dot_general x18 -> x2, matrix products: 136 us -> 7.72 us  [the longest x1 5.93 us: per_device(): jnp.einsum('tk,dk->td', back, flat[:, :2048], preferred_element_type=jnp....]
    all_gather x2 -> x0, blocking collectives: 87.8 us -> none  [the longest x1 46.5 us: per_device(): lax.all_gather(key_weight, ('head', 'blk'), axis=0, tiled=True)]
    psum x2 -> x0, blocking collectives: 76.6 us -> none  [per_device(): count_all, error_all = lax.psum((local_count, local_error), ('head', 'blk'))]
    all_gather x1, waiting for transfers between devices: 0.02 us -> 38.1 us  [per_device(): lax.all_gather(value_rows, 'blk', axis=0, tiled=True)]
    unnamed x1 -> x0, blocking collectives: 37.9 us -> none
  transfers between devices with their start and end apart: 17 -> 10, of which waited for: 13 -> 7; matrix products, arithmetic and copies ran while one was open for 5% -> 5% of each run, Pallas kernels for 0% -> 0%
where the time goes in v1:
time: 943 us; the launch traced here: 934 us
  Pallas kernels  488 us (52%)
  waiting for transfers between devices  266 us (28%)
  local copies, waits for them, and re-layouts  58.6 us (6%)
  matrix products  35.9 us (4%)
  other arithmetic  29.7 us (3%)
  starting transfers between devices  22.1 us (2%)
  between operations  17.8 us (2%)
  blocking collectives  15.1 us (2%)
    pallas_call x1, Pallas kernels, run_experts(): pl.pallas_call(experts_kernel, out_shape=(jax.ShapeDtypeStruct(wide, BF),...  237 us
    reduce_scatter x1, waiting for transfers between devices, per_device(): lax.psum_scatter(grad_keys_full, 'blk', scatter_dimension=0, tiled=True)  155 us
    pallas_call x1, Pallas kernels, return_grads(): pl.pallas_call(grads_kernel, out_shape=(jax.ShapeDtypeStruct(shard, F32),...  129 us
    pallas_call x1, Pallas kernels, bring_weights(): pl.pallas_call(weights_kernel, out_shape=(jax.ShapeDtypeStruct((32, 48, c...  121 us
    reduce_scatter x1, waiting for transfers between devices, per_device(): lax.psum_scatter(grad_values_full, 'blk', scatter_dimension=0, tiled=True)  58.7 us
    all_gather x1, waiting for transfers between devices, per_device(): lax.all_gather(value_rows, 'blk', axis=0, tiled=True)  38.1 us
  transfers between devices with their start and end apart: 10, of which 7 were waited for; matrix products, arithmetic and copies ran while one was open for 5% of the time, Pallas kernels for 0%

profile of v1, /device:TPU:0, one launch (start us, length us, event | category | flops | bytes accessed | tf_op | source)
XLA Modules:
  0.0 934.2 jit_solution(14196692004037687119)
XLA Ops:
  15.6 121.4 %bring_weights.1 = (bf16[32,48,3840]{2,1,0:T(8,128)(2,1)S(1)}, bf16[2,16,48,768]{3,2,1,0:T(8,128)(2,1)S(1)}, bf16[16,48,768]{2,1,0:T(8,128)(2,1)S(1)}) custom-call(bf16[48,3840]{1,0:T(8,128)(2,1)S(1)} %constant_dynamic-update-slice_fusion.dense, bf16[8,48,1536]{2,1,0:T(8,128)(2,1)S(1)} %copy-done.2, bf16[8,48,768]{2,1,0:T(8,128)(2,1)S(1)} %reshape.611.down), custom_call_target="tpu_custom_call" | custom-call | tf_op jit(solution)/shard_map/bring_weights/pallas_call | solution.py:748
  138.4 4.3 copy-done
  146.5 8.0 all_to_all.120
  156.8 7.2 all_to_all.121
  164.0 4.9 slice_bitcast_fusion
  168.9 6.6 copy.181
  175.5 3.8 fusion.81
  180.2 3.5 all-to-all-start.1
  190.6 38.1 %all-gather.5.cloned.1.call-done = bf16[4096,128]{1,0:T(8,128)(2,1)} async-done(((bf16[256,128]{1,0:T(8,128)(2,1)}), bf16[4096,128]{1,0:T(8,128)(2,1)}) %all-gather.5.cloned.1.call-update) | async-done | bytes 1048592 | tf_op jit(solution)/shard_map/all_gather | solution.py:1261
  228.8 4.4 while.36
  236.6 4.5 all-to-all-start.3
  252.8 236.9 %experts.1 = (bf16[128,1536]{1,0:T(8,128)(2,1)}, f32[8,128]{1,0:T(8,128)}, f32[128,1536]{1,0:T(8,128)}, f32[128,1536]{1,0:T(8,128)}, bf16[1536,768]{1,0:T(8,128)(2,1)}, /*index=5*/bf16[384,1536]{1,0:T(8,128)(2,1)}) custom-call(bf16[128,1536]{1,0:T(8,128)(2,1)} %multiply_convert_fusion.n2, f32[128,1536]{1,0:T(8,128)} %copy-done.3, ...), custom_call_target="tpu_custom_call" | custom-call | tf_op jit(solution)/shard_map/experts/pallas_call | solution.py:961
  493.4 4.0 fusion.54
  502.6 5.0 all-to-all-done.4
  511.6 8.7 while.37
  511.7 8.0 conditional.7
  535.7 3.5 convolution_convert_fusion.1
  542.5 155.3 %reduce-scatter.3.cloned.1.call-done = f32[256,128]{0,1:T(8,128)} async-done(((f32[4096,128]{0,1:T(8,128)}), f32[256,128]{0,1:T(8,128)}) %reduce-scatter.3.cloned.1.call-update) | async-done | bytes 131088 | tf_op jit(solution)/shard_map/reduce_scatter | solution.py:1361
  703.7 58.7 %reduce-scatter.5.cloned.1.call-done = f32[256,128]{1,0:T(8,128)} async-done(((f32[4096,128]{1,0:T(8,128)}), f32[256,128]{1,0:T(8,128)}) %reduce-scatter.5.cloned.1.call-update) | async-done | bytes 131088 | tf_op jit(solution)/shard_map/reduce_scatter | solution.py:1362
  764.7 3.6 all-to-all-start.7
  768.5 3.6 all-to-all-done.7
  772.3 5.9 fusion.65
  783.4 5.0 fusion.44.dense
  788.5 129.4 %return_grads.1 = (f32[48,3840]{1,0:T(8,128)}, bf16[8,48,1536]{2,1,0:T(8,128)(2,1)}, bf16[8,48,768]{2,1,0:T(8,128)(2,1)}) custom-call(bf16[32,48,3840]{2,1,0:T(8,128)(2,1)} %fusion.44.dense, bf16[2,16,48,768]{3,2,1,0:T(8,128)(2,1)} %bitcast.213, bf16[16,48,768]{2,1,0:T(8,128)(2,1)} %reshape.633.dwout), custom_call_target="tpu_custom_call" | custom-call | tf_op jit(solution)/shard_map/return_grads/pallas_call | solution.py:1104
  (291 shorter events, 105.3 us)
Async XLA Ops:
  7.2 8.4 copy-start.2
  7.2 183.4 %all-gather.3.cloned.1.call-start = ((), (), s32[]{:S(2)}) async-start(), calls=%async_computation.10 | async-start | bytes 1114112 | tf_op jit(solution)/shard_map/all_gather | solution.py:1260
  7.2 8.2 copy-start.26
  7.3 8.2 copy-start.28
  144.4 31.1 %copy-start.14 = (f32[1536]{0:T(1024)}, f32[1536]{0:T(1024)S(1)}, u32[]{:S(2)}) copy-start(f32[1536]{0:T(1024)S(1)} %convert_reduce_fusion.4) | copy-start | bytes 18436
  144.6 19.4 %copy-start.30 = (f32[128]{0:T(128)}, f32[128]{0:T(128)S(1)}, u32[]{:S(2)}) copy-start(f32[128]{0:T(128)S(1)} %fusion.66) | copy-start | bytes 1540
  144.6 30.9 %copy-start.24 = (f32[128]{0:T(128)}, f32[128]{0:T(128)S(1)}, u32[]{:S(2)}) copy-start(f32[128]{0:T(128)S(1)} %fusion.98) | copy-start | bytes 1540
  155.3 73.4 %all-gather.5.cloned.1.call-start = ((), (), s32[]{:S(2)}) async-start(), calls=%async_computation.11 | async-start | bytes 1114112 | tf_op jit(solution)/shard_map/all_gather | solution.py:1261
  179.3 9.0 copy-start.32
  180.2 9.5 %all-to-all-start.1 = ((bf16[128,2,768]{0,2,1:T(8,128)(2,1)}), bf16[128,2,768]{0,2,1:T(8,128)(2,1)S(1)}, u32[]{:S(2)}, u32[]{:S(2)}) async-start(bf16[128,2,768]{0,2,1:T(8,128)(2,1)} %bitcast.28), calls=%async_computation.1 | async-start | bytes 786432 | tf_op jit(solution)/shard_map/all_to_all | solution.py:1209
  236.6 8.5 copy-start.18
  236.6 10.3 %all-to-all-start.3 = ((bf16[2,2,49152]{2,1,0:T(2,128)(2,1)}), bf16[2,2,49152]{2,1,0:T(2,128)(2,1)}, u32[]{:S(2)}, u32[]{:S(2)}) async-start(bf16[2,2,49152]{2,1,0:T(2,128)(2,1)} %reshape.665), calls=%async_computation.3 | async-start | bytes 786432 | tf_op jit(solution)/shard_map/all_to_all | solution.py:1268
  498.3 9.3 all-to-all-start.4
  501.8 196.0 %reduce-scatter.3.cloned.1.call-start = ((), (), s32[]{:S(2)}) async-start(), calls=%async_computation.12 | async-start | bytes 2228224 | tf_op jit(solution)/shard_map/reduce_scatter | solution.py:1361
  523.4 239.1 %reduce-scatter.5.cloned.1.call-start = ((), (), s32[]{:S(2)}) async-start(), calls=%async_computation.13 | async-start | bytes 2228224 | tf_op jit(solution)/shard_map/reduce_scatter | solution.py:1362
  530.2 5.5 copy-start.8
  532.2 9.3 all-to-all-start.5
  542.4 229.9 %copy-start.15 = (f32[1536]{0:T(1024)S(1)}, f32[1536]{0:T(1024)}, u32[]{:S(2)}) copy-start(f32[1536]{0:T(1024)} %copy-done.14) | copy-start | bytes 18436
  542.4 229.9 %copy-start.25 = (f32[128]{0:T(128)S(1)}, f32[128]{0:T(128)}, u32[]{:S(2)}) copy-start(f32[128]{0:T(128)} %copy-done.24) | copy-start | bytes 1540
  700.4 64.3 %all-to-all-start.6 = ((bf16[2,2,8192]{2,1,0:T(2,128)(2,1)}), bf16[2,2,8192]{2,1,0:T(2,128)(2,1)S(1)}, u32[]{:S(2)}, u32[]{:S(2)}) async-start(bf16[2,2,8192]{2,1,0:T(2,128)(2,1)} %reshape.669), calls=%async_computation.7 | async-start | bytes 131072 | tf_op jit(solution)/shard_map/all_to_all | solution.py:1375
  764.7 7.4 all-to-all-start.7
  772.3 5.9 copy-start.31
  778.4 5.0 slice-start
  917.9 5.0 copy-start.9
  (21 other events, 48.5 us)
Sparse Core Ops, SparseCore 0:
  155.4 34.2 all-gather.2
  191.9 36.8 all-gather.4
  523.5 174.2 reduce-scatter.2
  701.8 60.5 reduce-scatter.4

commit v2 on v0

--- a/solution.py
+++ b/solution.py
@@ -1,6 +1,10 @@
+import functools
+
 import jax
 import jax.numpy as jnp
 from jax import lax
+from jax.experimental import pallas as pl
+from jax.experimental.pallas import tpu as pltpu
 from jax.sharding import PartitionSpec as P
 
 QUERY_HEADS = 12
@@ -10,10 +14,13 @@
 E = 8
 CAP = 96
 
-
 ROTARY_BASE = 10000.0
 FLOOR_SCORE = -1e30
 
+MESH = pl.DeviceIdType.MESH
+NZ = 4
+BF = jnp.bfloat16
+F32 = jnp.float32
 
 def product(left, right):
     return jnp.dot(left, right, preferred_element_type=jnp.float32)
@@ -59,7 +66,7 @@
     return lax.fori_loop(0, count_blocks, turn, carry)
 
 
-def per_device(
+def per_device_plain(
     states,
     teacher,
     valid,
@@ -389,6 +396,1129 @@
     )
 
 
+class Place:
+    def __init__(self):
+        self.x = lax.axis_index("head")
+        self.b = lax.axis_index("blk")
+        self.c = self.b % 2
+        self.y = (self.b // 2) % 2
+        self.z = self.b // 4
+
+    def near(self, kind):
+        x, y, z, c = self.x, self.y, self.z, self.c
+        if kind == "up":
+            z = jnp.minimum(z + 1, NZ - 1)
+        elif kind == "down":
+            z = jnp.maximum(z - 1, 0)
+        elif kind == "y":
+            y = 1 - y
+        elif kind == "x":
+            x = 1 - x
+        elif kind == "c":
+            c = 1 - c
+        return (x, z * 4 + y * 2 + c)
+
+    def blk(self, z, y, c):
+        return z * 4 + y * 2 + c
+
+    def outward(self, j):
+        inner = jnp.where(j < 2, 1 - j, j)
+        order = jnp.where((self.z == 0) | (self.z == NZ - 1), j, inner)
+        return jnp.where(self.z < 2, order, NZ - 1 - order)
+
+    def inward(self, j):
+        inner = jnp.where(j == 0, 3, jnp.where(j == 1, 0, jnp.where(j == 2, 2, 1)))
+        order = jnp.where((self.z == 0) | (self.z == NZ - 1), NZ - 1 - j, inner)
+        return jnp.where(self.z < 2, order, NZ - 1 - order)
+
+
+def greet_all(me):
+    barrier = pltpu.get_barrier_semaphore()
+
+    def one(k, carry):
+        pl.semaphore_signal(
+            barrier, inc=1, device_id=((me.x + k // 16) % 2, (me.b + k) % 16), device_id_type=MESH
+        )
+        return carry
+
+    lax.fori_loop(1, 32, one, 0)
+    pl.semaphore_wait(barrier, 31)
+
+
+def remote(src, dst, send, recv, to):
+    return pltpu.make_async_remote_copy(
+        src_ref=src, dst_ref=dst, send_sem=send, recv_sem=recv, device_id=to, device_id_type=MESH
+    )
+
+
+def arrived(ref, sem, me):
+    remote(ref, ref, sem, sem, me.near("c")).wait_recv()
+
+
+def left(ref, sem, me):
+    remote(ref, ref, sem, sem, me.near("c")).wait_send()
+
+
+class Gather:
+    def __init__(self, me, g, index, send, recv, causal=False):
+        self.me, self.g, self.index, self.send, self.recv, self.causal = me, g, index, send, recv, causal
+        half = g.shape[2] // 2
+        self.first, self.second = pl.ds(0, half), pl.ds(half, half)
+
+    def place(self, j):
+        return self.me.z - j if self.causal else self.me.outward(j)
+
+    def valid(self, j):
+        return (j >= 0) & (j <= (self.me.z if self.causal else NZ - 1))
+
+    def ups(self, zz):
+        if self.causal:
+            return self.me.z < NZ - 1
+        return (zz <= self.me.z) & (self.me.z < NZ - 1)
+
+    def downs(self, zz):
+        return (zz >= self.me.z) & (self.me.z > 0)
+
+    def put(self, j, kind, n, s, cols=None, slot=0):
+        ref = self.g.at[s] if cols is None else self.g.at[s, :, cols]
+        remote(ref, ref, self.send.at[j, n], self.recv.at[s, slot], self.me.near(kind)).start()
+
+    def wait(self, s):
+        arrived(self.g.at[s], self.recv.at[s, 0], self.me)
+
+    def turn(self, j):
+        me, index = self.me, self.index
+        x, y, c = me.x, me.y, me.c
+
+        @pl.when(self.valid(j) & (j > 0))
+        def _():
+            self.wait(index(x, self.place(j), y, c))
+
+        @pl.when(self.valid(j))
+        def _():
+            zz = self.place(j)
+            own = index(x, zz, y, c)
+            pl.when(self.ups(zz))(lambda: self.put(j, "up", 0, own))
+            if not self.causal:
+                pl.when(self.downs(zz))(lambda: self.put(j, "down", 1, own))
+            self.put(j, "y", 2, own)
+            self.put(j, "x", 3, own)
+            self.put(j, "c", 6, own)
+
+        @pl.when(self.valid(j - 1))
+        def _():
+            i = j - 1
+            zp = self.place(i)
+            s = index(x, zp, 1 - y, c)
+            self.wait(s)
+            self.put(i, "x", 4, s, self.first, 0)
+            self.put(i, "c", 7, s)
+            t = index(1 - x, zp, y, c)
+            self.wait(t)
+            self.put(i, "y", 5, t, self.second, 1)
+            self.put(i, "c", 8, t)
+
+        @pl.when(self.valid(j - 2))
+        def _():
+            i = j - 2
+            s = index(1 - x, self.place(i), 1 - y, c)
+            arrived(self.g.at[s, :, self.first], self.recv.at[s, 0], me)
+            arrived(self.g.at[s, :, self.second], self.recv.at[s, 1], me)
+            self.put(i, "c", 9, s)
+
+    def from_core(self, j):
+        me = self.me
+        for xx in (me.x, 1 - me.x):
+            for yy in (me.y, 1 - me.y):
+                self.wait(self.index(xx, self.place(j), yy, 1 - me.c))
+
+    def close(self, cores=True):
+        me = self.me
+
+        def one(j, carry):
+            @pl.when(self.valid(j))
+            def _():
+                zz = self.place(j)
+                own = self.index(me.x, zz, me.y, me.c)
+                whole, part = self.g.at[own], self.g.at[own, :, self.first]
+                pl.when(self.ups(zz))(lambda: left(whole, self.send.at[j, 0], me))
+                if not self.causal:
+                    pl.when(self.downs(zz))(lambda: left(whole, self.send.at[j, 1], me))
+                for n in (2, 3, 6, 7, 8, 9):
+                    left(whole, self.send.at[j, n], me)
+                for n in (4, 5):
+                    left(part, self.send.at[j, n], me)
+                if cores:
+                    self.from_core(j)
+
+            return carry
+
+        lax.fori_loop(0, 4, one, 0)
+
+    def run(self, between=None):
+        def one(j, carry):
+            self.turn(j)
+            if between is not None:
+                between(j)
+            return carry
+
+        lax.fori_loop(0, 6, one, 0)
+        self.close()
+
+
+class Sum:
+    def __init__(self, me, part, index, out, room, sems, causal=False):
+        self.me, self.part, self.index, self.out, self.causal = me, part, index, out, causal
+        self.rc, self.rd, self.rn, self.rz, self.acc = room
+        self.sc, self.ss, self.vc, self.vn, self.vz = sems
+        self.half = part.shape[2] // 2
+        self.first, self.second = pl.ds(0, self.half), pl.ds(self.half, self.half)
+
+    @staticmethod
+    def room(rows, columns):
+        return [
+            pltpu.VMEM((16, rows, columns), BF),
+            pltpu.VMEM((2, 4, rows, columns // 2), BF),
+            pltpu.VMEM((2, 4, rows, columns), BF),
+            pltpu.VMEM((5, rows, columns), BF),
+            pltpu.VMEM((rows, columns), F32),
+            DMA((16,)),
+            DMA((4, 6)),
+            DMA((16,)),
+            DMA((4, 4)),
+            DMA((5,)),
+        ]
+
+    def place(self, j):
+        return j if self.causal else self.me.inward(j)
+
+    def valid(self, j):
+        return (j >= 0) & (j <= (self.me.z if self.causal else NZ - 1))
+
+    def slot(self, xx, zz, yy):
+        return zz * 4 + xx * 2 + yy
+
+    def lead(self, j):
+        me = self.me
+        zz = self.place(j)
+        for xx in (1 - me.x, me.x):
+            for yy in (1 - me.y, me.y):
+                k = self.slot(xx, zz, yy)
+                src = self.part.at[self.index(xx, zz, yy, 1 - me.c)]
+                remote(src, self.rc.at[k], self.sc.at[k], self.vc.at[k], me.near("c")).start()
+
+    def with_core(self, xx, zz, yy):
+        k = self.slot(xx, zz, yy)
+        arrived(self.rc.at[k], self.vc.at[k], self.me)
+        return k, self.part[self.index(xx, zz, yy, self.me.c)].astype(F32) + self.rc[k].astype(F32)
+
+    def turn(self, j):
+        me, half, first, second = self.me, self.half, self.first, self.second
+        rc, rd, rn, ss, vn = self.rc, self.rd, self.rn, self.ss, self.vn
+        x, y = me.x, me.y
+
+        @pl.when(self.valid(j))
+        def _():
+            zz = self.place(j)
+            k, total = self.with_core(1 - x, zz, 1 - y)
+            rc[k] = total.astype(BF)
+            remote(rc.at[k, :, first], rd.at[0, zz], ss.at[j, 0], vn.at[zz, 0], me.near("x")).start()
+            remote(rc.at[k, :, second], rd.at[1, zz], ss.at[j, 1], vn.at[zz, 1], me.near("y")).start()
+
+        @pl.when(self.valid(j - 1))
+        def _():
+            i = j - 1
+            zz = self.place(i)
+            k, total = self.with_core(x, zz, 1 - y)
+            arrived(rd.at[0, zz], vn.at[zz, 0], me)
+            rc[k, :, second] = total[:, half:].astype(BF)
+            rc[k, :, first] = (total[:, :half] + rd[0, zz].astype(F32)).astype(BF)
+            remote(rc.at[k], rn.at[0, zz], ss.at[i, 2], vn.at[zz, 2], me.near("y")).start()
+            k, total = self.with_core(1 - x, zz, y)
+            arrived(rd.at[1, zz], vn.at[zz, 1], me)
+            rc[k, :, first] = total[:, :half].astype(BF)
+            rc[k, :, second] = (total[:, half:] + rd[1, zz].astype(F32)).astype(BF)
+            remote(rc.at[k], rn.at[1, zz], ss.at[i, 3], vn.at[zz, 3], me.near("x")).start()
+
+        @pl.when(self.valid(j - 2))
+        def _():
+            i = j - 2
+            zz = self.place(i)
+            k, total = self.with_core(x, zz, y)
+            arrived(rn.at[0, zz], vn.at[zz, 2], me)
+            arrived(rn.at[1, zz], vn.at[zz, 3], me)
+            self.acc[...] = total + rn[0, zz].astype(F32) + rn[1, zz].astype(F32)
+            along_z(me, i, zz, self.acc, rc.at[k], self.rz, ss, 4, self.vz, self.causal)
+
+            @pl.when(zz == me.z)
+            def _():
+                self.out[...] = self.acc[...]
+
+    def close(self):
+        me = self.me
+        whole, piece = self.rc.at[0], self.rc.at[0, :, self.first]
+
+        def one(j, carry):
+            @pl.when(self.valid(j))
+            def _():
+                zz = self.place(j)
+                for xx in (1 - me.x, me.x):
+                    for yy in (1 - me.y, me.y):
+                        left(whole, self.sc.at[self.slot(xx, zz, yy)], me)
+                for n in (0, 1):
+                    left(piece, self.ss.at[j, n], me)
+                for n in (2, 3):
+                    left(whole, self.ss.at[j, n], me)
+                if not self.causal:
+                    pl.when(zz > me.z)(lambda: left(whole, self.ss.at[j, 4], me))
+                pl.when(zz < me.z)(lambda: left(whole, self.ss.at[j, 5], me))
+
+            return carry
+
+        lax.fori_loop(0, 4, one, 0)
+
+    def run(self, between=None):
+        def one(j, carry):
+            self.lead(j)
+            return carry
+
+        lax.fori_loop(0, 4, one, 0)
+
+        def two(j, carry):
+            self.turn(j)
+            if between is not None:
+                between(j)
+            return carry
+
+        lax.fori_loop(0, 6, two, 0)
+        self.close()
+
+
+def along_z(me, i, zz, acc, room, rz, ss, n, vz, causal=False):
+    z = me.z
+
+    def add(slot):
+        arrived(rz.at[slot], vz.at[slot], me)
+        acc[...] += rz[slot].astype(F32)
+
+    if not causal:
+        pl.when((zz >= z) & (z > 0))(lambda: add(zz))
+    pl.when((zz < z) & (z < NZ - 1))(lambda: add(zz))
+    pl.when((zz == z) & (z < NZ - 1))(lambda: add(4))
+
+    if not causal:
+
+        @pl.when(zz > z)
+        def _():
+            room[...] = acc[...].astype(BF)
+            remote(room, rz.at[zz], ss.at[i, n], vz.at[zz], me.near("up")).start()
+
+    @pl.when(zz < z)
+    def _():
+        room[...] = acc[...].astype(BF)
+        there = jnp.where(zz == z - 1, 4, zz)
+        remote(room, rz.at[there], ss.at[i, n + 1], vz.at[there], me.near("down")).start()
+
+
+def by_weight(x, z, y, c):
+    return x * 16 + z * 4 + y * 2 + c
+
+
+def by_token(x, z, y, c):
+    return (z * 4 + y * 2 + c) * 2 + x
+
+
+ANY = pl.BlockSpec(memory_space=pl.ANY)
+VMEM = pl.BlockSpec(memory_space=pltpu.VMEM)
+DMA = pltpu.SemaphoreType.DMA
+
+
+def params(number, mib):
+    return pltpu.CompilerParams(
+        collective_id=number, has_side_effects=True, vmem_limit_bytes=mib << 20
+    )
+
+
+NT = (((1,), (1,)), ((), ()))
+TN = (((0,), (0,)), ((), ()))
+GROUP = QUERY_HEADS // KEY_VALUE_HEADS
+LANES = GROUP * 128
+SCALE = HEAD_SIZE ** (-0.5)
+POWER = SCALE * 1.4426950408889634
+
+
+def turned(u, cosine, sine):
+    return u * cosine + pltpu.roll(u, 64, 1) * sine
+
+
+def allowed_keys(start, bounds):
+    key = start + lax.broadcasted_iota(jnp.int32, (256, LANES), 0)
+    return (key >= bounds[0:1, :]) & (key <= bounds[1:2, :])
+
+
+def front_kernel(
+    states, wq, wk, wv, wo, extra, up, down, cosine, sine, bounds,
+    gq_out, go_out, kv_out, win, wout, h, n2, n1, qs, o_out, lse,
+    gq, go, kv, top, total, acc,
+    own_sem, qsend, qrecv, gsend, grecv, ksend, krecv, asend, arecv, xsend, xrecv, osend, orecv,
+):
+    me = Place()
+    x, y, z, b, c = me.x, me.y, me.z, me.b, me.c
+    here = by_weight(x, z, y, c)
+    mine = [
+        pltpu.make_async_copy(wq, gq.at[here, :, pl.ds(0, 1536)], own_sem.at[0]),
+        pltpu.make_async_copy(wk, gq.at[here, :, pl.ds(1536, 256)], own_sem.at[1]),
+        pltpu.make_async_copy(wv, gq.at[here, :, pl.ds(1792, 256)], own_sem.at[2]),
+        pltpu.make_async_copy(extra, gq.at[here, :, pl.ds(2048, 256)], own_sem.at[3]),
+        pltpu.make_async_copy(wo, go.at[here], own_sem.at[4]),
+    ]
+    for k in range(2):
+        col = pl.multiple_of(k * 768 + c * 384, 128)
+        mine.append(
+            pltpu.make_async_copy(
+                up.at[b // 2, :, pl.ds(col, 384)], win.at[x, b, :, pl.ds(k * 384, 384)], own_sem.at[5 + k]
+            )
+        )
+    held = pltpu.make_async_copy(down.at[b // 2], wout.at[b], own_sem.at[7])
+    for copy in mine:
+        copy.start()
+    pl.when(c == x)(held.start)
+    greet_all(me)
+    for copy in mine:
+        copy.wait()
+    pl.when(c == x)(held.wait)
+
+    def deal(k, carry):
+        t = (b + k) % 16
+        for n in range(2):
+            col = pl.multiple_of(n * 768 + (t % 2) * 384, 128)
+            remote(
+                up.at[t // 2, :, pl.ds(col, 384)],
+                win.at[x, b, :, pl.ds(n * 384, 384)],
+                asend.at[k, n],
+                arecv.at[b, n],
+                (x, t),
+            ).start()
+        pl.when(t % 2 == x)(
+            lambda: remote(down.at[t // 2], wout.at[b], osend.at[k], orecv.at[b], (x, t)).start()
+        )
+        return carry
+
+    def pass_on(k, carry):
+        f = (b + 16 - k) % 16
+
+        @pl.when(k > 0)
+        def _():
+            for n in range(2):
+                arrived(win.at[x, f, :, pl.ds(n * 384, 384)], arecv.at[f, n], me)
+
+        remote(win.at[x, f], win.at[x, f], xsend.at[k], xrecv.at[f], me.near("x")).start()
+
+        @pl.when(c == x)
+        def _():
+            pl.when(k > 0)(lambda: arrived(wout.at[f], orecv.at[f], me))
+            remote(wout.at[f], wout.at[f], osend.at[16 + k], orecv.at[f], me.near("x")).start()
+
+        return carry
+
+    Gather(me, gq, by_weight, qsend, qrecv).run()
+    lax.fori_loop(1, 16, deal, 0)
+    keep = pltpu.make_async_copy(gq, gq_out, own_sem.at[0])
+    keep.start()
+
+    rows = states[...].astype(F32)
+    gains = gq[:, :, pl.ds(2048, 128)].reshape(1536, 128).astype(F32).T
+    n1[...] = (
+        rows * lax.rsqrt(jnp.mean(rows * rows, axis=-1, keepdims=True) + 1e-06) * gains[0:1]
+    ).astype(BF)
+    qkv = jnp.dot(n1[...], gq[:, :, pl.ds(0, 2048)].reshape(1536, 2048), preferred_element_type=F32)
+    cos, sin = cosine[...], sine[...]
+    at = by_token(x, z, y, c)
+    for i in range(2):
+        kv[at, :, i * 128 : i * 128 + 128] = turned(qkv[:, 1536 + i * 128 : 1664 + i * 128], cos, sin).astype(BF)
+        kv[at, :, 256 + i * 128 : 384 + i * 128] = qkv[:, 1792 + i * 128 : 1920 + i * 128].astype(BF)
+    for i in range(QUERY_HEADS):
+        r = (i % GROUP) * 128
+        qs[i // GROUP, r : r + 128] = turned(qkv[:, i * 128 : i * 128 + 128], cos, sin).astype(BF)
+
+    top[...] = jnp.full_like(top, FLOOR_SCORE)
+    total[...] = jnp.zeros_like(total)
+    acc[...] = jnp.zeros_like(acc)
+    keys = Gather(me, kv, by_token, ksend, krecv, causal=True)
+    output = Gather(me, go, by_weight, gsend, grecv)
+
+    def block(n):
+        ok = allowed_keys(n * 256, bounds)
+        for i in range(2):
+            k = kv[pl.ds(n * 2, 2), :, i * 128 : i * 128 + 128].reshape(256, 128)
+            v = kv[pl.ds(n * 2, 2), :, 256 + i * 128 : 384 + i * 128].reshape(256, 128)
+            s = lax.dot_general(k, qs[i], NT, preferred_element_type=F32)
+            s = jnp.where(ok, s, FLOOR_SCORE)
+            old = top[i]
+            new = jnp.maximum(old, jnp.max(s, axis=0, keepdims=True))
+            factor = jnp.exp2((old - new) * POWER)
+            p = jnp.exp2((s - new) * POWER)
+            top[i] = new
+            total[i] = total[i] * factor + jnp.sum(p, axis=0, keepdims=True)
+            acc[i] = acc[i] * factor + lax.dot_general(v, p.astype(BF), TN, preferred_element_type=F32)
+
+    def turn(j, carry):
+        keys.turn(j)
+        output.turn(j - 2)
+
+        @pl.when(j == 4)
+        def _():
+            lax.fori_loop(0, 4, pass_on, 0)
+
+        @pl.when(j == 5)
+        def _():
+            lax.fori_loop(4, 8, pass_on, 0)
+
+        @pl.when(keys.valid(j - 2))
+        def _():
+            i = j - 2
+            keys.from_core(i)
+            zz = z - i
+            last = jnp.where(i == 0, y * 2 + c, 3)
+
+            def one(n, carry):
+                block(zz * 4 + last - n)
+                return carry
+
+            lax.fori_loop(0, last + 1, one, 0)
+
+        return carry
+
+    lax.fori_loop(0, 8, turn, 0)
+    lax.fori_loop(8, 16, pass_on, 0)
+    output.close()
+    keep_o = pltpu.make_async_copy(go, go_out, own_sem.at[1])
+    keep_o.start()
+    keep_k = pltpu.make_async_copy(kv, kv_out, own_sem.at[2])
+    keep_k.start()
+    for i in range(2):
+        lse[i] = top[i] * POWER + jnp.log2(total[i])
+        done = acc[i] / total[i]
+        for r in range(GROUP):
+            col = (i * GROUP + r) * 128
+            o_out[:, col : col + 128] = done[:, r * 128 : r * 128 + 128].T
+    res = rows + jnp.dot(
+        o_out[...].astype(BF), go[...].reshape(1536, 1536), preferred_element_type=F32
+    )
+    h[...] = res
+    n2[...] = (
+        res * lax.rsqrt(jnp.mean(res * res, axis=-1, keepdims=True) + 1e-06) * gains[1:2]
+    ).astype(BF)
+
+    keys.close(False)
+
+    def close(k, carry):
+        slab, piece = win.at[x, b], win.at[x, b, :, pl.ds(0, 384)]
+
+        @pl.when(k > 0)
+        def _():
+            for n in range(2):
+                left(piece, asend.at[k, n], me)
+            pl.when((b + k) % 2 == x)(lambda: left(wout.at[b], osend.at[k], me))
+
+        left(slab, xsend.at[k], me)
+        pl.when(c == x)(lambda: left(wout.at[b], osend.at[16 + k], me))
+        arrived(win.at[1 - x, k], xrecv.at[k], me)
+        pl.when(c != x)(lambda: arrived(wout.at[k], orecv.at[k], me))
+        return carry
+
+    lax.fori_loop(0, 16, close, 0)
+    keep.wait()
+    keep_o.wait()
+    keep_k.wait()
+
+
+def run_front(states, wq, wk, wv, wo, extra, up, down, cosine, sine, bounds):
+    shape = jax.ShapeDtypeStruct
+    return pl.pallas_call(
+        front_kernel,
+        out_shape=(
+            shape((32, 48, 2304), BF),
+            shape((32, 48, 1536), BF),
+            shape((32, 128, 512), BF),
+            shape((2, 16, 48, 768), BF),
+            shape((16, 48, 768), BF),
+            shape((128, 1536), F32),
+            shape((128, 1536), BF),
+            shape((128, 1536), BF),
+            shape((2, LANES, 128), BF),
+            shape((128, 1536), F32),
+            shape((2, 1, LANES), F32),
+        ),
+        in_specs=[VMEM] + [ANY] * 7 + [VMEM] * 3,
+        out_specs=(ANY,) * 5 + (VMEM,) * 6,
+        scratch_shapes=[
+            pltpu.VMEM((32, 48, 2304), BF),
+            pltpu.VMEM((32, 48, 1536), BF),
+            pltpu.VMEM((32, 128, 512), BF),
+            pltpu.VMEM((2, 1, LANES), F32),
+            pltpu.VMEM((2, 1, LANES), F32),
+            pltpu.VMEM((2, 128, LANES), F32),
+            DMA((8,)),
+            DMA((4, 10)),
+            DMA((32, 2)),
+            DMA((4, 10)),
+            DMA((32, 2)),
+            DMA((4, 10)),
+            DMA((32, 2)),
+            DMA((16, 2)),
+            DMA((16, 2)),
+            DMA((16,)),
+            DMA((16,)),
+            DMA((32,)),
+            DMA((16,)),
+        ],
+        compiler_params=params(1, 48),
+        name="front",
+    )(states, wq, wk, wv, wo, extra, up, down, cosine, sine, bounds)
+
+
+GELU_A = 0.7978845608028654
+GELU_B = 0.044715
+
+
+def experts_kernel(
+    n2, h, teacher, weight, gate, win, wout,
+    final, err, dn2, dy_out, dwin, dwout,
+    nall, dyall, pairs, zg, dpairs, part, rc, ry, rz, acc, errs,
+    gsend, grecv, csend, crecv, ysend, yrecv, zsend, zrecv, esend, erecv,
+):
+    me = Place()
+    x, y, z, b, c = me.x, me.y, me.z, me.b, me.c
+    greet_all(me)
+
+    def gather(buf, way, chunk):
+        def put(j, kind, n, s):
+            remote(buf.at[s], buf.at[s], gsend.at[way, j, n], grecv.at[way, s], me.near(kind)).start()
+
+        def turn(j, carry):
+            zz = me.outward(j)
+            own = me.blk(zz, y, c)
+
+            @pl.when((j > 0) & (j < 4))
+            def _():
+                arrived(buf.at[own], grecv.at[way, own], me)
+
+            @pl.when(j < 4)
+            def _():
+                pl.when((zz <= z) & (z < NZ - 1))(lambda: put(j, "up", 0, own))
+                pl.when((zz >= z) & (z > 0))(lambda: put(j, "down", 1, own))
+                put(j, "y", 2, own)
+                put(j, "c", 3, own)
+
+            @pl.when(j > 0)
+            def _():
+                i = j - 1
+                zp = me.outward(i)
+                s = me.blk(zp, 1 - y, c)
+                arrived(buf.at[s], grecv.at[way, s], me)
+                put(i, "c", 4, s)
+
+                def both(n, carry):
+                    yy = (y + n) % 2
+                    s = me.blk(zp, yy, 1 - c)
+                    arrived(buf.at[s], grecv.at[way, s], me)
+                    chunk(zp * 2 + yy)
+                    return carry
+
+                lax.fori_loop(0, 2, both, 0)
+
+            return carry
+
+        lax.fori_loop(0, 5, turn, 0)
+
+        def close(j, carry):
+            zz = me.outward(j)
+            whole = buf.at[b]
+            pl.when((zz <= z) & (z < NZ - 1))(lambda: left(whole, gsend.at[way, j, 0], me))
+            pl.when((zz >= z) & (z > 0))(lambda: left(whole, gsend.at[way, j, 1], me))
+            for n in (2, 3, 4):
+                left(whole, gsend.at[way, j, n], me)
+            return carry
+
+        lax.fori_loop(0, 4, close, 0)
+
+    def to_other_core(way, q):
+        remote(part.at[q * 2 + 1 - c], rc.at[way, q], csend.at[way, q], crecv.at[way, q], me.near("c")).start()
+
+    def reduce(way, between):
+        def lead(j, carry):
+            zz = me.inward(j)
+            q = zz * 2 + 1 - y
+            s = q * 2 + c
+            arrived(rc.at[way, q], crecv.at[way, q], me)
+            part[s] = (part[s].astype(F32) + rc[way, q].astype(F32)).astype(BF)
+            remote(part.at[s], ry.at[way, zz], ysend.at[way, j], yrecv.at[way, zz], me.near("y")).start()
+            return carry
+
+        lax.fori_loop(0, 4, lead, 0)
+
+        def turn(j, carry):
+            between(j)
+            zz = me.inward(j)
+            q = zz * 2 + y
+            s = q * 2 + c
+            arrived(rc.at[way, q], crecv.at[way, q], me)
+            arrived(ry.at[way, zz], yrecv.at[way, zz], me)
+            acc[...] = part[s].astype(F32) + rc[way, q].astype(F32) + ry[way, zz].astype(F32)
+            along_z(me, j, zz, acc, part.at[s], rz.at[way], zsend.at[way], 0, zrecv.at[way])
+            return carry
+
+        lax.fori_loop(0, 4, turn, 0)
+
+        def close(j, carry):
+            zz = me.inward(j)
+            whole = part.at[b]
+            left(whole, ysend.at[way, j], me)
+            left(whole, csend.at[way, j], me)
+            left(whole, csend.at[way, j + 4], me)
+            pl.when(zz > z)(lambda: left(whole, zsend.at[way, j, 0], me))
+            pl.when(zz < z)(lambda: left(whole, zsend.at[way, j, 1], me))
+            return carry
+
+        lax.fori_loop(0, 4, close, 0)
+
+    def gelu_parts(g):
+        t = jnp.tanh(GELU_A * (g + GELU_B * g * g * g))
+        return t, 0.5 * g * (1.0 + t)
+
+    def forward(q):
+        rows = nall[pl.ds(q * 2, 2)].reshape(256, 1536)
+        pair = jnp.dot(rows, win[...], preferred_element_type=F32)
+        pairs[q] = pair
+        unused, a = gelu_parts(pair[:, :384])
+        zq = (a * pair[:, 384:] * gate[q]).astype(BF)
+        zg[q] = zq
+        out = jnp.dot(zq, wout[...], preferred_element_type=F32)
+        part[pl.ds(q * 2, 2)] = out.astype(BF).reshape(2, 128, 1536)
+        to_other_core(0, q)
+
+    def backward(q):
+        rows = dyall[pl.ds(q * 2, 2)].reshape(256, 1536)
+        dz = lax.dot_general(rows, wout[...], NT, preferred_element_type=F32) * gate[q]
+        g, u = pairs[q, :, :384], pairs[q, :, 384:]
+        t, a = gelu_parts(g)
+        slope = 0.5 * (1.0 + t) + 0.5 * g * (1.0 - t * t) * (GELU_A * (1.0 + 3.0 * GELU_B * g * g))
+        dpairs[q, :, :384] = (dz * u * slope).astype(BF)
+        dpairs[q, :, 384:] = (dz * a).astype(BF)
+        out = lax.dot_general(dpairs[q], win[...], NT, preferred_element_type=F32)
+        part[pl.ds(q * 2, 2)] = out.astype(BF).reshape(2, 128, 1536)
+        to_other_core(1, q)
+
+    nall[b] = n2[...]
+    gather(nall, 0, forward)
+    reduce(0, lambda j: None)
+
+    done = h[...] + acc[...]
+    final[...] = done.astype(BF)
+    diff = done - teacher[...].astype(F32)
+    scaled = weight[:, 0:1] * diff
+    dy_out[...] = scaled
+    dyall[b] = scaled.astype(BF)
+    kept = jnp.sum(weight[:, 1:2] * diff * diff)
+    me_index = x * 16 + b
+    errs[me_index] = jnp.zeros((8, 128), F32) + kept
+
+    def tell(k, carry):
+        to = ((x + k // 16) % 2, (b + k) % 16)
+        remote(errs.at[me_index], errs.at[me_index], esend.at[k], erecv.at[me_index], to).start()
+        return carry
+
+    lax.fori_loop(1, 32, tell, 0)
+    gather(dyall, 1, backward)
+
+    def weight_part(j):
+        for i in range(2):
+
+            @pl.when(j * 2 + i < 6)
+            def _():
+                col = pl.ds(pl.multiple_of((j * 2 + i) * 256, 256), 256)
+                rows = nall[:, :, col].reshape(2048, 256)
+                both = dpairs[...].reshape(2048, 768)
+                dwin[col, :] = lax.dot_general(rows, both, TN, preferred_element_type=F32).astype(BF)
+                right = dyall[:, :, col].reshape(2048, 256)
+                zall = zg[...].reshape(2048, 384)
+                dwout[:, col] = lax.dot_general(zall, right, TN, preferred_element_type=F32).astype(BF)
+
+    reduce(1, weight_part)
+    dn2[...] = acc[...]
+
+    def hear(k, carry):
+        left(errs.at[0], esend.at[k], me)
+        s = ((x + k // 16) % 2) * 16 + (b + k) % 16
+        arrived(errs.at[s], erecv.at[s], me)
+        return carry
+
+    lax.fori_loop(1, 32, hear, 0)
+    total = errs[0]
+    for s in range(1, 32):
+        total = total + errs[s]
+    err[...] = total
+
+
+def run_experts(n2, h, teacher, weight, gate, win, wout):
+    wide = (128, 1536)
+    shard = (16,) + wide
+    return pl.pallas_call(
+        experts_kernel,
+        out_shape=(
+            jax.ShapeDtypeStruct(wide, BF),
+            jax.ShapeDtypeStruct((8, 128), F32),
+            jax.ShapeDtypeStruct(wide, F32),
+            jax.ShapeDtypeStruct(wide, F32),
+            jax.ShapeDtypeStruct((1536, 768), BF),
+            jax.ShapeDtypeStruct((384, 1536), BF),
+        ),
+        in_specs=[VMEM] * 7,
+        out_specs=(VMEM,) * 6,
+        scratch_shapes=[
+            pltpu.VMEM(shard, BF),
+            pltpu.VMEM(shard, BF),
+            pltpu.VMEM((8, 256, 768), F32),
+            pltpu.VMEM((8, 256, 384), BF),
+            pltpu.VMEM((8, 256, 768), BF),
+            pltpu.VMEM(shard, BF),
+            pltpu.VMEM((2, 8) + wide, BF),
+            pltpu.VMEM((2, 4) + wide, BF),
+            pltpu.VMEM((2, 5) + wide, BF),
+            pltpu.VMEM(wide, F32),
+            pltpu.VMEM((32, 8, 128), F32),
+            DMA((2, 4, 5)),
+            DMA((2, 16)),
+            DMA((2, 8)),
+            DMA((2, 8)),
+            DMA((2, 4)),
+            DMA((2, 4)),
+            DMA((2, 4, 2)),
+            DMA((2, 5)),
+            DMA((32,)),
+            DMA((32,)),
+        ],
+        compiler_params=params(2, 61),
+        name="experts",
+    )(n2, h, teacher, weight, gate, win, wout)
+
+
+def norm_back(values, gain, grad):
+    scale = lax.rsqrt(jnp.mean(values * values, axis=-1, keepdims=True) + 1e-06)
+    inner = grad * gain
+    mean = jnp.mean(inner * values, axis=-1, keepdims=True)
+    return scale * inner - values * (scale * scale * scale * mean), jnp.sum(
+        grad * values * scale, axis=0, keepdims=True
+    )
+
+
+def back_kernel(
+    states, h, n1, qs, o, lse, dn2, dy, cosine, sine, bounds, dwin, dwout, gq, go, kv_in,
+    gx, gqkv, gout, gup, gdown,
+    wq, wo, kv, pk, dos, delta, dh, dq, dkv, dqkv, xin, xout, *rest,
+):
+    sums = [(rest[i * 10 : i * 10 + 5], rest[i * 10 + 5 : i * 10 + 10]) for i in range(3)]
+    own_sem, xsend, xrecv, asend, arecv, osend, orecv = rest[30:]
+    me = Place()
+    x, y, z, b, c = me.x, me.y, me.z, me.b, me.c
+    loads = [
+        pltpu.make_async_copy(go, wo, own_sem.at[0]),
+        pltpu.make_async_copy(kv_in, kv, own_sem.at[1]),
+        pltpu.make_async_copy(gq, wq, own_sem.at[2]),
+    ]
+    for load in loads:
+        load.start()
+    greet_all(me)
+
+    def over(k, carry):
+        t = (b + k) % 16
+        remote(dwin.at[1 - x, t], xin.at[t], xsend.at[k], xrecv.at[t], me.near("x")).start()
+        pl.when(c != x)(
+            lambda: remote(dwout.at[t], xout.at[t], osend.at[k], orecv.at[t], me.near("x")).start()
+        )
+        return carry
+
+    lax.fori_loop(0, 16, over, 0)
+
+    def own_piece(n, t):
+        col = pl.multiple_of(n * 768 + c * 384, 128)
+        return (
+            xin.at[t, :, pl.ds(n * 384, 384)],
+            gup.at[b // 2, :, pl.ds(col, 384)],
+        )
+
+    def deal(k, carry):
+        t = (b + k) % 16
+        arrived(xin.at[t], xrecv.at[t], me)
+        xin[t] = (xin[t].astype(F32) + dwin[x, t].astype(F32)).astype(BF)
+
+        @pl.when(k > 0)
+        def _():
+            for n in range(2):
+                src, dst = own_piece(n, t)
+                remote(src, dst, asend.at[k, n], arecv.at[b, n], (x, t)).start()
+
+        @pl.when(k == 0)
+        def _():
+            for n in range(2):
+                src, dst = own_piece(n, t)
+                pltpu.make_async_copy(src, dst, own_sem.at[3 + n]).start()
+
+        @pl.when(c == x)
+        def _():
+            arrived(xout.at[t], orecv.at[t], me)
+            xout[t] = (xout[t].astype(F32) + dwout[t].astype(F32)).astype(BF)
+            pl.when(k > 0)(
+                lambda: remote(
+                    xout.at[t], gdown.at[b // 2], osend.at[16 + k], orecv.at[16 + b // 2], (x, t)
+                ).start()
+            )
+            pl.when(k == 0)(
+                lambda: pltpu.make_async_copy(xout.at[t], gdown.at[b // 2], own_sem.at[5]).start()
+            )
+
+        return carry
+
+    loads[2].wait()
+    gains = wq[:, :, pl.ds(2048, 128)].reshape(1536, 128).astype(F32).T
+    res_grad, gain_two = norm_back(h[...], gains[1:2], dn2[...])
+    dh[...] = dy[...] + res_grad
+    da = dh[...].astype(BF)
+    loads[0].wait()
+    do = lax.dot_general(
+        da, wo[...].reshape(1536, 1536), NT, preferred_element_type=F32
+    ).astype(BF)
+    low = o[...].astype(BF)
+    for i in range(4):
+        part = lax.dot_general(low[:, i * 384 : i * 384 + 384], da, TN, preferred_element_type=F32)
+        wo[i * 8 : i * 8 + 8] = part.astype(BF).reshape(8, 48, 1536)
+    out_sum = Sum(me, wo, by_weight, gout, *sums[0])
+    key_sum = Sum(me, pk, by_token, dkv, *sums[1], causal=True)
+
+    def lead_all(which):
+        def one(j, carry):
+            which.lead(j)
+            return carry
+
+        lax.fori_loop(0, 4, one, 0)
+
+    lead_all(out_sum)
+    for i in range(QUERY_HEADS):
+        col, r = i * 128, (i % GROUP) * 128
+        dos[i // GROUP, r : r + 128] = do[:, col : col + 128]
+        prod = do[:, col : col + 128].astype(F32) * o[:, col : col + 128]
+        delta[i // GROUP, :, r : r + 128] = jnp.sum(prod.T, axis=0, keepdims=True)
+    dq[...] = jnp.zeros_like(dq)
+    loads[1].wait()
+
+    def block(n):
+        ok = allowed_keys(n * 256, bounds)
+        for i in range(2):
+            k = kv[pl.ds(n * 2, 2), :, i * 128 : i * 128 + 128].reshape(256, 128)
+            v = kv[pl.ds(n * 2, 2), :, 256 + i * 128 : 384 + i * 128].reshape(256, 128)
+            s = lax.dot_general(k, qs[i], NT, preferred_element_type=F32)
+            p = jnp.where(ok, jnp.exp2(s * POWER - lse[i]), 0.0)
+            dp = lax.dot_general(v, dos[i], NT, preferred_element_type=F32)
+            ds = (p * (dp - delta[i])).astype(BF)
+            dv = jnp.dot(p.astype(BF), dos[i], preferred_element_type=F32)
+            dk = jnp.dot(ds, qs[i], preferred_element_type=F32) * SCALE
+            pk[pl.ds(n * 2, 2), :, i * 128 : i * 128 + 128] = dk.astype(BF).reshape(2, 128, 128)
+            pk[pl.ds(n * 2, 2), :, 256 + i * 128 : 384 + i * 128] = dv.astype(BF).reshape(2, 128, 128)
+            dq[i] += lax.dot_general(k, ds, TN, preferred_element_type=F32)
+
+    def turn(j, carry):
+        out_sum.turn(j)
+
+        @pl.when((j >= 2) & (j < 4))
+        def _():
+            lax.fori_loop((j - 2) * 8, (j - 2) * 8 + 8, deal, 0)
+
+        @pl.when(key_sum.valid(j))
+        def _():
+            last = jnp.where(j == z, y * 2 + c, 3)
+
+            def one(n, carry):
+                block(j * 4 + n)
+                return carry
+
+            lax.fori_loop(0, last + 1, one, 0)
+
+            def blank(n, carry):
+                pk[pl.ds((j * 4 + n) * 2, 2)] = jnp.zeros((2, 128, 512), BF)
+                return carry
+
+            lax.fori_loop(last + 1, 4, blank, 0)
+            key_sum.lead(j)
+
+        key_sum.turn(j)
+        return carry
+
+    lax.fori_loop(0, 6, turn, 0)
+
+    cos, sin = cosine[...], -sine[...]
+    for i in range(QUERY_HEADS):
+        r = (i % GROUP) * 128
+        head = dq[i // GROUP, :, r : r + 128].T * SCALE
+        dqkv[:, i * 128 : i * 128 + 128] = turned(head, cos, sin).astype(BF)
+    for i in range(2):
+        dqkv[:, 1536 + i * 128 : 1664 + i * 128] = turned(dkv[:, i * 128 : i * 128 + 128], cos, sin).astype(BF)
+        dqkv[:, 1792 + i * 128 : 1920 + i * 128] = dkv[:, 256 + i * 128 : 384 + i * 128].astype(BF)
+    dn1 = lax.dot_general(
+        dqkv[...], wq[:, :, pl.ds(0, 2048)].reshape(1536, 2048), NT, preferred_element_type=F32
+    )
+    in_grad, gain_one = norm_back(states[...].astype(F32), gains[0:1], dn1)
+    gx[...] = dh[...] + in_grad
+    rows = lax.broadcasted_iota(jnp.int32, (128, 1536), 0)
+    tail = jnp.where(rows == 0, gain_one, jnp.where(rows == 1, gain_two, 0.0)).T
+    wq[:, :, pl.ds(2048, 128)] = tail.astype(BF).reshape(32, 48, 128)
+    for i in range(4):
+        part = lax.dot_general(
+            n1[:, i * 384 : i * 384 + 384], dqkv[...], TN, preferred_element_type=F32
+        )
+        wq[i * 8 : i * 8 + 8, :, 0:2048] = part.astype(BF).reshape(8, 48, 2048)
+    proj_sum = Sum(me, wq, by_weight, gqkv, *sums[2])
+    lead_all(proj_sum)
+
+    def last_turn(j, carry):
+        proj_sum.turn(j)
+        return carry
+
+    lax.fori_loop(0, 6, last_turn, 0)
+    out_sum.close()
+    key_sum.close()
+    proj_sum.close()
+
+    def close(k, carry):
+        left(xin.at[0], xsend.at[k], me)
+        pl.when(c != x)(lambda: left(xout.at[0], osend.at[k], me))
+
+        @pl.when(k > 0)
+        def _():
+            f = (b + 16 - k) % 16
+            for n in range(2):
+                left(xin.at[0, :, pl.ds(0, 384)], asend.at[k, n], me)
+                col = pl.multiple_of(n * 768 + (f % 2) * 384, 128)
+                arrived(gup.at[f // 2, :, pl.ds(col, 384)], arecv.at[f, n], me)
+            pl.when(c == x)(lambda: left(xout.at[0], osend.at[16 + k], me))
+            pl.when(f % 2 == x)(lambda: arrived(gdown.at[f // 2], orecv.at[16 + f // 2], me))
+
+        @pl.when(k == 0)
+        def _():
+            for n in range(2):
+                src, dst = own_piece(n, b)
+                pltpu.make_async_copy(src, dst, own_sem.at[3 + n]).wait()
+            pl.when(c == x)(
+                lambda: pltpu.make_async_copy(xout.at[b], gdown.at[b // 2], own_sem.at[5]).wait()
+            )
+
+        return carry
+
+    lax.fori_loop(0, 16, close, 0)
+
+
+def run_back(*operands):
+    shape = jax.ShapeDtypeStruct
+    return pl.pallas_call(
+        back_kernel,
+        out_shape=(
+            shape((128, 1536), F32),
+            shape((48, 2304), F32),
+            shape((48, 1536), F32),
+            shape((8, 48, 1536), BF),
+            shape((8, 48, 768), BF),
+        ),
+        in_specs=[VMEM] * 13 + [ANY] * 3,
+        out_specs=(VMEM,) * 3 + (ANY,) * 2,
+        scratch_shapes=[
+            pltpu.VMEM((32, 48, 2304), BF),
+            pltpu.VMEM((32, 48, 1536), BF),
+            pltpu.VMEM((32, 128, 512), BF),
+            pltpu.VMEM((32, 128, 512), BF),
+            pltpu.VMEM((2, LANES, 128), BF),
+            pltpu.VMEM((2, 1, LANES), F32),
+            pltpu.VMEM((128, 1536), F32),
+            pltpu.VMEM((2, 128, LANES), F32),
+            pltpu.VMEM((128, 512), F32),
+            pltpu.VMEM((128, 2048), BF),
+            pltpu.VMEM((16, 48, 768), BF),
+            pltpu.VMEM((16, 48, 768), BF),
+        ]
+        + Sum.room(48, 1536)
+        + Sum.room(128, 512)
+        + Sum.room(48, 2304)
+        + [DMA((6,)), DMA((16,)), DMA((16,)), DMA((16, 2)), DMA((16, 2)), DMA((32,)), DMA((32,))],
+        compiler_params=params(3, 61),
+        name="back",
+    )(*operands)
+
+
+def per_device(
+    states, teacher, valid, routes, gates, doc_starts, norm_one,
+    w_query, key_weight, value_weight, w_output, norm_two, expert_in, expert_out,
+):
+    tokens = states.shape[2]
+    width = states.shape[3]
+    b, x = lax.axis_index("blk"), lax.axis_index("head")
+    span = tokens * lax.axis_size("head") * lax.axis_size("blk")
+    place = (b * 2 + x) * tokens + jnp.arange(tokens, dtype=jnp.int32)
+    unused_segment, position = doc_layout(place, doc_starts)
+    half = HEAD_SIZE // 2
+    freq = ROTARY_BASE ** (-jnp.arange(half).astype(jnp.float32) / half)
+    angle = position.astype(jnp.float32)[:, None] * freq[None, :]
+    cosine, sine = jnp.cos(angle), jnp.sin(angle)
+    cosine = jnp.concatenate([cosine, cosine], axis=1)
+    sine = jnp.concatenate([-sine, sine], axis=1)
+    bounds = jnp.tile(jnp.stack([place - position, place]), (1, GROUP))
+    keep_mask = valid.reshape(tokens).astype(F32)
+    route_rows = routes.reshape(tokens, TOP)
+    gate_rows = gates.reshape(tokens, TOP)
+
+    table = jnp.sum(
+        jnp.where(route_rows[None] == jnp.arange(E, dtype=jnp.int32)[:, None, None], gate_rows[None], 0.0), axis=-1
+    )
+    high = lax.reduce_precision(table, 8, 7)
+    column = jnp.arange(128)[None, :]
+    gains = jnp.where(
+        column == 0,
+        norm_one[:, None].astype(F32),
+        jnp.where(column == 1, norm_two[:, None].astype(F32), jnp.sum(keep_mask)),
+    )
+    routed = jnp.concatenate([high, table - high, jnp.zeros((32, 128), F32)], axis=0)
+    extra = jnp.concatenate([gains, routed], axis=1).astype(BF)
+    rows = states.reshape(tokens, width)
+    gq, go, kv, win, wout, h, n2, n1, qs, o, lse = run_front(
+        rows, w_query, key_weight, value_weight, w_output, extra, expert_in,
+        expert_out.reshape(E, 48, 768), cosine, sine, bounds,
+    )
+    count_all = jnp.sum(gq[:, 0, 2050].astype(F32))
+    tables = lax.dynamic_slice_in_dim(gq[:, :16, 2176:], x * 16, 16, 0).astype(F32)
+    mine = lax.dynamic_slice_in_dim(tables, b // 2, 1, 1) + lax.dynamic_slice_in_dim(tables, 8 + b // 2, 1, 1)
+    weight = jnp.stack([keep_mask * (span * 1.0 / count_all), keep_mask], axis=1)
+    final, error, dn2, dy, dwin, dwout = run_experts(
+        n2, h, teacher.reshape(tokens, width), weight, mine.reshape(8, 256, 1),
+        win.reshape(1536, 768), wout.reshape(384, 1536),
+    )
+    gx, gqkv, gout, gup, gdown = run_back(
+        rows, h, n1, qs, o, lse, dn2, dy, cosine, sine, bounds,
+        dwin.reshape(2, 16, 48, 768), dwout.reshape(16, 48, 768), gq, go, kv,
+    )
+    shape = states.shape
+    return (
+        final.reshape(shape),
+        error[0, 0] / (width * count_all),
+        gx.reshape(shape),
+        gqkv[:, 2048],
+        gqkv[:, :1536],
+        gqkv[:, 1536:1792],
+        gqkv[:, 1792:2048],
+        gout,
+        gqkv[:, 2049],
+        gup.astype(F32),
+        gdown.astype(F32).reshape(E, 24, 1536),
+    )
+
+
 def solution(mesh):
     in_specs = (
         P("blk", "head", None, None),
@@ -419,6 +1549,8 @@
         P(None, ("head", "blk"), None),
         P(None, ("head", "blk"), None),
     )
+    sizes = dict(mesh.shape)
+    plan = per_device if sizes == {"head": 2, "blk": 4 * NZ} else per_device_plain
     return jax.shard_map(
-        per_device, mesh=mesh, in_specs=in_specs, out_specs=out_specs, check_vma=False
-    )
+        plan, mesh=mesh, in_specs=in_specs, out_specs=out_specs, check_vma=False
+    )

time: 2460 us -> 558 us (0.23)
  waiting for transfers between devices: 1960 us -> 0 us
  Pallas kernels: 0 us -> 509 us
  blocking collectives: 239 us -> 0 us
  matrix products: 164 us -> 0 us
    reduce_scatter x8 -> x0, waiting for transfers between devices: 1610 us -> none  [the longest x1 667 us: per_device(): lax.psum_scatter(grad_up, ('head', 'blk'), scatter_dimension=1, tiled=True)]
    pallas_call x0 -> x3, Pallas kernels: none -> 509 us  [the longest x1 197 us: run_experts(): pl.pallas_call(experts_kernel, out_shape=(jax.ShapeDtypeStruct(wide, BF),...]
    all_gather x6 -> x0, waiting for transfers between devices: 322 us -> none  [the longest x1 212 us: per_device(): lax.all_gather(expert_in, ('head', 'blk'), axis=1, tiled=True)]
    dot_general x31 -> x0, matrix products: 164 us -> none  [the longest x1 30.2 us: per_device(): jnp.einsum('ecd,ecf->edf', expert_rows, grad_pair, preferred_element_type...]
    all_gather x2 -> x0, blocking collectives: 87.8 us -> none  [the longest x1 46.5 us: per_device(): lax.all_gather(key_weight, ('head', 'blk'), axis=0, tiled=True)]
    psum x2 -> x0, blocking collectives: 76.6 us -> none  [per_device(): count_all, error_all = lax.psum((local_count, local_error), ('head', 'blk'))]
    unnamed x1 -> x0, blocking collectives: 37.9 us -> none
    all_to_all x5 -> x0, blocking collectives: 36.7 us -> none  [the longest x1 8.28 us: per_device(): lax.all_to_all(grad_query_lin, 'head', split_axis=0, concat_axis=1, tiled...]
  transfers between devices with their start and end apart: 17 -> 0, of which waited for: 13 -> 0; matrix products, arithmetic and copies ran while one was open for 5% -> 0% of each run, Pallas kernels for 0% -> 0%
where the time goes in v2:
time: 558 us; the launch traced here: 550 us
  Pallas kernels  509 us (91%)
  local copies, waits for them, and re-layouts  28.5 us (5%)
  other arithmetic  8.58 us (2%)
    pallas_call x1, Pallas kernels, run_experts(): pl.pallas_call(experts_kernel, out_shape=(jax.ShapeDtypeStruct(wide, BF),...  197 us
    pallas_call x1, Pallas kernels, run_back(): pl.pallas_call(back_kernel, out_shape=(shape((128, 1536), F32), shape((48...  161 us
    pallas_call x1, Pallas kernels, run_front(): pl.pallas_call(front_kernel, out_shape=(shape((32, 48, 2304), BF), shape(...  152 us
    unnamed x43, local copies, waits for them, and re-layouts  11.3 us

profile of v2, /device:TPU:0, one launch (start us, length us, event | category | flops | bytes accessed | tf_op | source)
XLA Modules:
  0.0 550.3 jit_solution(12855261946523251805)
XLA Ops:
  0.7 1.3 convert_reduce_fusion.1
  4.2 1.4 select_convert_fusion
  6.1 1.3 reshape.125.down
  7.4 1.0 copy-done.1
  8.4 0.9 copy-done.8
  9.3 0.9 copy-done.9
  11.7 151.9 %front.1 = (bf16[32,48,2304]{2,1,0:T(8,128)(2,1)}, bf16[32,48,1536]{2,1,0:T(8,128)(2,1)}, bf16[32,128,512]{2,1,0:T(8,128)(2,1)}, bf16[2,16,48,768]{3,2,1,0:T(8,1...) custom-call(bf16[128,1536]{1,0:T(8,128)(2,1)S(1)} %bitcast.20, ...), custom_call_target="tpu_custom_call" | custom-call | tf_op jit(solution)/shard_map/front/pallas_call | solution.py:938
  163.6 0.9 copy-done
  164.5 0.9 copy-done.2
  166.9 0.8 copy-done.7
  168.3 1.5 convert_reduce_fusion
  171.9 0.9 slice.25
  173.0 1.8 reshape.138.gate
  174.8 1.2 reshape.129.wout
  176.0 196.8 %experts.1 = (bf16[128,1536]{1,0:T(8,128)(2,1)}, f32[8,128]{1,0:T(8,128)}, f32[128,1536]{1,0:T(8,128)}, f32[128,1536]{1,0:T(8,128)}, bf16[1536,768]{1,0:T(8,128)(2,1)}, /*index=5*/bf16[384,1536]{1,0:T(8,128)(2,1)}) custom-call(bf16[128,1536]{1,0:T(8,128)(2,1)} %copy-done.5, f32[128,1536]{1,0:T(8,128)} %copy-done, bf16[128,1536]{1,0:T(8,128)(2,1)} %bitcast.26, ...), custom_call_target="tpu_custom_call" | custom-call | tf_op jit(solution)/shard_map/experts/pallas_call | solution.py:1167
  372.8 1.2 slice.26
  374.6 2.9 reshape.132.dwout
  377.6 160.6 %back.1 = (f32[128,1536]{1,0:T(8,128)}, f32[48,2304]{1,0:T(8,128)}, f32[48,1536]{1,0:T(8,128)}, bf16[8,48,1536]{2,1,0:T(8,128)(2,1)}, bf16[8,48,768]{2,1,0:T(8,128)(2,1)}) custom-call(bf16[128,1536]{1,0:T(8,128)(2,1)} %bitcast.19, f32[128,1536]{1,0:T(8,128)} %copy-done, bf16[128,1536]{1,0:T(8,128)(2,1)} %copy-done.6, bf16[2,768,128]{2,1,0:T(8,128)(2,1)} %copy-done.7, ...), custom_call_target="tpu_custom_call" | custom-call | tf_op jit(solution)/shard_map/back/pallas_call | solution.py:1422
  538.2 1.6 slice_reduce_fusion
  539.7 1.5 fusion.2
  541.2 1.7 slice.28
  542.9 2.2 reshape.137
  545.1 1.7 convert_element_type.64
  547.6 0.9 copy.47
  (55 shorter events, 8.5 us)
Async XLA Ops:
  0.6 170.5 %copy-start.18 = (s32[1,1,128]{2,1,0:T(1,128)S(1)}, s32[1,1,128]{2,1,0:T(1,128)}, u32[]{:S(2)}) copy-start(s32[1,1,128]{2,1,0:T(1,128)} %param.16) | copy-start | bytes 1540
  4.2 168.7 %copy-start.10 = (s32[1,2,6,128]{3,1,2,0:T(2,128)}, s32[1,2,6,128]{3,1,2,0:T(2,128)S(1)}, u32[]{:S(2)}) copy-start(s32[1,2,6,128]{3,1,2,0:T(2,128)S(1)} %copy.42) | copy-start | bytes 18436
  6.0 168.8 %copy-start.3 = (f32[128,128]{1,0:T(8,128)}, f32[128,128]{1,0:T(8,128)S(1)}, u32[]{:S(2)}) copy-start(f32[128,128]{1,0:T(8,128)S(1)} %get-tuple-element.66.cosine) | copy-start | bytes 196612
  6.0 168.8 %copy-start.4 = (f32[128,128]{1,0:T(8,128)}, f32[128,128]{1,0:T(8,128)S(1)}, u32[]{:S(2)}) copy-start(f32[128,128]{1,0:T(8,128)S(1)} %get-tuple-element.67.sine) | copy-start | bytes 196612
  7.4 1.0 copy-start.1
  8.4 0.9 copy-start.8
  9.3 0.9 copy-start.9
  10.2 0.7 copy-start.11
  11.0 0.7 copy-start.12
  163.6 0.9 copy-start
  164.5 0.9 copy-start.2
  165.4 0.7 copy-start.5
  166.1 0.8 copy-start.6
  166.9 0.8 copy-start.7
  167.7 0.6 copy-start.13
  538.2 7.0 %copy-start.14 = (bf16[8,48,1536]{2,1,0:T(8,128)(2,1)S(1)}, bf16[8,48,1536]{2,1,0:T(8,128)(2,1)}, u32[]{:S(2)}) copy-start(bf16[8,48,1536]{2,1,0:T(8,128)(2,1)} %get-tuple-element.53) | copy-start | bytes 3538948
  542.9 4.0 copy-start.16
  545.1 2.5 copy-start.15
  545.1 3.3 copy-start.17

commit v3 on v2

--- a/solution.py
+++ b/solution.py
@@ -2,6 +2,7 @@
 
 import jax
 import jax.numpy as jnp
+import numpy as np
 from jax import lax
 from jax.experimental import pallas as pl
 from jax.experimental.pallas import tpu as pltpu
@@ -19,6 +20,7 @@
 
 MESH = pl.DeviceIdType.MESH
 NZ = 4
+SPAN = 32 * 128.0
 BF = jnp.bfloat16
 F32 = jnp.float32
 
@@ -460,10 +462,12 @@
 
 
 class Gather:
-    def __init__(self, me, g, index, send, recv, causal=False):
+    def __init__(self, me, g, index, send, recv, cols=None, causal=False):
         self.me, self.g, self.index, self.send, self.recv, self.causal = me, g, index, send, recv, causal
-        half = g.shape[2] // 2
-        self.first, self.second = pl.ds(0, half), pl.ds(half, half)
+        start, width = cols or (0, g.shape[2])
+        cut = (width // 2 + 127) // 128 * 128
+        self.cols = pl.ds(start, width)
+        self.first, self.second = pl.ds(start, cut), pl.ds(start + cut, width - cut)
 
     def place(self, j):
         return self.me.z - j if self.causal else self.me.outward(j)
@@ -480,11 +484,11 @@
         return (zz >= self.me.z) & (self.me.z > 0)
 
     def put(self, j, kind, n, s, cols=None, slot=0):
-        ref = self.g.at[s] if cols is None else self.g.at[s, :, cols]
+        ref = self.g.at[s, :, self.cols if cols is None else cols]
         remote(ref, ref, self.send.at[j, n], self.recv.at[s, slot], self.me.near(kind)).start()
 
     def wait(self, s):
-        arrived(self.g.at[s], self.recv.at[s, 0], self.me)
+        arrived(self.g.at[s, :, self.cols], self.recv.at[s, 0], self.me)
 
     def turn(self, j):
         me, index = self.me, self.index
@@ -540,14 +544,15 @@
             def _():
                 zz = self.place(j)
                 own = self.index(me.x, zz, me.y, me.c)
-                whole, part = self.g.at[own], self.g.at[own, :, self.first]
+                whole = self.g.at[own, :, self.cols]
+                first, second = self.g.at[own, :, self.first], self.g.at[own, :, self.second]
                 pl.when(self.ups(zz))(lambda: left(whole, self.send.at[j, 0], me))
                 if not self.causal:
                     pl.when(self.downs(zz))(lambda: left(whole, self.send.at[j, 1], me))
                 for n in (2, 3, 6, 7, 8, 9):
                     left(whole, self.send.at[j, n], me)
-                for n in (4, 5):
-                    left(part, self.send.at[j, n], me)
+                left(first, self.send.at[j, 4], me)
+                left(second, self.send.at[j, 5], me)
                 if cores:
                     self.from_core(j)
 
@@ -555,30 +560,24 @@
 
         lax.fori_loop(0, 4, one, 0)
 
-    def run(self, between=None):
-        def one(j, carry):
-            self.turn(j)
-            if between is not None:
-                between(j)
-            return carry
-
-        lax.fori_loop(0, 6, one, 0)
-        self.close()
-
 
 class Sum:
-    def __init__(self, me, part, index, out, room, sems, causal=False):
+    def __init__(self, me, part, index, out, room, sems, cols=None, causal=False):
         self.me, self.part, self.index, self.out, self.causal = me, part, index, out, causal
-        self.rc, self.rd, self.rn, self.rz, self.acc = room
+        start, width = cols or (0, part.shape[2])
+        self.cols = pl.ds(start, width)
+        self.rc, self.rx, self.ry, self.rn, self.rz, self.acc = room
         self.sc, self.ss, self.vc, self.vn, self.vz = sems
-        self.half = part.shape[2] // 2
-        self.first, self.second = pl.ds(0, self.half), pl.ds(self.half, self.half)
+        self.half = (width // 2 + 127) // 128 * 128
+        self.first, self.second = pl.ds(0, self.half), pl.ds(self.half, width - self.half)
 
     @staticmethod
     def room(rows, columns):
+        half = (columns // 2 + 127) // 128 * 128
         return [
             pltpu.VMEM((16, rows, columns), BF),
-            pltpu.VMEM((2, 4, rows, columns // 2), BF),
+            pltpu.VMEM((4, rows, half), BF),
+            pltpu.VMEM((4, rows, columns - half), BF),
             pltpu.VMEM((2, 4, rows, columns), BF),
             pltpu.VMEM((5, rows, columns), BF),
             pltpu.VMEM((rows, columns), F32),
@@ -604,17 +603,18 @@
         for xx in (1 - me.x, me.x):
             for yy in (1 - me.y, me.y):
                 k = self.slot(xx, zz, yy)
-                src = self.part.at[self.index(xx, zz, yy, 1 - me.c)]
+                src = self.part.at[self.index(xx, zz, yy, 1 - me.c), :, self.cols]
                 remote(src, self.rc.at[k], self.sc.at[k], self.vc.at[k], me.near("c")).start()
 
     def with_core(self, xx, zz, yy):
         k = self.slot(xx, zz, yy)
         arrived(self.rc.at[k], self.vc.at[k], self.me)
-        return k, self.part[self.index(xx, zz, yy, self.me.c)].astype(F32) + self.rc[k].astype(F32)
+        own = self.part[self.index(xx, zz, yy, self.me.c), :, self.cols]
+        return k, own.astype(F32) + self.rc[k].astype(F32)
 
     def turn(self, j):
         me, half, first, second = self.me, self.half, self.first, self.second
-        rc, rd, rn, ss, vn = self.rc, self.rd, self.rn, self.ss, self.vn
+        rc, rx, ry, rn, ss, vn = self.rc, self.rx, self.ry, self.rn, self.ss, self.vn
         x, y = me.x, me.y
 
         @pl.when(self.valid(j))
@@ -622,22 +622,22 @@
             zz = self.place(j)
             k, total = self.with_core(1 - x, zz, 1 - y)
             rc[k] = total.astype(BF)
-            remote(rc.at[k, :, first], rd.at[0, zz], ss.at[j, 0], vn.at[zz, 0], me.near("x")).start()
-            remote(rc.at[k, :, second], rd.at[1, zz], ss.at[j, 1], vn.at[zz, 1], me.near("y")).start()
+            remote(rc.at[k, :, first], rx.at[zz], ss.at[j, 0], vn.at[zz, 0], me.near("x")).start()
+            remote(rc.at[k, :, second], ry.at[zz], ss.at[j, 1], vn.at[zz, 1], me.near("y")).start()
 
         @pl.when(self.valid(j - 1))
         def _():
             i = j - 1
             zz = self.place(i)
             k, total = self.with_core(x, zz, 1 - y)
-            arrived(rd.at[0, zz], vn.at[zz, 0], me)
+            arrived(rx.at[zz], vn.at[zz, 0], me)
             rc[k, :, second] = total[:, half:].astype(BF)
-            rc[k, :, first] = (total[:, :half] + rd[0, zz].astype(F32)).astype(BF)
+            rc[k, :, first] = (total[:, :half] + rx[zz].astype(F32)).astype(BF)
             remote(rc.at[k], rn.at[0, zz], ss.at[i, 2], vn.at[zz, 2], me.near("y")).start()
             k, total = self.with_core(1 - x, zz, y)
-            arrived(rd.at[1, zz], vn.at[zz, 1], me)
+            arrived(ry.at[zz], vn.at[zz, 1], me)
             rc[k, :, first] = total[:, :half].astype(BF)
-            rc[k, :, second] = (total[:, half:] + rd[1, zz].astype(F32)).astype(BF)
+            rc[k, :, second] = (total[:, half:] + ry[zz].astype(F32)).astype(BF)
             remote(rc.at[k], rn.at[1, zz], ss.at[i, 3], vn.at[zz, 3], me.near("x")).start()
 
         @pl.when(self.valid(j - 2))
@@ -652,11 +652,12 @@
 
             @pl.when(zz == me.z)
             def _():
-                self.out[...] = self.acc[...]
+                self.out[:, self.cols] = self.acc[...]
 
     def close(self):
         me = self.me
-        whole, piece = self.rc.at[0], self.rc.at[0, :, self.first]
+        whole = self.rc.at[0]
+        first, second = self.rc.at[0, :, self.first], self.rc.at[0, :, self.second]
 
         def one(j, carry):
             @pl.when(self.valid(j))
@@ -665,8 +666,8 @@
                 for xx in (1 - me.x, me.x):
                     for yy in (1 - me.y, me.y):
                         left(whole, self.sc.at[self.slot(xx, zz, yy)], me)
-                for n in (0, 1):
-                    left(piece, self.ss.at[j, n], me)
+                left(first, self.ss.at[j, 0], me)
+                left(second, self.ss.at[j, 1], me)
                 for n in (2, 3):
                     left(whole, self.ss.at[j, n], me)
                 if not self.causal:
@@ -676,22 +677,6 @@
             return carry
 
         lax.fori_loop(0, 4, one, 0)
-
-    def run(self, between=None):
-        def one(j, carry):
-            self.lead(j)
-            return carry
-
-        lax.fori_loop(0, 4, one, 0)
-
-        def two(j, carry):
-            self.turn(j)
-            if between is not None:
-                between(j)
-            return carry
-
-        lax.fori_loop(0, 6, two, 0)
-        self.close()
 
 
 def along_z(me, i, zz, acc, room, rz, ss, n, vz, causal=False):
@@ -751,16 +736,54 @@
     return u * cosine + pltpu.roll(u, 64, 1) * sine
 
 
+def begin_of(place, doc):
+    begin = jnp.zeros_like(place)
+    for i in range(doc.shape[0]):
+        begin = jnp.where(place >= doc[i], jnp.maximum(begin, doc[i]), begin)
+    return begin
+
+
+def rotary_tables(me, doc, freq):
+    first = (me.b * 2 + me.x) * 128
+    place = first + lax.broadcasted_iota(jnp.int32, (128, 128), 0)
+    angle = (place - begin_of(place, doc)).astype(F32) * freq[...]
+    sine = jnp.sin(angle)
+    lane = lax.broadcasted_iota(jnp.int32, (128, 128), 1)
+    return jnp.cos(angle), jnp.where(lane < 64, -sine, sine)
+
+
+def query_bounds(me, doc):
+    place = (me.b * 2 + me.x) * 128 + lax.broadcasted_iota(jnp.int32, (1, LANES), 1) % 128
+    return begin_of(place, doc), place
+
+
 def allowed_keys(start, bounds):
     key = start + lax.broadcasted_iota(jnp.int32, (256, LANES), 0)
-    return (key >= bounds[0:1, :]) & (key <= bounds[1:2, :])
+    return (key >= bounds[0]) & (key <= bounds[1])
+
+
+def eye(n):
+    return lax.broadcasted_iota(jnp.int32, (n, n), 0) == lax.broadcasted_iota(jnp.int32, (n, n), 1)
+
+
+def as_column(row):
+    return jnp.sum(jnp.where(eye(row.shape[1]), row, 0.0), axis=1, keepdims=True)
+
+
+def as_row(column):
+    return jnp.sum(jnp.where(eye(column.shape[0]), column, 0.0), axis=0, keepdims=True)
+
+
+QKV = 2048
+WIDE = QKV + 128
+PIECES = ((0, 1152), (1152, 1024))
 
 
 def front_kernel(
-    states, wq, wk, wv, wo, extra, up, down, cosine, sine, bounds,
-    gq_out, go_out, kv_out, win, wout, h, n2, n1, qs, o_out, lse,
-    gq, go, kv, top, total, acc,
-    own_sem, qsend, qrecv, gsend, grecv, ksend, krecv, asend, arecv, xsend, xrecv, osend, orecv,
+    states, doc, freq, norm_one, norm_two, valid, down_in, wq, wk, wv, wo, up,
+    gq_out, go_out, kv_out, win, wout, h, n2, n1, qs, o_out, lse, count,
+    gq, go, kv, down, top, total, acc,
+    own_sem, qsend, qrecv, gsend, grecv, ksend, krecv, asend, arecv, osend, orecv,
 ):
     me = Place()
     x, y, z, b, c = me.x, me.y, me.z, me.b, me.c
@@ -769,24 +792,34 @@
         pltpu.make_async_copy(wq, gq.at[here, :, pl.ds(0, 1536)], own_sem.at[0]),
         pltpu.make_async_copy(wk, gq.at[here, :, pl.ds(1536, 256)], own_sem.at[1]),
         pltpu.make_async_copy(wv, gq.at[here, :, pl.ds(1792, 256)], own_sem.at[2]),
-        pltpu.make_async_copy(extra, gq.at[here, :, pl.ds(2048, 256)], own_sem.at[3]),
-        pltpu.make_async_copy(wo, go.at[here], own_sem.at[4]),
+        pltpu.make_async_copy(wo, go.at[here], own_sem.at[3]),
     ]
-    for k in range(2):
-        col = pl.multiple_of(k * 768 + c * 384, 128)
-        mine.append(
-            pltpu.make_async_copy(
-                up.at[b // 2, :, pl.ds(col, 384)], win.at[x, b, :, pl.ds(k * 384, 384)], own_sem.at[5 + k]
-            )
-        )
-    held = pltpu.make_async_copy(down.at[b // 2], wout.at[b], own_sem.at[7])
     for copy in mine:
         copy.start()
-    pl.when(c == x)(held.start)
+
+    lane = lax.broadcasted_iota(jnp.int32, (48, 128), 1)
+    kept = jnp.sum(valid[...].astype(F32))
+    extra = jnp.where(
+        lane == 0,
+        as_column(norm_one[...].astype(F32)),
+        jnp.where(lane == 1, as_column(norm_two[...].astype(F32)), jnp.where(lane == 2, kept, 0.0)),
+    )
+    gq[here, :, pl.ds(QKV, 128)] = extra.astype(BF)
+    for e in range(E):
+        wide = down_in[e].astype(F32)
+        down[e] = jnp.concatenate([wide[:, :768], wide[:, 768:]], axis=0).astype(BF)
     greet_all(me)
     for copy in mine:
         copy.wait()
-    pl.when(c == x)(held.wait)
+
+    def own_piece(n):
+        col = pl.multiple_of(n * 768 + c * 384, 128)
+        return pltpu.make_async_copy(
+            up.at[b // 2, :, pl.ds(col, 384)], win.at[b, :, pl.ds(n * 384, 384)], own_sem.at[4 + n]
+        )
+
+    def own_down():
+        return pltpu.make_async_copy(down.at[b // 2], wout.at[b], own_sem.at[6])
 
     def deal(k, carry):
         t = (b + k) % 16
@@ -794,7 +827,7 @@
             col = pl.multiple_of(n * 768 + (t % 2) * 384, 128)
             remote(
                 up.at[t // 2, :, pl.ds(col, 384)],
-                win.at[x, b, :, pl.ds(n * 384, 384)],
+                win.at[b, :, pl.ds(n * 384, 384)],
                 asend.at[k, n],
                 arecv.at[b, n],
                 (x, t),
@@ -804,35 +837,34 @@
         )
         return carry
 
-    def pass_on(k, carry):
-        f = (b + 16 - k) % 16
-
-        @pl.when(k > 0)
-        def _():
-            for n in range(2):
-                arrived(win.at[x, f, :, pl.ds(n * 384, 384)], arecv.at[f, n], me)
-
-        remote(win.at[x, f], win.at[x, f], xsend.at[k], xrecv.at[f], me.near("x")).start()
-
-        @pl.when(c == x)
-        def _():
-            pl.when(k > 0)(lambda: arrived(wout.at[f], orecv.at[f], me))
-            remote(wout.at[f], wout.at[f], osend.at[16 + k], orecv.at[f], me.near("x")).start()
-
+    weights = [
+        Gather(me, gq, by_weight, qsend.at[i], qrecv.at[i], PIECES[i]) for i in range(len(PIECES))
+    ]
+
+    def first_turn(j, carry):
+        for piece in weights:
+            piece.turn(j)
+        lax.fori_loop(1 + j * 3, jnp.minimum(4 + j * 3, 16), deal, 0)
         return carry
 
-    Gather(me, gq, by_weight, qsend, qrecv).run()
-    lax.fori_loop(1, 16, deal, 0)
+    lax.fori_loop(0, 6, first_turn, 0)
+    for n in range(2):
+        own_piece(n).start()
+    pl.when(c == x)(lambda: own_down().start())
+    cos, sin = rotary_tables(me, doc, freq)
+    bounds = query_bounds(me, doc)
+    for piece in weights:
+        piece.close()
     keep = pltpu.make_async_copy(gq, gq_out, own_sem.at[0])
     keep.start()
 
     rows = states[...].astype(F32)
-    gains = gq[:, :, pl.ds(2048, 128)].reshape(1536, 128).astype(F32).T
+    gains = gq[:, :, pl.ds(QKV, 128)].reshape(1536, 128).astype(F32).T
+    count[...] = jnp.zeros((8, 128), F32) + jnp.sum(gains[2:3]) / 48.0
     n1[...] = (
         rows * lax.rsqrt(jnp.mean(rows * rows, axis=-1, keepdims=True) + 1e-06) * gains[0:1]
     ).astype(BF)
-    qkv = jnp.dot(n1[...], gq[:, :, pl.ds(0, 2048)].reshape(1536, 2048), preferred_element_type=F32)
-    cos, sin = cosine[...], sine[...]
+    qkv = jnp.dot(n1[...], gq[:, :, pl.ds(0, QKV)].reshape(1536, QKV), preferred_element_type=F32)
     at = by_token(x, z, y, c)
     for i in range(2):
         kv[at, :, i * 128 : i * 128 + 128] = turned(qkv[:, 1536 + i * 128 : 1664 + i * 128], cos, sin).astype(BF)
@@ -866,14 +898,6 @@
         keys.turn(j)
         output.turn(j - 2)
 
-        @pl.when(j == 4)
-        def _():
-            lax.fori_loop(0, 4, pass_on, 0)
-
-        @pl.when(j == 5)
-        def _():
-            lax.fori_loop(4, 8, pass_on, 0)
-
         @pl.when(keys.valid(j - 2))
         def _():
             i = j - 2
@@ -890,7 +914,6 @@
         return carry
 
     lax.fori_loop(0, 8, turn, 0)
-    lax.fori_loop(8, 16, pass_on, 0)
     output.close()
     keep_o = pltpu.make_async_copy(go, go_out, own_sem.at[1])
     keep_o.start()
@@ -913,35 +936,34 @@
     keys.close(False)
 
     def close(k, carry):
-        slab, piece = win.at[x, b], win.at[x, b, :, pl.ds(0, 384)]
-
-        @pl.when(k > 0)
-        def _():
-            for n in range(2):
-                left(piece, asend.at[k, n], me)
-            pl.when((b + k) % 2 == x)(lambda: left(wout.at[b], osend.at[k], me))
-
-        left(slab, xsend.at[k], me)
-        pl.when(c == x)(lambda: left(wout.at[b], osend.at[16 + k], me))
-        arrived(win.at[1 - x, k], xrecv.at[k], me)
-        pl.when(c != x)(lambda: arrived(wout.at[k], orecv.at[k], me))
+        piece = win.at[b, :, pl.ds(0, 384)]
+        f = (b + 16 - k) % 16
+        for n in range(2):
+            left(piece, asend.at[k, n], me)
+            arrived(win.at[f, :, pl.ds(n * 384, 384)], arecv.at[f, n], me)
+        pl.when((b + k) % 2 == x)(lambda: left(wout.at[b], osend.at[k], me))
+        pl.when(c == x)(lambda: arrived(wout.at[f], orecv.at[f], me))
         return carry
 
-    lax.fori_loop(0, 16, close, 0)
+    lax.fori_loop(1, 16, close, 0)
+    for n in range(2):
+        own_piece(n).wait()
+    pl.when(c == x)(lambda: own_down().wait())
     keep.wait()
     keep_o.wait()
     keep_k.wait()
 
 
-def run_front(states, wq, wk, wv, wo, extra, up, down, cosine, sine, bounds):
+def run_front(*operands):
     shape = jax.ShapeDtypeStruct
+    smem = pl.BlockSpec(memory_space=pltpu.SMEM)
     return pl.pallas_call(
         front_kernel,
         out_shape=(
-            shape((32, 48, 2304), BF),
+            shape((32, 48, WIDE), BF),
             shape((32, 48, 1536), BF),
             shape((32, 128, 512), BF),
-            shape((2, 16, 48, 768), BF),
+            shape((16, 48, 768), BF),
             shape((16, 48, 768), BF),
             shape((128, 1536), F32),
             shape((128, 1536), BF),
@@ -949,19 +971,21 @@
             shape((2, LANES, 128), BF),
             shape((128, 1536), F32),
             shape((2, 1, LANES), F32),
+            shape((8, 128), F32),
         ),
-        in_specs=[VMEM] + [ANY] * 7 + [VMEM] * 3,
-        out_specs=(ANY,) * 5 + (VMEM,) * 6,
+        in_specs=[VMEM, smem] + [VMEM] * 5 + [ANY] * 5,
+        out_specs=(ANY,) * 5 + (VMEM,) * 7,
         scratch_shapes=[
-            pltpu.VMEM((32, 48, 2304), BF),
+            pltpu.VMEM((32, 48, WIDE), BF),
             pltpu.VMEM((32, 48, 1536), BF),
             pltpu.VMEM((32, 128, 512), BF),
+            pltpu.VMEM((8, 48, 768), BF),
             pltpu.VMEM((2, 1, LANES), F32),
             pltpu.VMEM((2, 1, LANES), F32),
             pltpu.VMEM((2, 128, LANES), F32),
-            DMA((8,)),
-            DMA((4, 10)),
-            DMA((32, 2)),
+            DMA((7,)),
+            DMA((2, 4, 10)),
+            DMA((2, 32, 2)),
             DMA((4, 10)),
             DMA((32, 2)),
             DMA((4, 10)),
@@ -970,115 +994,139 @@
             DMA((16, 2)),
             DMA((16,)),
             DMA((16,)),
-            DMA((32,)),
-            DMA((16,)),
         ],
         compiler_params=params(1, 48),
         name="front",
-    )(states, wq, wk, wv, wo, extra, up, down, cosine, sine, bounds)
+    )(*operands)
 
 
 GELU_A = 0.7978845608028654
 GELU_B = 0.044715
 
 
+CUTS = 2
+CUT = 128 // CUTS
+
+
 def experts_kernel(
-    n2, h, teacher, weight, gate, win, wout,
-    final, err, dn2, dy_out, dwin, dwout,
-    nall, dyall, pairs, zg, dpairs, part, rc, ry, rz, acc, errs,
-    gsend, grecv, csend, crecv, ysend, yrecv, zsend, zrecv, esend, erecv,
+    n2, h, teacher, routes, gates, valid, count, win, wout,
+    final, err, dn2, dy_out, dwin_out, dwout_out,
+    nall, dyall, pairs, zg, dpairs, part, rc, ry, rz, acc, errs, tables, gate,
+    wfull, slab, wdown, dwin, dwin_in, dwout, dwout_in,
+    own_sem, gsend, grecv, csend, crecv, ysend, yrecv, zsend, zrecv, esend, erecv,
+    tsend, trecv, xsend, xrecv,
 ):
     me = Place()
     x, y, z, b, c = me.x, me.y, me.z, me.b, me.c
+    half = pltpu.make_async_copy(win, wfull.at[x], own_sem.at[0])
+    half.start()
+    held = pltpu.make_async_copy(wout, slab, own_sem.at[1])
+    pl.when(c == x)(held.start)
+    lane = lax.broadcasted_iota(jnp.int32, (128, 128), 1)
+    table = jnp.zeros((128, 128), F32)
+    for k in range(TOP):
+        table = table + jnp.where(routes[:, k : k + 1] == lane, gates[:, k : k + 1], 0.0)
+    tables[b] = table.T[0:8]
     greet_all(me)
 
-    def gather(buf, way, chunk):
-        def put(j, kind, n, s):
-            remote(buf.at[s], buf.at[s], gsend.at[way, j, n], grecv.at[way, s], me.near(kind)).start()
+    def rows_of(p):
+        return pl.ds(p * CUT, CUT)
+
+    def over_weights(k):
+        cut = pl.ds(k * 4, 4)
+        return remote(win.at[cut], wfull.at[x, cut], xsend.at[k], xrecv.at[k], me.near("x"))
+
+    def over_down():
+        return remote(wout, slab, xsend.at[4], xrecv.at[4], me.near("x"))
+
+    def gather(buf, way, between):
+        def put(j, p, kind, n, s):
+            ref = buf.at[s, rows_of(p)]
+            remote(ref, ref, gsend.at[way, j, p, n], grecv.at[way, s, p], me.near(kind)).start()
 
         def turn(j, carry):
-            zz = me.outward(j)
-            own = me.blk(zz, y, c)
-
-            @pl.when((j > 0) & (j < 4))
-            def _():
-                arrived(buf.at[own], grecv.at[way, own], me)
-
-            @pl.when(j < 4)
-            def _():
-                pl.when((zz <= z) & (z < NZ - 1))(lambda: put(j, "up", 0, own))
-                pl.when((zz >= z) & (z > 0))(lambda: put(j, "down", 1, own))
-                put(j, "y", 2, own)
-                put(j, "c", 3, own)
-
-            @pl.when(j > 0)
-            def _():
-                i = j - 1
-                zp = me.outward(i)
-                s = me.blk(zp, 1 - y, c)
-                arrived(buf.at[s], grecv.at[way, s], me)
-                put(i, "c", 4, s)
-
-                def both(n, carry):
-                    yy = (y + n) % 2
-                    s = me.blk(zp, yy, 1 - c)
-                    arrived(buf.at[s], grecv.at[way, s], me)
-                    chunk(zp * 2 + yy)
-                    return carry
-
-                lax.fori_loop(0, 2, both, 0)
-
+            for p in range(CUTS):
+                zz = me.outward(j)
+                own = me.blk(zz, y, c)
+
+                @pl.when((j > 0) & (j < 4))
+                def _():
+                    arrived(buf.at[own, rows_of(p)], grecv.at[way, own, p], me)
+
+                @pl.when(j < 4)
+                def _():
+                    pl.when((zz <= z) & (z < NZ - 1))(lambda: put(j, p, "up", 0, own))
+                    pl.when((zz >= z) & (z > 0))(lambda: put(j, p, "down", 1, own))
+                    put(j, p, "y", 2, own)
+                    put(j, p, "c", 3, own)
+
+                @pl.when((j > 0) & (j < 5))
+                def _():
+                    i = j - 1
+                    s = me.blk(me.outward(i), 1 - y, c)
+                    arrived(buf.at[s, rows_of(p)], grecv.at[way, s, p], me)
+                    put(i, p, "c", 4, s)
+
+                between(j, p)
             return carry
 
-        lax.fori_loop(0, 5, turn, 0)
+        lax.fori_loop(0, 6, turn, 0)
 
         def close(j, carry):
             zz = me.outward(j)
-            whole = buf.at[b]
-            pl.when((zz <= z) & (z < NZ - 1))(lambda: left(whole, gsend.at[way, j, 0], me))
-            pl.when((zz >= z) & (z > 0))(lambda: left(whole, gsend.at[way, j, 1], me))
-            for n in (2, 3, 4):
-                left(whole, gsend.at[way, j, n], me)
+            whole = buf.at[b, rows_of(0)]
+            for p in range(CUTS):
+                pl.when((zz <= z) & (z < NZ - 1))(lambda: left(whole, gsend.at[way, j, p, 0], me))
+                pl.when((zz >= z) & (z > 0))(lambda: left(whole, gsend.at[way, j, p, 1], me))
+                for n in (2, 3, 4):
+                    left(whole, gsend.at[way, j, p, n], me)
             return carry
 
         lax.fori_loop(0, 4, close, 0)
 
+    def from_core(buf, way, zz, yy):
+        s = me.blk(zz, yy, 1 - c)
+        for p in range(CUTS):
+            arrived(buf.at[s, rows_of(p)], grecv.at[way, s, p], me)
+
     def to_other_core(way, q):
-        remote(part.at[q * 2 + 1 - c], rc.at[way, q], csend.at[way, q], crecv.at[way, q], me.near("c")).start()
-
-    def reduce(way, between):
-        def lead(j, carry):
-            zz = me.inward(j)
-            q = zz * 2 + 1 - y
-            s = q * 2 + c
-            arrived(rc.at[way, q], crecv.at[way, q], me)
-            part[s] = (part[s].astype(F32) + rc[way, q].astype(F32)).astype(BF)
-            remote(part.at[s], ry.at[way, zz], ysend.at[way, j], yrecv.at[way, zz], me.near("y")).start()
-            return carry
-
-        lax.fori_loop(0, 4, lead, 0)
-
-        def turn(j, carry):
-            between(j)
-            zz = me.inward(j)
-            q = zz * 2 + y
-            s = q * 2 + c
-            arrived(rc.at[way, q], crecv.at[way, q], me)
-            arrived(ry.at[way, zz], yrecv.at[way, zz], me)
-            acc[...] = part[s].astype(F32) + rc[way, q].astype(F32) + ry[way, zz].astype(F32)
-            along_z(me, j, zz, acc, part.at[s], rz.at[way], zsend.at[way], 0, zrecv.at[way])
-            return carry
-
-        lax.fori_loop(0, 4, turn, 0)
-
+        remote(part.at[q * 2 + 1 - c], rc.at[q], csend.at[way, q], crecv.at[way, q], me.near("c")).start()
+
+    def lead(way, j):
+        zz = me.inward(j)
+        q = zz * 2 + 1 - y
+        s = q * 2 + c
+        arrived(rc.at[q], crecv.at[way, q], me)
+        part[s] = (part[s].astype(F32) + rc[q].astype(F32)).astype(BF)
+        for p in range(CUTS):
+            remote(
+                part.at[s, rows_of(p)], ry.at[zz, rows_of(p)], ysend.at[way, j, p], yrecv.at[way, zz, p], me.near("y")
+            ).start()
+
+    def follow(way, j):
+        zz = me.inward(j)
+        q = zz * 2 + y
+        s = q * 2 + c
+        arrived(rc.at[q], crecv.at[way, q], me)
+        for p in range(CUTS):
+            cut = rows_of(p)
+            arrived(ry.at[zz, cut], yrecv.at[way, zz, p], me)
+            piece = acc.at[cut]
+            piece[...] = part[s, cut].astype(F32) + rc[q, cut].astype(F32) + ry[zz, cut].astype(F32)
+            along_z(
+                me, j, zz, piece, part.at[s, cut], rz.at[:, cut], zsend.at[way, :, p], 0, zrecv.at[way, :, p]
+            )
+
+    def close_sum(way):
         def close(j, carry):
             zz = me.inward(j)
-            whole = part.at[b]
-            left(whole, ysend.at[way, j], me)
+            whole, piece = part.at[b], part.at[b, rows_of(0)]
             left(whole, csend.at[way, j], me)
             left(whole, csend.at[way, j + 4], me)
-            pl.when(zz > z)(lambda: left(whole, zsend.at[way, j, 0], me))
-            pl.when(zz < z)(lambda: left(whole, zsend.at[way, j, 1], me))
+            for p in range(CUTS):
+                left(piece, ysend.at[way, j, p], me)
+                pl.when(zz > z)(lambda: left(piece, zsend.at[way, j, p, 0], me))
+                pl.when(zz < z)(lambda: left(piece, zsend.at[way, j, p, 1], me))
             return carry
 
         lax.fori_loop(0, 4, close, 0)
@@ -1089,38 +1137,107 @@
 
     def forward(q):
         rows = nall[pl.ds(q * 2, 2)].reshape(256, 1536)
-        pair = jnp.dot(rows, win[...], preferred_element_type=F32)
+        pair = jnp.dot(rows, wfull[...].reshape(1536, 768), preferred_element_type=F32)
         pairs[q] = pair
         unused, a = gelu_parts(pair[:, :384])
-        zq = (a * pair[:, 384:] * gate[q]).astype(BF)
+        scale = gate[pl.ds(q * 2, 2)].reshape(256, 1)
+        zq = (a * pair[:, 384:] * scale).astype(BF)
         zg[q] = zq
-        out = jnp.dot(zq, wout[...], preferred_element_type=F32)
+        out = jnp.dot(zq, wdown[...], preferred_element_type=F32)
         part[pl.ds(q * 2, 2)] = out.astype(BF).reshape(2, 128, 1536)
         to_other_core(0, q)
 
     def backward(q):
         rows = dyall[pl.ds(q * 2, 2)].reshape(256, 1536)
-        dz = lax.dot_general(rows, wout[...], NT, preferred_element_type=F32) * gate[q]
+        scale = gate[pl.ds(q * 2, 2)].reshape(256, 1)
+        dz = lax.dot_general(rows, wdown[...], NT, preferred_element_type=F32) * scale
         g, u = pairs[q, :, :384], pairs[q, :, 384:]
         t, a = gelu_parts(g)
         slope = 0.5 * (1.0 + t) + 0.5 * g * (1.0 - t * t) * (GELU_A * (1.0 + 3.0 * GELU_B * g * g))
         dpairs[q, :, :384] = (dz * u * slope).astype(BF)
         dpairs[q, :, 384:] = (dz * a).astype(BF)
-        out = lax.dot_general(dpairs[q], win[...], NT, preferred_element_type=F32)
+        out = lax.dot_general(dpairs[q], wfull[...].reshape(1536, 768), NT, preferred_element_type=F32)
         part[pl.ds(q * 2, 2)] = out.astype(BF).reshape(2, 128, 1536)
         to_other_core(1, q)
 
     nall[b] = n2[...]
-    gather(nall, 0, forward)
-    reduce(0, lambda j: None)
-
+    held_wait = held.wait
+    pl.when(c == x)(held_wait)
+
+    def tell_gates(k, carry):
+        to = (b + k) % 16
+        remote(tables.at[b], tables.at[b], tsend.at[k], trecv.at[b], (x, to)).start()
+        return carry
+
+    def with_tokens(j, p):
+        if p == 0:
+            pl.when((j == 0) & (c == x))(lambda: over_down().start())
+            for k in range(4):
+                pl.when(j == k)(over_weights(k).start)
+        else:
+
+            @pl.when(j == 0)
+            def _():
+                lax.fori_loop(1, 16, tell_gates, 0)
+
+    gather(nall, 0, with_tokens)
+
+    def all_cores(buf, way):
+        def one(j, carry):
+            from_core(buf, way, j, y)
+            from_core(buf, way, j, 1 - y)
+            return carry
+
+        lax.fori_loop(0, 4, one, 0)
+
+    all_cores(nall, 0)
+    def hear_gates(k, carry):
+        left(tables.at[0], tsend.at[k], me)
+        arrived(tables.at[(b + 16 - k) % 16], trecv.at[(b + 16 - k) % 16], me)
+        return carry
+
+    lax.fori_loop(1, 16, hear_gates, 0)
+
+    def gate_of(s, carry):
+        row = lax.broadcasted_iota(jnp.int32, (8, 128), 0)
+        picked = jnp.sum(jnp.where(row == b // 2, tables[s], 0.0), axis=0, keepdims=True)
+        gate[s] = as_column(picked)
+        return carry
+
+    lax.fori_loop(0, 16, gate_of, 0)
+    half.wait()
+    for k in range(4):
+        arrived(wfull.at[1 - x, pl.ds(k * 4, 4)], xrecv.at[k], me)
+    pl.when(c != x)(lambda: arrived(slab, xrecv.at[4], me))
+    wide = slab[...].astype(F32).reshape(16, 2, 24, 768)
+    wdown[:, :768] = wide[:, 0].reshape(384, 768).astype(BF)
+    wdown[:, 768:] = wide[:, 1].reshape(384, 768).astype(BF)
+
+    def outputs(j, carry):
+        @pl.when(j < 4)
+        def _():
+            forward(me.inward(j) * 2 + 1 - y)
+
+        pl.when(j > 0)(lambda: follow(0, j - 1))
+
+        @pl.when(j < 4)
+        def _():
+            lead(0, j)
+            forward(me.inward(j) * 2 + y)
+
+        return carry
+
+    lax.fori_loop(0, 5, outputs, 0)
+    close_sum(0)
+
+    keep = as_column(valid[...].astype(F32))
     done = h[...] + acc[...]
     final[...] = done.astype(BF)
     diff = done - teacher[...].astype(F32)
-    scaled = weight[:, 0:1] * diff
+    scaled = (keep * (SPAN / count[0:1, 0:1])) * diff
     dy_out[...] = scaled
     dyall[b] = scaled.astype(BF)
-    kept = jnp.sum(weight[:, 1:2] * diff * diff)
+    kept = jnp.sum(keep * diff * diff)
     me_index = x * 16 + b
     errs[me_index] = jnp.zeros((8, 128), F32) + kept
 
@@ -1129,24 +1246,84 @@
         remote(errs.at[me_index], errs.at[me_index], esend.at[k], erecv.at[me_index], to).start()
         return carry
 
-    lax.fori_loop(1, 32, tell, 0)
-    gather(dyall, 1, backward)
-
-    def weight_part(j):
-        for i in range(2):
-
-            @pl.when(j * 2 + i < 6)
+    def with_dy(j, p):
+        if p == 0:
+
+            @pl.when((j > 0) & (j < 5))
             def _():
-                col = pl.ds(pl.multiple_of((j * 2 + i) * 256, 256), 256)
-                rows = nall[:, :, col].reshape(2048, 256)
-                both = dpairs[...].reshape(2048, 768)
-                dwin[col, :] = lax.dot_general(rows, both, TN, preferred_element_type=F32).astype(BF)
-                right = dyall[:, :, col].reshape(2048, 256)
-                zall = zg[...].reshape(2048, 384)
-                dwout[:, col] = lax.dot_general(zall, right, TN, preferred_element_type=F32).astype(BF)
-
-    reduce(1, weight_part)
+                zz = me.outward(j - 1)
+                from_core(dyall, 1, zz, y)
+                backward(zz * 2 + y)
+
+        else:
+
+            @pl.when(j == 0)
+            def _():
+                lax.fori_loop(1, 32, tell, 0)
+
+            @pl.when(j > 1)
+            def _():
+                zz = me.outward(j - 2)
+                from_core(dyall, 1, zz, 1 - y)
+                backward(zz * 2 + 1 - y)
+
+    gather(dyall, 1, with_dy)
+
+    def in_grad(i):
+        col = pl.ds(pl.multiple_of(i * 256, 256), 256)
+        rows = nall[:, :, col].reshape(2048, 256)
+        dwin[col, :] = lax.dot_general(
+            rows, dpairs[...].reshape(2048, 768), TN, preferred_element_type=F32
+        ).astype(BF)
+
+    def out_grad(i):
+        col = pl.ds(i * 256, 256)
+        right = dyall[:, :, col].reshape(2048, 256)
+        value = lax.dot_general(zg[...].reshape(2048, 384), right, TN, preferred_element_type=F32)
+        there = i // 3 * 24
+        dwout[:, there : there + 24, (i % 3) * 256 : (i % 3) * 256 + 256] = value.reshape(16, 24, 256)
+
+    def over_in(k):
+        src = dwin.at[pl.ds(pl.multiple_of((1 - x) * 768 + k * 256, 256), 256)]
+        return remote(src, dwin_in.at[pl.ds(k * 256, 256)], xsend.at[5 + k], xrecv.at[5 + k], me.near("x"))
+
+    def over_out():
+        return remote(slab, dwout_in, xsend.at[8], xrecv.at[8], me.near("x"))
+
+    def leads(j, carry):
+        lead(1, j)
+        return carry
+
+    lax.fori_loop(0, 4, leads, 0)
+
+    def sums(j, carry):
+        @pl.when(j == 0)
+        def _():
+            for k in range(3):
+                in_grad((1 - x) * 3 + k)
+                over_in(k).start()
+
+        @pl.when(j == 1)
+        def _():
+            for k in range(6):
+                out_grad(k)
+            slab[...] = dwout[...].astype(BF)
+            pl.when(c != x)(lambda: over_out().start())
+
+        @pl.when(j == 2)
+        def _():
+            for k in range(3):
+                in_grad(x * 3 + k)
+
+        follow(1, j)
+        return carry
+
+    for k in range(4):
+        over_weights(k).wait_send()
+    pl.when(c == x)(lambda: over_down().wait_send())
+    lax.fori_loop(0, 4, sums, 0)
     dn2[...] = acc[...]
+    close_sum(1)
 
     def hear(k, carry):
         left(errs.at[0], esend.at[k], me)
@@ -1158,24 +1335,45 @@
     total = errs[0]
     for s in range(1, 32):
         total = total + errs[s]
-    err[...] = total
-
-
-def run_experts(n2, h, teacher, weight, gate, win, wout):
+    err[...] = total / (1536.0 * count[...])
+
+    for k in range(3):
+        over_in(k).wait_send()
+        here = pl.ds(pl.multiple_of(x * 768 + k * 256, 256), 256)
+        there = pl.ds(k * 256, 256)
+        arrived(dwin_in.at[there], xrecv.at[5 + k], me)
+        dwin_in[there] = (dwin_in[there].astype(F32) + dwin[here, :].astype(F32)).astype(BF)
+    out = pltpu.make_async_copy(dwin_in, dwin_out, own_sem.at[0])
+    out.start()
+
+    @pl.when(c == x)
+    def _():
+        arrived(dwout_in, xrecv.at[8], me)
+        dwout_in[...] = (dwout_in[...].astype(F32) + dwout[...]).astype(BF)
+        copy = pltpu.make_async_copy(dwout_in, dwout_out, own_sem.at[1])
+        copy.start()
+        copy.wait()
+
+    pl.when(c != x)(lambda: over_out().wait_send())
+    out.wait()
+
+
+def run_experts(*operands):
     wide = (128, 1536)
     shard = (16,) + wide
+    shape = jax.ShapeDtypeStruct
     return pl.pallas_call(
         experts_kernel,
         out_shape=(
-            jax.ShapeDtypeStruct(wide, BF),
-            jax.ShapeDtypeStruct((8, 128), F32),
-            jax.ShapeDtypeStruct(wide, F32),
-            jax.ShapeDtypeStruct(wide, F32),
-            jax.ShapeDtypeStruct((1536, 768), BF),
-            jax.ShapeDtypeStruct((384, 1536), BF),
+            shape(wide, BF),
+            shape((8, 128), F32),
+            shape(wide, F32),
+            shape(wide, F32),
+            shape((768, 768), BF),
+            shape((16, 48, 768), BF),
         ),
-        in_specs=[VMEM] * 7,
-        out_specs=(VMEM,) * 6,
+        in_specs=[VMEM] * 7 + [ANY] * 2,
+        out_specs=(VMEM,) * 4 + (ANY,) * 2,
         scratch_shapes=[
             pltpu.VMEM(shard, BF),
             pltpu.VMEM(shard, BF),
@@ -1183,25 +1381,39 @@
             pltpu.VMEM((8, 256, 384), BF),
             pltpu.VMEM((8, 256, 768), BF),
             pltpu.VMEM(shard, BF),
-            pltpu.VMEM((2, 8) + wide, BF),
-            pltpu.VMEM((2, 4) + wide, BF),
-            pltpu.VMEM((2, 5) + wide, BF),
+            pltpu.VMEM((8,) + wide, BF),
+            pltpu.VMEM((4,) + wide, BF),
+            pltpu.VMEM((5,) + wide, BF),
             pltpu.VMEM(wide, F32),
             pltpu.VMEM((32, 8, 128), F32),
-            DMA((2, 4, 5)),
-            DMA((2, 16)),
+            pltpu.VMEM((16, 8, 128), F32),
+            pltpu.VMEM((16, 128, 1), F32),
+            pltpu.VMEM((2, 16, 48, 768), BF),
+            pltpu.VMEM((16, 48, 768), BF),
+            pltpu.VMEM((384, 1536), BF),
+            pltpu.VMEM((1536, 768), BF),
+            pltpu.VMEM((768, 768), BF),
+            pltpu.VMEM((16, 48, 768), F32),
+            pltpu.VMEM((16, 48, 768), BF),
+            DMA((2,)),
+            DMA((2, 4, CUTS, 5)),
+            DMA((2, 16, CUTS)),
             DMA((2, 8)),
             DMA((2, 8)),
-            DMA((2, 4)),
-            DMA((2, 4)),
-            DMA((2, 4, 2)),
-            DMA((2, 5)),
+            DMA((2, 4, CUTS)),
+            DMA((2, 4, CUTS)),
+            DMA((2, 4, CUTS, 2)),
+            DMA((2, 5, CUTS)),
             DMA((32,)),
             DMA((32,)),
+            DMA((16,)),
+            DMA((16,)),
+            DMA((9,)),
+            DMA((9,)),
         ],
-        compiler_params=params(2, 61),
+        compiler_params=params(2, 62),
         name="experts",
-    )(n2, h, teacher, weight, gate, win, wout)
+    )(*operands)
 
 
 def norm_back(values, gain, grad):
@@ -1214,12 +1426,12 @@
 
 
 def back_kernel(
-    states, h, n1, qs, o, lse, dn2, dy, cosine, sine, bounds, dwin, dwout, gq, go, kv_in,
-    gx, gqkv, gout, gup, gdown,
-    wq, wo, kv, pk, dos, delta, dh, dq, dkv, dqkv, xin, xout, *rest,
+    states, h, n1, qs, o, lse, dn2, dy, doc, freq, dwin, dwout, gq, go, kv_in,
+    gx, gqw, gkw, gvw, gnorm, gout, gup, gdown,
+    wq, wo, kv, pk, dos, delta, dh, dq, dkv, dqkv, gqkv, *rest,
 ):
-    sums = [(rest[i * 10 : i * 10 + 5], rest[i * 10 + 5 : i * 10 + 10]) for i in range(3)]
-    own_sem, xsend, xrecv, asend, arecv, osend, orecv = rest[30:]
+    sums = [(rest[i * 11 : i * 11 + 6], rest[i * 11 + 6 : i * 11 + 11]) for i in range(4)]
+    own_sem, asend, arecv, osend, orecv = rest[44:]
     me = Place()
     x, y, z, b, c = me.x, me.y, me.z, me.b, me.c
     loads = [
@@ -1231,57 +1443,36 @@
         load.start()
     greet_all(me)
 
-    def over(k, carry):
+    def own_piece(n):
+        col = pl.multiple_of(n * 768 + c * 384, 128)
+        return pltpu.make_async_copy(
+            dwin.at[b, :, pl.ds(n * 384, 384)], gup.at[b // 2, :, pl.ds(col, 384)], own_sem.at[3 + n]
+        )
+
+    def own_down():
+        return pltpu.make_async_copy(dwout.at[b], gdown.at[b // 2], own_sem.at[5])
+
+    def deal(k, carry):
         t = (b + k) % 16
-        remote(dwin.at[1 - x, t], xin.at[t], xsend.at[k], xrecv.at[t], me.near("x")).start()
-        pl.when(c != x)(
-            lambda: remote(dwout.at[t], xout.at[t], osend.at[k], orecv.at[t], me.near("x")).start()
+        for n in range(2):
+            col = pl.multiple_of(n * 768 + c * 384, 128)
+            remote(
+                dwin.at[t, :, pl.ds(n * 384, 384)],
+                gup.at[b // 2, :, pl.ds(col, 384)],
+                asend.at[k, n],
+                arecv.at[b, n],
+                (x, t),
+            ).start()
+        pl.when(c == x)(
+            lambda: remote(dwout.at[t], gdown.at[b // 2], osend.at[k], orecv.at[b // 2], (x, t)).start()
         )
         return carry
 
-    lax.fori_loop(0, 16, over, 0)
-
-    def own_piece(n, t):
-        col = pl.multiple_of(n * 768 + c * 384, 128)
-        return (
-            xin.at[t, :, pl.ds(n * 384, 384)],
-            gup.at[b // 2, :, pl.ds(col, 384)],
-        )
-
-    def deal(k, carry):
-        t = (b + k) % 16
-        arrived(xin.at[t], xrecv.at[t], me)
-        xin[t] = (xin[t].astype(F32) + dwin[x, t].astype(F32)).astype(BF)
-
-        @pl.when(k > 0)
-        def _():
-            for n in range(2):
-                src, dst = own_piece(n, t)
-                remote(src, dst, asend.at[k, n], arecv.at[b, n], (x, t)).start()
-
-        @pl.when(k == 0)
-        def _():
-            for n in range(2):
-                src, dst = own_piece(n, t)
-                pltpu.make_async_copy(src, dst, own_sem.at[3 + n]).start()
-
-        @pl.when(c == x)
-        def _():
-            arrived(xout.at[t], orecv.at[t], me)
-            xout[t] = (xout[t].astype(F32) + dwout[t].astype(F32)).astype(BF)
-            pl.when(k > 0)(
-                lambda: remote(
-                    xout.at[t], gdown.at[b // 2], osend.at[16 + k], orecv.at[16 + b // 2], (x, t)
-                ).start()
-            )
-            pl.when(k == 0)(
-                lambda: pltpu.make_async_copy(xout.at[t], gdown.at[b // 2], own_sem.at[5]).start()
-            )
-
-        return carry
-
+    for n in range(2):
+        own_piece(n).start()
+    pl.when(c == x)(lambda: own_down().start())
     loads[2].wait()
-    gains = wq[:, :, pl.ds(2048, 128)].reshape(1536, 128).astype(F32).T
+    gains = wq[:, :, pl.ds(QKV, 128)].reshape(1536, 128).astype(F32).T
     res_grad, gain_two = norm_back(h[...], gains[1:2], dn2[...])
     dh[...] = dy[...] + res_grad
     da = dh[...].astype(BF)
@@ -1310,6 +1501,7 @@
         prod = do[:, col : col + 128].astype(F32) * o[:, col : col + 128]
         delta[i // GROUP, :, r : r + 128] = jnp.sum(prod.T, axis=0, keepdims=True)
     dq[...] = jnp.zeros_like(dq)
+    bounds = query_bounds(me, doc)
     loads[1].wait()
 
     def block(n):
@@ -1329,10 +1521,7 @@
 
     def turn(j, carry):
         out_sum.turn(j)
-
-        @pl.when((j >= 2) & (j < 4))
-        def _():
-            lax.fori_loop((j - 2) * 8, (j - 2) * 8 + 8, deal, 0)
+        lax.fori_loop(1 + j * 3, jnp.minimum(4 + j * 3, 16), deal, 0)
 
         @pl.when(key_sum.valid(j))
         def _():
@@ -1356,82 +1545,82 @@
 
     lax.fori_loop(0, 6, turn, 0)
 
-    cos, sin = cosine[...], -sine[...]
+    cos, sin = rotary_tables(me, doc, freq)
     for i in range(QUERY_HEADS):
         r = (i % GROUP) * 128
         head = dq[i // GROUP, :, r : r + 128].T * SCALE
-        dqkv[:, i * 128 : i * 128 + 128] = turned(head, cos, sin).astype(BF)
+        dqkv[:, i * 128 : i * 128 + 128] = turned(head, cos, -sin).astype(BF)
     for i in range(2):
-        dqkv[:, 1536 + i * 128 : 1664 + i * 128] = turned(dkv[:, i * 128 : i * 128 + 128], cos, sin).astype(BF)
+        dqkv[:, 1536 + i * 128 : 1664 + i * 128] = turned(dkv[:, i * 128 : i * 128 + 128], cos, -sin).astype(BF)
         dqkv[:, 1792 + i * 128 : 1920 + i * 128] = dkv[:, 256 + i * 128 : 384 + i * 128].astype(BF)
     dn1 = lax.dot_general(
-        dqkv[...], wq[:, :, pl.ds(0, 2048)].reshape(1536, 2048), NT, preferred_element_type=F32
+        dqkv[...], wq[:, :, pl.ds(0, QKV)].reshape(1536, QKV), NT, preferred_element_type=F32
     )
     in_grad, gain_one = norm_back(states[...].astype(F32), gains[0:1], dn1)
     gx[...] = dh[...] + in_grad
     rows = lax.broadcasted_iota(jnp.int32, (128, 1536), 0)
     tail = jnp.where(rows == 0, gain_one, jnp.where(rows == 1, gain_two, 0.0)).T
-    wq[:, :, pl.ds(2048, 128)] = tail.astype(BF).reshape(32, 48, 128)
+    wq[:, :, pl.ds(QKV, 128)] = tail.astype(BF).reshape(32, 48, 128)
     for i in range(4):
         part = lax.dot_general(
             n1[:, i * 384 : i * 384 + 384], dqkv[...], TN, preferred_element_type=F32
         )
-        wq[i * 8 : i * 8 + 8, :, 0:2048] = part.astype(BF).reshape(8, 48, 2048)
-    proj_sum = Sum(me, wq, by_weight, gqkv, *sums[2])
-    lead_all(proj_sum)
+        wq[i * 8 : i * 8 + 8, :, 0:QKV] = part.astype(BF).reshape(8, 48, QKV)
+    proj = [Sum(me, wq, by_weight, gqkv, *sums[2 + i], PIECES[i]) for i in range(2)]
+    for piece in proj:
+        lead_all(piece)
 
     def last_turn(j, carry):
-        proj_sum.turn(j)
+        for piece in proj:
+            piece.turn(j)
         return carry
 
     lax.fori_loop(0, 6, last_turn, 0)
+    gqw[...] = gqkv[:, 0:1536]
+    gkw[...] = gqkv[:, 1536:1792]
+    gvw[...] = gqkv[:, 1792:2048]
+    gnorm[0:1, :] = as_row(gqkv[:, 2048:2049])
+    gnorm[1:2, :] = as_row(gqkv[:, 2049:2050])
     out_sum.close()
     key_sum.close()
-    proj_sum.close()
+    for piece in proj:
+        piece.close()
 
     def close(k, carry):
-        left(xin.at[0], xsend.at[k], me)
-        pl.when(c != x)(lambda: left(xout.at[0], osend.at[k], me))
-
-        @pl.when(k > 0)
-        def _():
-            f = (b + 16 - k) % 16
-            for n in range(2):
-                left(xin.at[0, :, pl.ds(0, 384)], asend.at[k, n], me)
-                col = pl.multiple_of(n * 768 + (f % 2) * 384, 128)
-                arrived(gup.at[f // 2, :, pl.ds(col, 384)], arecv.at[f, n], me)
-            pl.when(c == x)(lambda: left(xout.at[0], osend.at[16 + k], me))
-            pl.when(f % 2 == x)(lambda: arrived(gdown.at[f // 2], orecv.at[16 + f // 2], me))
-
-        @pl.when(k == 0)
-        def _():
-            for n in range(2):
-                src, dst = own_piece(n, b)
-                pltpu.make_async_copy(src, dst, own_sem.at[3 + n]).wait()
-            pl.when(c == x)(
-                lambda: pltpu.make_async_copy(xout.at[b], gdown.at[b // 2], own_sem.at[5]).wait()
-            )
-
+        f = (b + 16 - k) % 16
+        for n in range(2):
+            left(dwin.at[0, :, pl.ds(0, 384)], asend.at[k, n], me)
+            col = pl.multiple_of(n * 768 + (f % 2) * 384, 128)
+            arrived(gup.at[f // 2, :, pl.ds(col, 384)], arecv.at[f, n], me)
+        pl.when(c == x)(lambda: left(dwout.at[0], osend.at[k], me))
+        pl.when(f % 2 == x)(lambda: arrived(gdown.at[f // 2], orecv.at[f // 2], me))
         return carry
 
-    lax.fori_loop(0, 16, close, 0)
+    lax.fori_loop(1, 16, close, 0)
+    for n in range(2):
+        own_piece(n).wait()
+    pl.when(c == x)(lambda: own_down().wait())
 
 
 def run_back(*operands):
     shape = jax.ShapeDtypeStruct
+    smem = pl.BlockSpec(memory_space=pltpu.SMEM)
     return pl.pallas_call(
         back_kernel,
         out_shape=(
             shape((128, 1536), F32),
-            shape((48, 2304), F32),
+            shape((48, 1536), F32),
+            shape((48, 256), F32),
+            shape((48, 256), F32),
+            shape((2, 48), F32),
             shape((48, 1536), F32),
             shape((8, 48, 1536), BF),
             shape((8, 48, 768), BF),
         ),
-        in_specs=[VMEM] * 13 + [ANY] * 3,
-        out_specs=(VMEM,) * 3 + (ANY,) * 2,
+        in_specs=[VMEM] * 8 + [smem, VMEM] + [ANY] * 5,
+        out_specs=(VMEM,) * 6 + (ANY,) * 2,
         scratch_shapes=[
-            pltpu.VMEM((32, 48, 2304), BF),
+            pltpu.VMEM((32, 48, WIDE), BF),
             pltpu.VMEM((32, 48, 1536), BF),
             pltpu.VMEM((32, 128, 512), BF),
             pltpu.VMEM((32, 128, 512), BF),
@@ -1440,14 +1629,14 @@
             pltpu.VMEM((128, 1536), F32),
             pltpu.VMEM((2, 128, LANES), F32),
             pltpu.VMEM((128, 512), F32),
-            pltpu.VMEM((128, 2048), BF),
-            pltpu.VMEM((16, 48, 768), BF),
-            pltpu.VMEM((16, 48, 768), BF),
+            pltpu.VMEM((128, QKV), BF),
+            pltpu.VMEM((48, WIDE), F32),
         ]
         + Sum.room(48, 1536)
         + Sum.room(128, 512)
-        + Sum.room(48, 2304)
-        + [DMA((6,)), DMA((16,)), DMA((16,)), DMA((16, 2)), DMA((16, 2)), DMA((32,)), DMA((32,))],
+        + Sum.room(48, PIECES[0][1])
+        + Sum.room(48, PIECES[1][1])
+        + [DMA((6,)), DMA((16, 2)), DMA((16, 2)), DMA((16,)), DMA((8,))],
         compiler_params=params(3, 61),
         name="back",
     )(*operands)
@@ -1459,63 +1648,35 @@
 ):
     tokens = states.shape[2]
     width = states.shape[3]
-    b, x = lax.axis_index("blk"), lax.axis_index("head")
-    span = tokens * lax.axis_size("head") * lax.axis_size("blk")
-    place = (b * 2 + x) * tokens + jnp.arange(tokens, dtype=jnp.int32)
-    unused_segment, position = doc_layout(place, doc_starts)
     half = HEAD_SIZE // 2
-    freq = ROTARY_BASE ** (-jnp.arange(half).astype(jnp.float32) / half)
-    angle = position.astype(jnp.float32)[:, None] * freq[None, :]
-    cosine, sine = jnp.cos(angle), jnp.sin(angle)
-    cosine = jnp.concatenate([cosine, cosine], axis=1)
-    sine = jnp.concatenate([-sine, sine], axis=1)
-    bounds = jnp.tile(jnp.stack([place - position, place]), (1, GROUP))
-    keep_mask = valid.reshape(tokens).astype(F32)
-    route_rows = routes.reshape(tokens, TOP)
-    gate_rows = gates.reshape(tokens, TOP)
-
-    table = jnp.sum(
-        jnp.where(route_rows[None] == jnp.arange(E, dtype=jnp.int32)[:, None, None], gate_rows[None], 0.0), axis=-1
-    )
-    high = lax.reduce_precision(table, 8, 7)
-    column = jnp.arange(128)[None, :]
-    gains = jnp.where(
-        column == 0,
-        norm_one[:, None].astype(F32),
-        jnp.where(column == 1, norm_two[:, None].astype(F32), jnp.sum(keep_mask)),
-    )
-    routed = jnp.concatenate([high, table - high, jnp.zeros((32, 128), F32)], axis=0)
-    extra = jnp.concatenate([gains, routed], axis=1).astype(BF)
+    freq = np.float32(ROTARY_BASE) ** (-np.arange(half).astype(np.float32) / np.float32(half))
+    freq = jnp.asarray(np.concatenate([freq, freq])[None, :], F32)
     rows = states.reshape(tokens, width)
-    gq, go, kv, win, wout, h, n2, n1, qs, o, lse = run_front(
-        rows, w_query, key_weight, value_weight, w_output, extra, expert_in,
-        expert_out.reshape(E, 48, 768), cosine, sine, bounds,
-    )
-    count_all = jnp.sum(gq[:, 0, 2050].astype(F32))
-    tables = lax.dynamic_slice_in_dim(gq[:, :16, 2176:], x * 16, 16, 0).astype(F32)
-    mine = lax.dynamic_slice_in_dim(tables, b // 2, 1, 1) + lax.dynamic_slice_in_dim(tables, 8 + b // 2, 1, 1)
-    weight = jnp.stack([keep_mask * (span * 1.0 / count_all), keep_mask], axis=1)
+    kept = valid.reshape(1, tokens)
+    gq, go, kv, win, wout, h, n2, n1, qs, o, lse, count = run_front(
+        rows, doc_starts, freq, norm_one.reshape(1, -1), norm_two.reshape(1, -1), kept, expert_out,
+        w_query, key_weight, value_weight, w_output, expert_in,
+    )
     final, error, dn2, dy, dwin, dwout = run_experts(
-        n2, h, teacher.reshape(tokens, width), weight, mine.reshape(8, 256, 1),
-        win.reshape(1536, 768), wout.reshape(384, 1536),
-    )
-    gx, gqkv, gout, gup, gdown = run_back(
-        rows, h, n1, qs, o, lse, dn2, dy, cosine, sine, bounds,
-        dwin.reshape(2, 16, 48, 768), dwout.reshape(16, 48, 768), gq, go, kv,
+        n2, h, teacher.reshape(tokens, width), routes.reshape(tokens, TOP), gates.reshape(tokens, TOP),
+        kept, count, win, wout,
+    )
+    gx, gqw, gkw, gvw, gnorm, gout, gup, gdown = run_back(
+        rows, h, n1, qs, o, lse, dn2, dy, doc_starts, freq, dwin.reshape(16, 48, 768), dwout, gq, go, kv
     )
     shape = states.shape
     return (
         final.reshape(shape),
-        error[0, 0] / (width * count_all),
+        error[0, 0],
         gx.reshape(shape),
-        gqkv[:, 2048],
-        gqkv[:, :1536],
-        gqkv[:, 1536:1792],
-        gqkv[:, 1792:2048],
+        gnorm[0],
+        gqw,
+        gkw,
+        gvw,
         gout,
-        gqkv[:, 2049],
+        gnorm[1],
         gup.astype(F32),
-        gdown.astype(F32).reshape(E, 24, 1536),
+        gdown.astype(F32).reshape(E, 2, 24, 768).transpose(0, 2, 1, 3).reshape(E, 24, 1536),
     )
 
 

time: 558 us -> 440 us (0.79)
  Pallas kernels: 509 us -> 407 us
    pallas_call x2, Pallas kernels: 349 us -> 296 us  [the longest x1 184 us: run_experts(): pl.pallas_call(experts_kernel, out_shape=(shape(wide, BF), shape((8, 128)...]
    pallas_call x1, Pallas kernels: 161 us -> 112 us  [run_back(): pl.pallas_call(back_kernel, out_shape=(shape((128, 1536), F32), shape((48...]
    unnamed x43 -> x64, local copies, waits for them, and re-layouts: 11.3 us -> 20.7 us
    reshape x5 -> x1, local copies, waits for them, and re-layouts: 9.59 us -> 1.14 us  [per_device(): gdown.astype(F32).reshape(E, 2, 24, 768).transpose(0, 2, 1, 3)]
    slice x5 -> x1, local copies, waits for them, and re-layouts: 6.82 us -> 1.19 us  [per_device(): error[0, 0]]
where the time goes in v3:
time: 440 us; the launch traced here: 436 us
  Pallas kernels  407 us (92%)
  local copies, waits for them, and re-layouts  24.2 us (6%)
    pallas_call x1, Pallas kernels, run_experts(): pl.pallas_call(experts_kernel, out_shape=(shape(wide, BF), shape((8, 128)...  184 us
    pallas_call x1, Pallas kernels, run_back(): pl.pallas_call(back_kernel, out_shape=(shape((128, 1536), F32), shape((48...  112 us
    pallas_call x1, Pallas kernels, run_front(): pl.pallas_call(front_kernel, out_shape=(shape((32, 48, WIDE), BF), shape(...  111 us
    unnamed x64, local copies, waits for them, and re-layouts  20.7 us

profile of v3, /device:TPU:0, one launch (start us, length us, event | category | flops | bytes accessed | tf_op | source)
XLA Modules:
  0.0 435.5 jit_solution(7011936372778611368)
XLA Ops:
  0.7 1.0 copy-done.1
  1.6 1.1 copy-done.4
  2.7 0.9 copy-done.8
  3.6 0.9 copy-done.9
  4.5 0.7 copy-done.10
  5.3 0.7 copy-done.11
  9.3 111.3 %front.1 = (bf16[32,48,2176]{2,1,0:T(8,128)(2,1)}, bf16[32,48,1536]{2,1,0:T(8,128)(2,1)}, bf16[32,128,512]{2,1,0:T(8,128)(2,1)}, bf16[16,48,768]{2,1,0:T(8,128)(...) custom-call(bf16[128,1536]{1,0:T(8,128)(2,1)S(1)} %bitcast.22, ...), custom_call_target="tpu_custom_call" | custom-call | tf_op jit(solution)/shard_map/front/pallas_call | solution.py:960
  120.7 0.9 copy-done
  121.5 1.0 copy-done.2
  122.5 0.9 copy-done.3
  123.4 0.7 copy-done.5
  124.2 0.8 copy-done.6
  124.9 0.8 copy-done.7
  126.9 0.7 copy.26
  127.6 0.7 copy.27
  128.4 184.5 %experts.1 = (bf16[128,1536]{1,0:T(8,128)(2,1)}, f32[8,128]{1,0:T(8,128)}, f32[128,1536]{1,0:T(8,128)}, f32[128,1536]{1,0:T(8,128)}, bf16[768,768]{1,0:T(8,128)(2,1)}, /*index=5*/bf16[16,48,768]{2,1,0:T(8,128)(2,1)}) custom-call(bf16[128,1536]{1,0:T(8,128)(2,1)} %copy-done.5, f32[128,1536]{1,0:T(8,128)} %copy-done, bf16[128,1536]{1,0:T(8,128)(2,1)} %bitcast.31, ...), custom_call_target="tpu_custom_call" | custom-call | tf_op jit(solution)/shard_map/experts/pallas_call | solution.py:1365
  312.9 1.2 slice.9
  314.0 111.6 %back.1 = (f32[128,1536]{1,0:T(8,128)}, f32[48,1536]{1,0:T(8,128)}, f32[48,256]{1,0:T(8,128)}, f32[48,256]{1,0:T(8,128)}, f32[2,48]{1,0:T(2,128)}, /*index=5*/f3...) custom-call(bf16[128,1536]{1,0:T(8,128)(2,1)} %bitcast.21, f32[128,1536]{1,0:T(8,128)} %copy-done, ...), custom_call_target="tpu_custom_call" | custom-call | tf_op jit(solution)/shard_map/back/pallas_call | solution.py:1608
  425.6 1.3 slice_bitcast_fusion
  426.9 3.0 convert_element_type.4
  430.1 1.1 copy.29
  431.2 0.7 copy.36
  432.0 0.9 copy.37
  432.9 0.7 copy.38
  (48 shorter events, 6.6 us)
Async XLA Ops:
  0.6 1.0 copy-start.1
  1.6 1.1 copy-start.4
  2.7 0.9 copy-start.8
  3.6 0.9 copy-start.9
  4.5 0.7 copy-start.10
  5.3 0.7 copy-start.11
  6.0 0.7 copy-start.14
  7.3 0.7 copy-start.16
  8.6 0.7 copy-start.18
  9.3 117.6 %copy-start.26 = (s32[1,1,128,4]{2,3,1,0:T(4,128)S(1)}, s32[1,1,128,4]{2,3,1,0:T(4,128)}, u32[]{:S(2)}) copy-start(s32[1,1,128,4]{2,3,1,0:T(4,128)} %param.18) | copy-start | bytes 6148
  9.3 118.3 %copy-start.27 = (f32[1,1,128,4]{2,3,1,0:T(4,128)S(1)}, f32[1,1,128,4]{2,3,1,0:T(4,128)}, u32[]{:S(2)}) copy-start(f32[1,1,128,4]{2,3,1,0:T(4,128)} %param.19) | copy-start | bytes 6148
  120.6 0.9 copy-start
  121.5 1.0 copy-start.2
  122.5 0.9 copy-start.3
  123.4 0.7 copy-start.5
  124.2 0.8 copy-start.6
  124.9 0.8 copy-start.7
  426.9 3.0 copy-start.20
  430.0 1.2 copy-start.21
  430.1 1.9 copy-start.19
  431.2 1.6 copy-start.23
  432.0 1.6 copy-start.25
  432.0 2.2 copy-start.24
  432.0 2.9 copy-start.22
  (4 other events, 2.5 us)

commit v4 on v3

--- a/solution.py
+++ b/solution.py
@@ -780,10 +780,10 @@
 
 
 def front_kernel(
-    states, doc, freq, norm_one, norm_two, valid, down_in, wq, wk, wv, wo, up,
-    gq_out, go_out, kv_out, win, wout, h, n2, n1, qs, o_out, lse, count,
-    gq, go, kv, down, top, total, acc,
-    own_sem, qsend, qrecv, gsend, grecv, ksend, krecv, asend, arecv, osend, orecv,
+    doc, freq, norm_one, norm_two, valid, states, down_in, wq, wk, wv, wo, up,
+    gq_out, go_out, kv_out, win, wout, h_out, n2_out, n1_out, qs_out, o_out, lse, count,
+    gq, go, kv, down, top, total, acc, low_rows, down_raw, cos, sin, n1, qs, o, h, n2,
+    load_sem, own_sem, qsend, qrecv, gsend, grecv, ksend, krecv, asend, arecv, osend, orecv,
 ):
     me = Place()
     x, y, z, b, c = me.x, me.y, me.z, me.b, me.c
@@ -794,7 +794,11 @@
         pltpu.make_async_copy(wv, gq.at[here, :, pl.ds(1792, 256)], own_sem.at[2]),
         pltpu.make_async_copy(wo, go.at[here], own_sem.at[3]),
     ]
-    for copy in mine:
+    loads = [
+        pltpu.make_async_copy(down_in, down_raw, load_sem.at[0]),
+        pltpu.make_async_copy(states, low_rows, load_sem.at[1]),
+    ]
+    for copy in mine + loads:
         copy.start()
 
     lane = lax.broadcasted_iota(jnp.int32, (48, 128), 1)
@@ -805,8 +809,9 @@
         jnp.where(lane == 1, as_column(norm_two[...].astype(F32)), jnp.where(lane == 2, kept, 0.0)),
     )
     gq[here, :, pl.ds(QKV, 128)] = extra.astype(BF)
+    loads[0].wait()
     for e in range(E):
-        wide = down_in[e].astype(F32)
+        wide = down_raw[e].astype(F32)
         down[e] = jnp.concatenate([wide[:, :768], wide[:, 768:]], axis=0).astype(BF)
     greet_all(me)
     for copy in mine:
@@ -845,40 +850,52 @@
         for piece in weights:
             piece.turn(j)
         lax.fori_loop(1 + j * 3, jnp.minimum(4 + j * 3, 16), deal, 0)
+
+        @pl.when(j == 0)
+        def _():
+            cos[...], sin[...] = rotary_tables(me, doc, freq)
+
         return carry
 
     lax.fori_loop(0, 6, first_turn, 0)
     for n in range(2):
         own_piece(n).start()
     pl.when(c == x)(lambda: own_down().start())
-    cos, sin = rotary_tables(me, doc, freq)
     bounds = query_bounds(me, doc)
+    loads[1].wait()
+    rows = low_rows[...].astype(F32)
+    level = rows * lax.rsqrt(jnp.mean(rows * rows, axis=-1, keepdims=True) + 1e-06)
     for piece in weights:
         piece.close()
     keep = pltpu.make_async_copy(gq, gq_out, own_sem.at[0])
     keep.start()
 
-    rows = states[...].astype(F32)
     gains = gq[:, :, pl.ds(QKV, 128)].reshape(1536, 128).astype(F32).T
-    count[...] = jnp.zeros((8, 128), F32) + jnp.sum(gains[2:3]) / 48.0
-    n1[...] = (
-        rows * lax.rsqrt(jnp.mean(rows * rows, axis=-1, keepdims=True) + 1e-06) * gains[0:1]
-    ).astype(BF)
-    qkv = jnp.dot(n1[...], gq[:, :, pl.ds(0, QKV)].reshape(1536, QKV), preferred_element_type=F32)
+    n1[...] = (level * gains[0:1]).astype(BF)
+    turns = cos[...], sin[...]
     at = by_token(x, z, y, c)
+    keys = Gather(me, kv, by_token, ksend, krecv, causal=True)
+    output = Gather(me, go, by_weight, gsend, grecv)
+    both = jnp.dot(n1[...], gq[:, :, pl.ds(1536, 512)].reshape(1536, 512), preferred_element_type=F32)
     for i in range(2):
-        kv[at, :, i * 128 : i * 128 + 128] = turned(qkv[:, 1536 + i * 128 : 1664 + i * 128], cos, sin).astype(BF)
-        kv[at, :, 256 + i * 128 : 384 + i * 128] = qkv[:, 1792 + i * 128 : 1920 + i * 128].astype(BF)
+        kv[at, :, i * 128 : i * 128 + 128] = turned(both[:, i * 128 : i * 128 + 128], *turns).astype(BF)
+    kv[at, :, 256:512] = both[:, 256:512].astype(BF)
+    keys.turn(0)
+    query = jnp.dot(n1[...], gq[:, :, pl.ds(0, 1536)].reshape(1536, 1536), preferred_element_type=F32)
     for i in range(QUERY_HEADS):
         r = (i % GROUP) * 128
-        qs[i // GROUP, r : r + 128] = turned(qkv[:, i * 128 : i * 128 + 128], cos, sin).astype(BF)
+        qs[i // GROUP, r : r + 128] = turned(query[:, i * 128 : i * 128 + 128], *turns).astype(BF)
+    count[...] = jnp.zeros((8, 128), F32) + jnp.sum(gains[2:3]) / 48.0
+    saved = [
+        pltpu.make_async_copy(n1, n1_out, load_sem.at[0]),
+        pltpu.make_async_copy(qs, qs_out, load_sem.at[1]),
+    ]
+    for copy in saved:
+        copy.start()
 
     top[...] = jnp.full_like(top, FLOOR_SCORE)
     total[...] = jnp.zeros_like(total)
     acc[...] = jnp.zeros_like(acc)
-    keys = Gather(me, kv, by_token, ksend, krecv, causal=True)
-    output = Gather(me, go, by_weight, gsend, grecv)
-
     def block(n):
         ok = allowed_keys(n * 256, bounds)
         for i in range(2):
@@ -895,7 +912,7 @@
             acc[i] = acc[i] * factor + lax.dot_general(v, p.astype(BF), TN, preferred_element_type=F32)
 
     def turn(j, carry):
-        keys.turn(j)
+        pl.when(j > 0)(lambda: keys.turn(j))
         output.turn(j - 2)
 
         @pl.when(keys.valid(j - 2))
@@ -924,14 +941,20 @@
         done = acc[i] / total[i]
         for r in range(GROUP):
             col = (i * GROUP + r) * 128
-            o_out[:, col : col + 128] = done[:, r * 128 : r * 128 + 128].T
-    res = rows + jnp.dot(
-        o_out[...].astype(BF), go[...].reshape(1536, 1536), preferred_element_type=F32
+            o[:, col : col + 128] = done[:, r * 128 : r * 128 + 128].T
+    saved.append(pltpu.make_async_copy(o, o_out, load_sem.at[2]))
+    saved[2].start()
+    res = low_rows[...].astype(F32) + jnp.dot(
+        o[...].astype(BF), go[...].reshape(1536, 1536), preferred_element_type=F32
     )
     h[...] = res
     n2[...] = (
         res * lax.rsqrt(jnp.mean(res * res, axis=-1, keepdims=True) + 1e-06) * gains[1:2]
     ).astype(BF)
+    saved.append(pltpu.make_async_copy(h, h_out, load_sem.at[3]))
+    saved.append(pltpu.make_async_copy(n2, n2_out, load_sem.at[4]))
+    saved[3].start()
+    saved[4].start()
 
     keys.close(False)
 
@@ -949,9 +972,8 @@
     for n in range(2):
         own_piece(n).wait()
     pl.when(c == x)(lambda: own_down().wait())
-    keep.wait()
-    keep_o.wait()
-    keep_k.wait()
+    for copy in [keep, keep_o, keep_k] + saved:
+        copy.wait()
 
 
 def run_front(*operands):
@@ -973,8 +995,8 @@
             shape((2, 1, LANES), F32),
             shape((8, 128), F32),
         ),
-        in_specs=[VMEM, smem] + [VMEM] * 5 + [ANY] * 5,
-        out_specs=(ANY,) * 5 + (VMEM,) * 7,
+        in_specs=[smem] + [VMEM] * 4 + [ANY] * 7,
+        out_specs=(ANY,) * 10 + (VMEM,) * 2,
         scratch_shapes=[
             pltpu.VMEM((32, 48, WIDE), BF),
             pltpu.VMEM((32, 48, 1536), BF),
@@ -983,6 +1005,16 @@
             pltpu.VMEM((2, 1, LANES), F32),
             pltpu.VMEM((2, 1, LANES), F32),
             pltpu.VMEM((2, 128, LANES), F32),
+            pltpu.VMEM((128, 1536), BF),
+            pltpu.VMEM((8, 24, 1536), BF),
+            pltpu.VMEM((128, 128), F32),
+            pltpu.VMEM((128, 128), F32),
+            pltpu.VMEM((128, 1536), BF),
+            pltpu.VMEM((2, LANES, 128), BF),
+            pltpu.VMEM((128, 1536), F32),
+            pltpu.VMEM((128, 1536), F32),
+            pltpu.VMEM((128, 1536), BF),
+            DMA((5,)),
             DMA((7,)),
             DMA((2, 4, 10)),
             DMA((2, 32, 2)),
@@ -995,7 +1027,7 @@
             DMA((16,)),
             DMA((16,)),
         ],
-        compiler_params=params(1, 48),
+        compiler_params=params(1, 62),
         name="front",
     )(*operands)
 
@@ -1009,24 +1041,31 @@
 
 
 def experts_kernel(
-    n2, h, teacher, routes, gates, valid, count, win, wout,
-    final, err, dn2, dy_out, dwin_out, dwout_out,
-    nall, dyall, pairs, zg, dpairs, part, rc, ry, rz, acc, errs, tables, gate,
+    routes, gates, valid, count, n2, h_in, teacher_in, win, wout,
+    err, final_out, dn2_out, dy_out, dwin_out, dwout_out,
+    h, teacher, final, dy, nall, dyall, pairs, zg, dpairs, part, rc, ry, rz, acc, errs, tables, gate,
     wfull, slab, wdown, dwin, dwin_in, dwout, dwout_in,
-    own_sem, gsend, grecv, csend, crecv, ysend, yrecv, zsend, zrecv, esend, erecv,
+    load_sem, own_sem, gsend, grecv, csend, crecv, ysend, yrecv, zsend, zrecv, esend, erecv,
     tsend, trecv, xsend, xrecv,
 ):
     me = Place()
     x, y, z, b, c = me.x, me.y, me.z, me.b, me.c
     half = pltpu.make_async_copy(win, wfull.at[x], own_sem.at[0])
     half.start()
+    loads = [
+        pltpu.make_async_copy(n2, nall.at[b], load_sem.at[0]),
+        pltpu.make_async_copy(h_in, h, load_sem.at[1]),
+        pltpu.make_async_copy(teacher_in, teacher, load_sem.at[2]),
+    ]
+    for load in loads:
+        load.start()
     held = pltpu.make_async_copy(wout, slab, own_sem.at[1])
     pl.when(c == x)(held.start)
-    lane = lax.broadcasted_iota(jnp.int32, (128, 128), 1)
-    table = jnp.zeros((128, 128), F32)
+    expert = lax.broadcasted_iota(jnp.int32, (8, 128), 0)
+    table = jnp.zeros((8, 128), F32)
     for k in range(TOP):
-        table = table + jnp.where(routes[:, k : k + 1] == lane, gates[:, k : k + 1], 0.0)
-    tables[b] = table.T[0:8]
+        table = table + jnp.where(routes[k : k + 1, :] == expert, gates[k : k + 1, :], 0.0)
+    tables[b] = table
     greet_all(me)
 
     def rows_of(p):
@@ -1160,9 +1199,8 @@
         part[pl.ds(q * 2, 2)] = out.astype(BF).reshape(2, 128, 1536)
         to_other_core(1, q)
 
-    nall[b] = n2[...]
-    held_wait = held.wait
-    pl.when(c == x)(held_wait)
+    loads[0].wait()
+    pl.when(c == x)(held.wait)
 
     def tell_gates(k, carry):
         to = (b + k) % 16
@@ -1174,7 +1212,7 @@
             pl.when((j == 0) & (c == x))(lambda: over_down().start())
             for k in range(4):
                 pl.when(j == k)(over_weights(k).start)
-        else:
+        elif p == 1:
 
             @pl.when(j == 0)
             def _():
@@ -1231,12 +1269,20 @@
     close_sum(0)
 
     keep = as_column(valid[...].astype(F32))
+    loads[1].wait()
+    loads[2].wait()
     done = h[...] + acc[...]
     final[...] = done.astype(BF)
     diff = done - teacher[...].astype(F32)
     scaled = (keep * (SPAN / count[0:1, 0:1])) * diff
-    dy_out[...] = scaled
+    dy[...] = scaled
     dyall[b] = scaled.astype(BF)
+    saved = [
+        pltpu.make_async_copy(final, final_out, load_sem.at[0]),
+        pltpu.make_async_copy(dy, dy_out, load_sem.at[1]),
+    ]
+    for copy in saved:
+        copy.start()
     kept = jnp.sum(keep * diff * diff)
     me_index = x * 16 + b
     errs[me_index] = jnp.zeros((8, 128), F32) + kept
@@ -1255,7 +1301,7 @@
                 from_core(dyall, 1, zz, y)
                 backward(zz * 2 + y)
 
-        else:
+        elif p == CUTS - 1:
 
             @pl.when(j == 0)
             def _():
@@ -1322,7 +1368,8 @@
         over_weights(k).wait_send()
     pl.when(c == x)(lambda: over_down().wait_send())
     lax.fori_loop(0, 4, sums, 0)
-    dn2[...] = acc[...]
+    saved.append(pltpu.make_async_copy(acc, dn2_out, load_sem.at[2]))
+    saved[2].start()
     close_sum(1)
 
     def hear(k, carry):
@@ -1355,7 +1402,8 @@
         copy.wait()
 
     pl.when(c != x)(lambda: over_out().wait_send())
-    out.wait()
+    for copy in saved + [out]:
+        copy.wait()
 
 
 def run_experts(*operands):
@@ -1365,16 +1413,20 @@
     return pl.pallas_call(
         experts_kernel,
         out_shape=(
+            shape((8, 128), F32),
             shape(wide, BF),
-            shape((8, 128), F32),
             shape(wide, F32),
             shape(wide, F32),
             shape((768, 768), BF),
             shape((16, 48, 768), BF),
         ),
-        in_specs=[VMEM] * 7 + [ANY] * 2,
-        out_specs=(VMEM,) * 4 + (ANY,) * 2,
+        in_specs=[VMEM] * 4 + [ANY] * 5,
+        out_specs=(VMEM,) + (ANY,) * 5,
         scratch_shapes=[
+            pltpu.VMEM(wide, F32),
+            pltpu.VMEM(wide, BF),
+            pltpu.VMEM(wide, BF),
+            pltpu.VMEM(wide, F32),
             pltpu.VMEM(shard, BF),
             pltpu.VMEM(shard, BF),
             pltpu.VMEM((8, 256, 768), F32),
@@ -1395,6 +1447,7 @@
             pltpu.VMEM((768, 768), BF),
             pltpu.VMEM((16, 48, 768), F32),
             pltpu.VMEM((16, 48, 768), BF),
+            DMA((3,)),
             DMA((2,)),
             DMA((2, 4, CUTS, 5)),
             DMA((2, 16, CUTS)),
@@ -1425,13 +1478,18 @@
     )
 
 
+Q_PIECES = ((0, 768), (768, 768))
+LAST = (1536, 640)
+
+
 def back_kernel(
-    states, h, n1, qs, o, lse, dn2, dy, doc, freq, dwin, dwout, gq, go, kv_in,
-    gx, gqw, gkw, gvw, gnorm, gout, gup, gdown,
-    wq, wo, kv, pk, dos, delta, dh, dq, dkv, dqkv, gqkv, *rest,
+    doc, freq, states_in, h_in, n1_in, qs_in, o_in, lse_in, dn2_in, dy_in, dwin, dwout, gq, go, kv_in,
+    gx_out, gqw, gkw, gvw, gnorm, gout_out, gup, gdown,
+    states, h, n1, qs, o, lse, dn2, dy, gx, gout, gkv,
+    wq, wo, kv, pk, pw, dos, delta, dh, dq, dkv, dqkv, gqkv, *rest,
 ):
-    sums = [(rest[i * 11 : i * 11 + 6], rest[i * 11 + 6 : i * 11 + 11]) for i in range(4)]
-    own_sem, asend, arecv, osend, orecv = rest[44:]
+    sums = [(rest[i * 11 : i * 11 + 6], rest[i * 11 + 6 : i * 11 + 11]) for i in range(5)]
+    load_sem, own_sem, asend, arecv, osend, orecv = rest[55:]
     me = Place()
     x, y, z, b, c = me.x, me.y, me.z, me.b, me.c
     loads = [
@@ -1439,7 +1497,16 @@
         pltpu.make_async_copy(kv_in, kv, own_sem.at[1]),
         pltpu.make_async_copy(gq, wq, own_sem.at[2]),
     ]
-    for load in loads:
+    small = [
+        pltpu.make_async_copy(src, dst, load_sem.at[i])
+        for i, (src, dst) in enumerate(
+            (
+                (h_in, h), (dn2_in, dn2), (dy_in, dy), (o_in, o), (qs_in, qs), (lse_in, lse),
+                (n1_in, n1), (states_in, states),
+            )
+        )
+    ]
+    for load in [loads[2]] + small[:3] + loads[:2] + small[3:]:
         load.start()
     greet_all(me)
 
@@ -1472,6 +1539,8 @@
         own_piece(n).start()
     pl.when(c == x)(lambda: own_down().start())
     loads[2].wait()
+    for load in small[:3]:
+        load.wait()
     gains = wq[:, :, pl.ds(QKV, 128)].reshape(1536, 128).astype(F32).T
     res_grad, gain_two = norm_back(h[...], gains[1:2], dn2[...])
     dh[...] = dy[...] + res_grad
@@ -1480,6 +1549,7 @@
     do = lax.dot_general(
         da, wo[...].reshape(1536, 1536), NT, preferred_element_type=F32
     ).astype(BF)
+    small[3].wait()
     low = o[...].astype(BF)
     for i in range(4):
         part = lax.dot_general(low[:, i * 384 : i * 384 + 384], da, TN, preferred_element_type=F32)
@@ -1503,6 +1573,8 @@
     dq[...] = jnp.zeros_like(dq)
     bounds = query_bounds(me, doc)
     loads[1].wait()
+    for load in small[4:6]:
+        load.wait()
 
     def block(n):
         ok = allowed_keys(n * 256, bounds)
@@ -1521,7 +1593,7 @@
 
     def turn(j, carry):
         out_sum.turn(j)
-        lax.fori_loop(1 + j * 3, jnp.minimum(4 + j * 3, 16), deal, 0)
+        lax.fori_loop(1 + j * 4, jnp.minimum(5 + j * 4, 16), deal, 0)
 
         @pl.when(key_sum.valid(j))
         def _():
@@ -1543,46 +1615,71 @@
         key_sum.turn(j)
         return carry
 
-    lax.fori_loop(0, 6, turn, 0)
+    lax.fori_loop(0, 4, turn, 0)
 
     cos, sin = rotary_tables(me, doc, freq)
+    for load in small[6:]:
+        load.wait()
     for i in range(QUERY_HEADS):
         r = (i % GROUP) * 128
         head = dq[i // GROUP, :, r : r + 128].T * SCALE
         dqkv[:, i * 128 : i * 128 + 128] = turned(head, cos, -sin).astype(BF)
-    for i in range(2):
-        dqkv[:, 1536 + i * 128 : 1664 + i * 128] = turned(dkv[:, i * 128 : i * 128 + 128], cos, -sin).astype(BF)
-        dqkv[:, 1792 + i * 128 : 1920 + i * 128] = dkv[:, 256 + i * 128 : 384 + i * 128].astype(BF)
-    dn1 = lax.dot_general(
-        dqkv[...], wq[:, :, pl.ds(0, QKV)].reshape(1536, QKV), NT, preferred_element_type=F32
-    )
-    in_grad, gain_one = norm_back(states[...].astype(F32), gains[0:1], dn1)
-    gx[...] = dh[...] + in_grad
-    rows = lax.broadcasted_iota(jnp.int32, (128, 1536), 0)
-    tail = jnp.where(rows == 0, gain_one, jnp.where(rows == 1, gain_two, 0.0)).T
-    wq[:, :, pl.ds(QKV, 128)] = tail.astype(BF).reshape(32, 48, 128)
-    for i in range(4):
-        part = lax.dot_general(
-            n1[:, i * 384 : i * 384 + 384], dqkv[...], TN, preferred_element_type=F32
-        )
-        wq[i * 8 : i * 8 + 8, :, 0:QKV] = part.astype(BF).reshape(8, 48, QKV)
-    proj = [Sum(me, wq, by_weight, gqkv, *sums[2 + i], PIECES[i]) for i in range(2)]
+
+    def weight_grad(start, width):
+        for i in range(4):
+            part = lax.dot_general(
+                n1[:, i * 384 : i * 384 + 384], dqkv[:, start : start + width], TN, preferred_element_type=F32
+            )
+            pw[i * 8 : i * 8 + 8, :, start : start + width] = part.astype(BF).reshape(8, 48, width)
+
+    weight_grad(0, 1536)
+    proj = [Sum(me, pw, by_weight, gqkv, *sums[2 + i], Q_PIECES[i]) for i in range(2)]
+    rest_sum = Sum(me, pw, by_weight, gqkv, *sums[4], LAST)
     for piece in proj:
         lead_all(piece)
 
     def last_turn(j, carry):
         for piece in proj:
             piece.turn(j)
+        out_sum.turn(j + 4)
+        pl.when(j < 2)(lambda: key_sum.turn(j + 4))
+
+        @pl.when(j == 1)
+        def _():
+            for i in range(2):
+                part = dkv[:, i * 128 : i * 128 + 128]
+                dqkv[:, 1536 + i * 128 : 1664 + i * 128] = turned(part, cos, -sin).astype(BF)
+            dqkv[:, 1792:2048] = dkv[:, 256:512].astype(BF)
+            weight_grad(1536, 512)
+            dn1 = lax.dot_general(
+                dqkv[...], wq[:, :, pl.ds(0, QKV)].reshape(1536, QKV), NT, preferred_element_type=F32
+            )
+            in_grad, gain_one = norm_back(states[...].astype(F32), gains[0:1], dn1)
+            rows = lax.broadcasted_iota(jnp.int32, (128, 1536), 0)
+            tail = jnp.where(rows == 0, gain_one, jnp.where(rows == 1, gain_two, 0.0)).T
+            pw[:, :, pl.ds(QKV, 128)] = tail.astype(BF).reshape(32, 48, 128)
+            lead_all(rest_sum)
+            gx[...] = dh[...] + in_grad
+
+        rest_sum.turn(j - 2)
         return carry
 
-    lax.fori_loop(0, 6, last_turn, 0)
-    gqw[...] = gqkv[:, 0:1536]
-    gkw[...] = gqkv[:, 1536:1792]
-    gvw[...] = gqkv[:, 1792:2048]
+    lax.fori_loop(0, 8, last_turn, 0)
+    gkv[...] = gqkv[:, 1536:2048]
+    stores = [
+        pltpu.make_async_copy(gx, gx_out, load_sem.at[0]),
+        pltpu.make_async_copy(gout, gout_out, load_sem.at[1]),
+        pltpu.make_async_copy(gqkv.at[:, pl.ds(0, 1536)], gqw, load_sem.at[2]),
+        pltpu.make_async_copy(gkv.at[:, pl.ds(0, 256)], gkw, load_sem.at[3]),
+        pltpu.make_async_copy(gkv.at[:, pl.ds(256, 256)], gvw, load_sem.at[4]),
+    ]
+    for store in stores:
+        store.start()
     gnorm[0:1, :] = as_row(gqkv[:, 2048:2049])
     gnorm[1:2, :] = as_row(gqkv[:, 2049:2050])
     out_sum.close()
     key_sum.close()
+    rest_sum.close()
     for piece in proj:
         piece.close()
 
@@ -1600,6 +1697,8 @@
     for n in range(2):
         own_piece(n).wait()
     pl.when(c == x)(lambda: own_down().wait())
+    for store in stores:
+        store.wait()
 
 
 def run_back(*operands):
@@ -1617,13 +1716,25 @@
             shape((8, 48, 1536), BF),
             shape((8, 48, 768), BF),
         ),
-        in_specs=[VMEM] * 8 + [smem, VMEM] + [ANY] * 5,
-        out_specs=(VMEM,) * 6 + (ANY,) * 2,
+        in_specs=[smem, VMEM] + [ANY] * 13,
+        out_specs=(ANY,) * 4 + (VMEM,) + (ANY,) * 3,
         scratch_shapes=[
+            pltpu.VMEM((128, 1536), BF),
+            pltpu.VMEM((128, 1536), F32),
+            pltpu.VMEM((128, 1536), BF),
+            pltpu.VMEM((2, LANES, 128), BF),
+            pltpu.VMEM((128, 1536), F32),
+            pltpu.VMEM((2, 1, LANES), F32),
+            pltpu.VMEM((128, 1536), F32),
+            pltpu.VMEM((128, 1536), F32),
+            pltpu.VMEM((128, 1536), F32),
+            pltpu.VMEM((48, 1536), F32),
+            pltpu.VMEM((48, 512), F32),
             pltpu.VMEM((32, 48, WIDE), BF),
             pltpu.VMEM((32, 48, 1536), BF),
             pltpu.VMEM((32, 128, 512), BF),
             pltpu.VMEM((32, 128, 512), BF),
+            pltpu.VMEM((32, 48, WIDE), BF),
             pltpu.VMEM((2, LANES, 128), BF),
             pltpu.VMEM((2, 1, LANES), F32),
             pltpu.VMEM((128, 1536), F32),
@@ -1634,11 +1745,85 @@
         ]
         + Sum.room(48, 1536)
         + Sum.room(128, 512)
-        + Sum.room(48, PIECES[0][1])
-        + Sum.room(48, PIECES[1][1])
-        + [DMA((6,)), DMA((16, 2)), DMA((16, 2)), DMA((16,)), DMA((8,))],
-        compiler_params=params(3, 61),
+        + Sum.room(48, 768)
+        + Sum.room(48, 768)
+        + Sum.room(48, LAST[1])
+        + [DMA((8,)), DMA((6,)), DMA((16, 2)), DMA((16, 2)), DMA((16,)), DMA((8,))],
+        compiler_params=params(3, 62),
         name="back",
+    )(*operands)
+
+
+def finish_kernel(
+    err, gnorm, final, gx, gqw, gkw, gvw, gout, gup, gdown,
+    loss, one, two, final_out, gx_out, gqw_out, gkw_out, gvw_out, gout_out, gup_out, gdown_out,
+    low_up, low_down, wide_up, wide_down, *rest,
+):
+    rooms, sem, out_sem = rest[:6], rest[6], rest[7]
+    whole = ((gup, low_up), (gdown, low_down), *zip((final, gx, gqw, gkw, gvw, gout), rooms))
+    copies = [pltpu.make_async_copy(src, dst, sem.at[i]) for i, (src, dst) in enumerate(whole)]
+    for copy in copies:
+        copy.start()
+    loss[...] = err[0:1, 0:1]
+    one[...] = gnorm[0:1, :]
+    two[...] = gnorm[1:2, :]
+    outs = (final_out, gx_out, gqw_out, gkw_out, gvw_out, gout_out)
+    last = []
+    for i in range(6):
+        copies[2 + i].wait()
+        last.append(pltpu.make_async_copy(rooms[i], outs[i], out_sem.at[i]))
+        last[i].start()
+    copies[0].wait()
+    wide_up[...] = low_up[...].astype(F32)
+    last.append(pltpu.make_async_copy(wide_up, gup_out, out_sem.at[6]))
+    last[6].start()
+    copies[1].wait()
+    for e in range(E):
+        wide = low_down[e].astype(F32)
+        wide_down[e, :, :768] = wide[:24]
+        wide_down[e, :, 768:] = wide[24:]
+    last.append(pltpu.make_async_copy(wide_down, gdown_out, out_sem.at[7]))
+    last[7].start()
+    for copy in last:
+        copy.wait()
+
+
+def run_finish(*operands):
+    shape = jax.ShapeDtypeStruct
+    up, down = (8, 48, 1536), (8, 24, 1536)
+    return pl.pallas_call(
+        finish_kernel,
+        out_shape=(
+            shape((1, 1), F32),
+            shape((1, 48), F32),
+            shape((1, 48), F32),
+            shape((128, 1536), BF),
+            shape((128, 1536), F32),
+            shape((48, 1536), F32),
+            shape((48, 256), F32),
+            shape((48, 256), F32),
+            shape((48, 1536), F32),
+            shape(up, F32),
+            shape(down, F32),
+        ),
+        in_specs=[VMEM] * 2 + [ANY] * 8,
+        out_specs=(VMEM,) * 3 + (ANY,) * 8,
+        scratch_shapes=[
+            pltpu.VMEM(up, BF),
+            pltpu.VMEM((8, 48, 768), BF),
+            pltpu.VMEM(up, F32),
+            pltpu.VMEM(down, F32),
+            pltpu.VMEM((128, 1536), BF),
+            pltpu.VMEM((128, 1536), F32),
+            pltpu.VMEM((48, 1536), F32),
+            pltpu.VMEM((48, 256), F32),
+            pltpu.VMEM((48, 256), F32),
+            pltpu.VMEM((48, 1536), F32),
+            DMA((8,)),
+            DMA((8,)),
+        ],
+        compiler_params=pltpu.CompilerParams(vmem_limit_bytes=60 << 20),
+        name="finish",
     )(*operands)
 
 
@@ -1654,29 +1839,32 @@
     rows = states.reshape(tokens, width)
     kept = valid.reshape(1, tokens)
     gq, go, kv, win, wout, h, n2, n1, qs, o, lse, count = run_front(
-        rows, doc_starts, freq, norm_one.reshape(1, -1), norm_two.reshape(1, -1), kept, expert_out,
+        doc_starts, freq, norm_one.reshape(1, -1), norm_two.reshape(1, -1), kept, rows, expert_out,
         w_query, key_weight, value_weight, w_output, expert_in,
     )
-    final, error, dn2, dy, dwin, dwout = run_experts(
-        n2, h, teacher.reshape(tokens, width), routes.reshape(tokens, TOP), gates.reshape(tokens, TOP),
-        kept, count, win, wout,
+    error, final, dn2, dy, dwin, dwout = run_experts(
+        routes.reshape(tokens, TOP).T, gates.reshape(tokens, TOP).T, kept, count,
+        n2, h, teacher.reshape(tokens, width), win, wout,
     )
     gx, gqw, gkw, gvw, gnorm, gout, gup, gdown = run_back(
-        rows, h, n1, qs, o, lse, dn2, dy, doc_starts, freq, dwin.reshape(16, 48, 768), dwout, gq, go, kv
+        doc_starts, freq, rows, h, n1, qs, o, lse, dn2, dy, dwin.reshape(16, 48, 768), dwout, gq, go, kv
+    )
+    loss, one, two, final, gx, gqw, gkw, gvw, gout, gup, gdown = run_finish(
+        error, gnorm, final, gx, gqw, gkw, gvw, gout, gup, gdown
     )
     shape = states.shape
     return (
         final.reshape(shape),
-        error[0, 0],
+        loss.reshape(()),
         gx.reshape(shape),
-        gnorm[0],
+        one.reshape(-1),
         gqw,
         gkw,
         gvw,
         gout,
-        gnorm[1],
-        gup.astype(F32),
-        gdown.astype(F32).reshape(E, 2, 24, 768).transpose(0, 2, 1, 3).reshape(E, 24, 1536),
+        two.reshape(-1),
+        gup,
+        gdown,
     )
 
 

time: 440 us -> 409 us (0.930)
  local copies, waits for them, and re-layouts: 24.2 us -> 0 us
    unnamed x64 -> x0, local copies, waits for them, and re-layouts: 20.7 us -> none
    pallas_call x1, Pallas kernels: 112 us -> 107 us  [run_back(): pl.pallas_call(back_kernel, out_shape=(shape((128, 1536), F32), shape((48...]
    pallas_call x1 -> x2, Pallas kernels: 184 us -> 188 us  [the longest x1 183 us: run_experts(): pl.pallas_call(experts_kernel, out_shape=(shape((8, 128), F32), shape(wid...]
where the time goes in v4:
time: 409 us
  Pallas kernels  408 us (100%)
    pallas_call x1, Pallas kernels, run_experts(): pl.pallas_call(experts_kernel, out_shape=(shape((8, 128), F32), shape(wid...  183 us
    pallas_call x1, Pallas kernels, run_front(): pl.pallas_call(front_kernel, out_shape=(shape((32, 48, WIDE), BF), shape(...  113 us
    pallas_call x1, Pallas kernels, run_back(): pl.pallas_call(back_kernel, out_shape=(shape((128, 1536), F32), shape((48...  107 us

profile of v4, /device:TPU:0, one launch (start us, length us, event | category | flops | bytes accessed | tf_op | source)
XLA Modules:
  0.0 408.9 jit_solution(4522393866438802745)
XLA Ops:
  0.6 112.9 %front.1 = (bf16[32,48,2176]{2,1,0:T(8,128)(2,1)}, bf16[32,48,1536]{2,1,0:T(8,128)(2,1)}, bf16[32,128,512]{2,1,0:T(8,128)(2,1)}, bf16[16,48,768]{2,1,0:T(8,128)(...) custom-call(s32[3]{0:T(128)} %doc.3, ...), custom_call_target="tpu_custom_call" | custom-call | tf_op jit(solution)/shard_map/front/pallas_call | solution.py:982
  113.6 182.6 %experts.1 = (f32[8,128]{1,0:T(8,128)}, bf16[128,1536]{1,0:T(8,128)(2,1)}, f32[128,1536]{1,0:T(8,128)}, f32[128,1536]{1,0:T(8,128)}, bf16[768,768]{1,0:T(8,128)(2,1)}, /*index=5*/bf16[16,48,768]{2,1,0:T(8,128)(2,1)}) custom-call(s32[4,128]{1,0:T(4,128)} %bitcast.21, f32[4,128]{1,0:T(4,128)} %bitcast.22, s32[1,128]{1,0:T(1,128)} %bitcast.24, ...), custom_call_target="tpu_custom_call" | custom-call | tf_op jit(solution)/shard_map/experts/pallas_call | solution.py:1413
  296.2 107.1 %back.1 = (f32[128,1536]{1,0:T(8,128)}, f32[48,1536]{1,0:T(8,128)}, f32[48,256]{1,0:T(8,128)}, f32[48,256]{1,0:T(8,128)}, f32[2,48]{1,0:T(2,128)}, /*index=5*/f3...) custom-call(s32[3]{0:T(128)} %doc.3, f32[1,128]{1,0:T(1,128)} %constant.2.clone.freq, ...), custom_call_target="tpu_custom_call" | custom-call | tf_op jit(solution)/shard_map/back/pallas_call | solution.py:1707
  403.3 5.4 %finish.1 = (f32[1,1]{1,0:T(1,128)}, f32[1,48]{1,0:T(1,128)}, f32[1,48]{1,0:T(1,128)}, bf16[128,1536]{1,0:T(8,128)(2,1)}, f32[128,1536]{1,0:T(8,128)}, /*index=5...) custom-call(f32[8,128]{1,0:T(8,128)} %get-tuple-element.53.err, ...), custom_call_target="tpu_custom_call" | custom-call | tf_op jit(solution)/shard_map/finish/pallas_call | solution.py:1794

commit v5 on v4

--- a/solution.py
+++ b/solution.py
@@ -738,8 +738,9 @@
 
 def begin_of(place, doc):
     begin = jnp.zeros_like(place)
-    for i in range(doc.shape[0]):
-        begin = jnp.where(place >= doc[i], jnp.maximum(begin, doc[i]), begin)
+    for i in range(doc.shape[1]):
+        start = doc[0:1, i : i + 1]
+        begin = jnp.where(place >= start, jnp.maximum(begin, start), begin)
     return begin
 
 
@@ -780,9 +781,9 @@
 
 
 def front_kernel(
-    doc, freq, norm_one, norm_two, valid, states, down_in, wq, wk, wv, wo, up,
-    gq_out, go_out, kv_out, win, wout, h_out, n2_out, n1_out, qs_out, o_out, lse, count,
-    gq, go, kv, down, top, total, acc, low_rows, down_raw, cos, sin, n1, qs, o, h, n2,
+    doc_in, freq_in, one_in, two_in, valid_in, states, down_in, wq, wk, wv, wo, up,
+    gq_out, go_out, kv_out, win, wout, h_out, n2_out, n1_out, qs_out, o_out, lse_out, count_out, gains_out,
+    doc, freq, norm_one, norm_two, valid, lse, count, gains_row, gq, go, kv, down, top, total, acc, low_rows, down_raw, cos, sin, n1, qs, o, h, n2,
     load_sem, own_sem, qsend, qrecv, gsend, grecv, ksend, krecv, asend, arecv, osend, orecv,
 ):
     me = Place()
@@ -794,12 +795,15 @@
         pltpu.make_async_copy(wv, gq.at[here, :, pl.ds(1792, 256)], own_sem.at[2]),
         pltpu.make_async_copy(wo, go.at[here], own_sem.at[3]),
     ]
-    loads = [
-        pltpu.make_async_copy(down_in, down_raw, load_sem.at[0]),
-        pltpu.make_async_copy(states, low_rows, load_sem.at[1]),
-    ]
-    for copy in mine + loads:
+    pairs = (
+        (down_in, down_raw), (states, low_rows), (doc_in, doc), (freq_in, freq),
+        (one_in, norm_one), (two_in, norm_two), (valid_in, valid),
+    )
+    loads = [pltpu.make_async_copy(src, dst, load_sem.at[i]) for i, (src, dst) in enumerate(pairs)]
+    for copy in loads[4:] + mine + loads[:4]:
         copy.start()
+    for load in loads[4:]:
+        load.wait()
 
     lane = lax.broadcasted_iota(jnp.int32, (48, 128), 1)
     kept = jnp.sum(valid[...].astype(F32))
@@ -809,10 +813,6 @@
         jnp.where(lane == 1, as_column(norm_two[...].astype(F32)), jnp.where(lane == 2, kept, 0.0)),
     )
     gq[here, :, pl.ds(QKV, 128)] = extra.astype(BF)
-    loads[0].wait()
-    for e in range(E):
-        wide = down_raw[e].astype(F32)
-        down[e] = jnp.concatenate([wide[:, :768], wide[:, 768:]], axis=0).astype(BF)
     greet_all(me)
     for copy in mine:
         copy.wait()
@@ -849,12 +849,17 @@
     def first_turn(j, carry):
         for piece in weights:
             piece.turn(j)
-        lax.fori_loop(1 + j * 3, jnp.minimum(4 + j * 3, 16), deal, 0)
 
         @pl.when(j == 0)
         def _():
+            for load in loads[:4]:
+                load.wait()
+            for e in range(E):
+                wide = down_raw[e].astype(F32)
+                down[e] = jnp.concatenate([wide[:, :768], wide[:, 768:]], axis=0).astype(BF)
             cos[...], sin[...] = rotary_tables(me, doc, freq)
 
+        lax.fori_loop(1 + j * 3, jnp.minimum(4 + j * 3, 16), deal, 0)
         return carry
 
     lax.fori_loop(0, 6, first_turn, 0)
@@ -862,7 +867,6 @@
         own_piece(n).start()
     pl.when(c == x)(lambda: own_down().start())
     bounds = query_bounds(me, doc)
-    loads[1].wait()
     rows = low_rows[...].astype(F32)
     level = rows * lax.rsqrt(jnp.mean(rows * rows, axis=-1, keepdims=True) + 1e-06)
     for piece in weights:
@@ -886,7 +890,10 @@
         r = (i % GROUP) * 128
         qs[i // GROUP, r : r + 128] = turned(query[:, i * 128 : i * 128 + 128], *turns).astype(BF)
     count[...] = jnp.zeros((8, 128), F32) + jnp.sum(gains[2:3]) / 48.0
+    gains_row[...] = gains[0:8]
     saved = [
+        pltpu.make_async_copy(count, count_out, load_sem.at[5]),
+        pltpu.make_async_copy(gains_row, gains_out, load_sem.at[6]),
         pltpu.make_async_copy(n1, n1_out, load_sem.at[0]),
         pltpu.make_async_copy(qs, qs_out, load_sem.at[1]),
     ]
@@ -942,8 +949,9 @@
         for r in range(GROUP):
             col = (i * GROUP + r) * 128
             o[:, col : col + 128] = done[:, r * 128 : r * 128 + 128].T
-    saved.append(pltpu.make_async_copy(o, o_out, load_sem.at[2]))
-    saved[2].start()
+    more = [pltpu.make_async_copy(o, o_out, load_sem.at[2]), pltpu.make_async_copy(lse, lse_out, load_sem.at[7])]
+    for copy in more:
+        copy.start()
     res = low_rows[...].astype(F32) + jnp.dot(
         o[...].astype(BF), go[...].reshape(1536, 1536), preferred_element_type=F32
     )
@@ -951,10 +959,10 @@
     n2[...] = (
         res * lax.rsqrt(jnp.mean(res * res, axis=-1, keepdims=True) + 1e-06) * gains[1:2]
     ).astype(BF)
-    saved.append(pltpu.make_async_copy(h, h_out, load_sem.at[3]))
-    saved.append(pltpu.make_async_copy(n2, n2_out, load_sem.at[4]))
-    saved[3].start()
-    saved[4].start()
+    more.append(pltpu.make_async_copy(h, h_out, load_sem.at[3]))
+    more.append(pltpu.make_async_copy(n2, n2_out, load_sem.at[4]))
+    more[2].start()
+    more[3].start()
 
     keys.close(False)
 
@@ -972,13 +980,12 @@
     for n in range(2):
         own_piece(n).wait()
     pl.when(c == x)(lambda: own_down().wait())
-    for copy in [keep, keep_o, keep_k] + saved:
+    for copy in [keep, keep_o, keep_k] + saved + more:
         copy.wait()
 
 
 def run_front(*operands):
     shape = jax.ShapeDtypeStruct
-    smem = pl.BlockSpec(memory_space=pltpu.SMEM)
     return pl.pallas_call(
         front_kernel,
         out_shape=(
@@ -994,10 +1001,19 @@
             shape((128, 1536), F32),
             shape((2, 1, LANES), F32),
             shape((8, 128), F32),
+            shape((8, 1536), F32),
         ),
-        in_specs=[smem] + [VMEM] * 4 + [ANY] * 7,
-        out_specs=(ANY,) * 10 + (VMEM,) * 2,
+        in_specs=[ANY] * 12,
+        out_specs=(ANY,) * 13,
         scratch_shapes=[
+            pltpu.VMEM(operands[0].shape, jnp.int32),
+            pltpu.VMEM((1, 128), F32),
+            pltpu.VMEM((1, 48), BF),
+            pltpu.VMEM((1, 48), BF),
+            pltpu.VMEM((1, 128), jnp.int32),
+            pltpu.VMEM((2, 1, LANES), F32),
+            pltpu.VMEM((8, 128), F32),
+            pltpu.VMEM((8, 1536), F32),
             pltpu.VMEM((32, 48, WIDE), BF),
             pltpu.VMEM((32, 48, 1536), BF),
             pltpu.VMEM((32, 128, 512), BF),
@@ -1014,7 +1030,7 @@
             pltpu.VMEM((128, 1536), F32),
             pltpu.VMEM((128, 1536), F32),
             pltpu.VMEM((128, 1536), BF),
-            DMA((5,)),
+            DMA((8,)),
             DMA((7,)),
             DMA((2, 4, 10)),
             DMA((2, 32, 2)),
@@ -1041,9 +1057,9 @@
 
 
 def experts_kernel(
-    routes, gates, valid, count, n2, h_in, teacher_in, win, wout,
-    err, final_out, dn2_out, dy_out, dwin_out, dwout_out,
-    h, teacher, final, dy, nall, dyall, pairs, zg, dpairs, part, rc, ry, rz, acc, errs, tables, gate,
+    routes_in, gates_in, valid_in, count_in, n2, h_in, teacher_in, win, wout,
+    err_out, final_out, dn2_out, dy_out, dwin_out, dwout_out,
+    routes, gates, valid, count, err, h, teacher, final, dy, nall, dyall, pairs, zg, dpairs, part, rc, ry, rz, acc, errs, tables, gate,
     wfull, slab, wdown, dwin, dwin_in, dwout, dwout_in,
     load_sem, own_sem, gsend, grecv, csend, crecv, ysend, yrecv, zsend, zrecv, esend, erecv,
     tsend, trecv, xsend, xrecv,
@@ -1056,16 +1072,15 @@
         pltpu.make_async_copy(n2, nall.at[b], load_sem.at[0]),
         pltpu.make_async_copy(h_in, h, load_sem.at[1]),
         pltpu.make_async_copy(teacher_in, teacher, load_sem.at[2]),
+        pltpu.make_async_copy(routes_in, routes, load_sem.at[3]),
+        pltpu.make_async_copy(gates_in, gates, load_sem.at[4]),
+        pltpu.make_async_copy(valid_in, valid, load_sem.at[5]),
+        pltpu.make_async_copy(count_in, count, load_sem.at[6]),
     ]
     for load in loads:
         load.start()
     held = pltpu.make_async_copy(wout, slab, own_sem.at[1])
     pl.when(c == x)(held.start)
-    expert = lax.broadcasted_iota(jnp.int32, (8, 128), 0)
-    table = jnp.zeros((8, 128), F32)
-    for k in range(TOP):
-        table = table + jnp.where(routes[k : k + 1, :] == expert, gates[k : k + 1, :], 0.0)
-    tables[b] = table
     greet_all(me)
 
     def rows_of(p):
@@ -1216,6 +1231,13 @@
 
             @pl.when(j == 0)
             def _():
+                for load in loads[3:]:
+                    load.wait()
+                expert = lax.broadcasted_iota(jnp.int32, (8, 128), 0)
+                table = jnp.zeros((8, 128), F32)
+                for k in range(TOP):
+                    table = table + jnp.where(routes[k : k + 1, :] == expert, gates[k : k + 1, :], 0.0)
+                tables[b] = table
                 lax.fori_loop(1, 16, tell_gates, 0)
 
     gather(nall, 0, with_tokens)
@@ -1266,7 +1288,6 @@
         return carry
 
     lax.fori_loop(0, 5, outputs, 0)
-    close_sum(0)
 
     keep = as_column(valid[...].astype(F32))
     loads[1].wait()
@@ -1280,8 +1301,10 @@
     saved = [
         pltpu.make_async_copy(final, final_out, load_sem.at[0]),
         pltpu.make_async_copy(dy, dy_out, load_sem.at[1]),
+        pltpu.make_async_copy(acc, dn2_out, load_sem.at[2]),
+        pltpu.make_async_copy(err, err_out, load_sem.at[3]),
     ]
-    for copy in saved:
+    for copy in saved[:2]:
         copy.start()
     kept = jnp.sum(keep * diff * diff)
     me_index = x * 16 + b
@@ -1306,6 +1329,7 @@
             @pl.when(j == 0)
             def _():
                 lax.fori_loop(1, 32, tell, 0)
+                close_sum(0)
 
             @pl.when(j > 1)
             def _():
@@ -1368,7 +1392,6 @@
         over_weights(k).wait_send()
     pl.when(c == x)(lambda: over_down().wait_send())
     lax.fori_loop(0, 4, sums, 0)
-    saved.append(pltpu.make_async_copy(acc, dn2_out, load_sem.at[2]))
     saved[2].start()
     close_sum(1)
 
@@ -1383,6 +1406,7 @@
     for s in range(1, 32):
         total = total + errs[s]
     err[...] = total / (1536.0 * count[...])
+    saved[3].start()
 
     for k in range(3):
         over_in(k).wait_send()
@@ -1420,9 +1444,14 @@
             shape((768, 768), BF),
             shape((16, 48, 768), BF),
         ),
-        in_specs=[VMEM] * 4 + [ANY] * 5,
-        out_specs=(VMEM,) + (ANY,) * 5,
+        in_specs=[ANY] * 9,
+        out_specs=(ANY,) * 6,
         scratch_shapes=[
+            pltpu.VMEM((TOP, 128), jnp.int32),
+            pltpu.VMEM((TOP, 128), F32),
+            pltpu.VMEM((1, 128), jnp.int32),
+            pltpu.VMEM((8, 128), F32),
+            pltpu.VMEM((8, 128), F32),
             pltpu.VMEM(wide, F32),
             pltpu.VMEM(wide, BF),
             pltpu.VMEM(wide, BF),
@@ -1447,7 +1476,7 @@
             pltpu.VMEM((768, 768), BF),
             pltpu.VMEM((16, 48, 768), F32),
             pltpu.VMEM((16, 48, 768), BF),
-            DMA((3,)),
+            DMA((7,)),
             DMA((2,)),
             DMA((2, 4, CUTS, 5)),
             DMA((2, 16, CUTS)),
@@ -1483,9 +1512,9 @@
 
 
 def back_kernel(
-    doc, freq, states_in, h_in, n1_in, qs_in, o_in, lse_in, dn2_in, dy_in, dwin, dwout, gq, go, kv_in,
-    gx_out, gqw, gkw, gvw, gnorm, gout_out, gup, gdown,
-    states, h, n1, qs, o, lse, dn2, dy, gx, gout, gkv,
+    doc_in, freq_in, gains_in, states_in, h_in, n1_in, qs_in, o_in, lse_in, dn2_in, dy_in, dwin, dwout, gq, go, kv_in,
+    gx_out, gqw, gkw, gvw, gnorm_out, gout_out, gup, gdown,
+    doc, freq, gains, gnorm, states, h, n1, qs, o, lse, dn2, dy, gx, gout, gkv,
     wq, wo, kv, pk, pw, dos, delta, dh, dq, dkv, dqkv, gqkv, *rest,
 ):
     sums = [(rest[i * 11 : i * 11 + 6], rest[i * 11 + 6 : i * 11 + 11]) for i in range(5)]
@@ -1502,11 +1531,11 @@
         for i, (src, dst) in enumerate(
             (
                 (h_in, h), (dn2_in, dn2), (dy_in, dy), (o_in, o), (qs_in, qs), (lse_in, lse),
-                (n1_in, n1), (states_in, states),
+                (n1_in, n1), (states_in, states), (doc_in, doc), (freq_in, freq), (gains_in, gains),
             )
         )
     ]
-    for load in [loads[2]] + small[:3] + loads[:2] + small[3:]:
+    for load in small[:3] + [small[10], loads[0]] + small[3:10] + [loads[1], loads[2]]:
         load.start()
     greet_all(me)
 
@@ -1538,10 +1567,9 @@
     for n in range(2):
         own_piece(n).start()
     pl.when(c == x)(lambda: own_down().start())
-    loads[2].wait()
-    for load in small[:3]:
+    lax.fori_loop(1, 16, deal, 0)
+    for load in small[:3] + small[8:]:
         load.wait()
-    gains = wq[:, :, pl.ds(QKV, 128)].reshape(1536, 128).astype(F32).T
     res_grad, gain_two = norm_back(h[...], gains[1:2], dn2[...])
     dh[...] = dy[...] + res_grad
     da = dh[...].astype(BF)
@@ -1593,7 +1621,6 @@
 
     def turn(j, carry):
         out_sum.turn(j)
-        lax.fori_loop(1 + j * 4, jnp.minimum(5 + j * 4, 16), deal, 0)
 
         @pl.when(key_sum.valid(j))
         def _():
@@ -1618,7 +1645,7 @@
     lax.fori_loop(0, 4, turn, 0)
 
     cos, sin = rotary_tables(me, doc, freq)
-    for load in small[6:]:
+    for load in small[6:8] + [loads[2]]:
         load.wait()
     for i in range(QUERY_HEADS):
         r = (i % GROUP) * 128
@@ -1675,8 +1702,10 @@
     ]
     for store in stores:
         store.start()
-    gnorm[0:1, :] = as_row(gqkv[:, 2048:2049])
-    gnorm[1:2, :] = as_row(gqkv[:, 2049:2050])
+    gnorm[0:1, 0:48] = as_row(gqkv[:, 2048:2049])
+    gnorm[1:2, 0:48] = as_row(gqkv[:, 2049:2050])
+    stores.append(pltpu.make_async_copy(gnorm, gnorm_out, load_sem.at[5]))
+    stores[5].start()
     out_sum.close()
     key_sum.close()
     rest_sum.close()
@@ -1703,7 +1732,6 @@
 
 def run_back(*operands):
     shape = jax.ShapeDtypeStruct
-    smem = pl.BlockSpec(memory_space=pltpu.SMEM)
     return pl.pallas_call(
         back_kernel,
         out_shape=(
@@ -1711,14 +1739,18 @@
             shape((48, 1536), F32),
             shape((48, 256), F32),
             shape((48, 256), F32),
-            shape((2, 48), F32),
+            shape((8, 128), F32),
             shape((48, 1536), F32),
             shape((8, 48, 1536), BF),
             shape((8, 48, 768), BF),
         ),
-        in_specs=[smem, VMEM] + [ANY] * 13,
-        out_specs=(ANY,) * 4 + (VMEM,) + (ANY,) * 3,
+        in_specs=[ANY] * 16,
+        out_specs=(ANY,) * 8,
         scratch_shapes=[
+            pltpu.VMEM(operands[0].shape, jnp.int32),
+            pltpu.VMEM((1, 128), F32),
+            pltpu.VMEM((8, 1536), F32),
+            pltpu.VMEM((8, 128), F32),
             pltpu.VMEM((128, 1536), BF),
             pltpu.VMEM((128, 1536), F32),
             pltpu.VMEM((128, 1536), BF),
@@ -1748,25 +1780,24 @@
         + Sum.room(48, 768)
         + Sum.room(48, 768)
         + Sum.room(48, LAST[1])
-        + [DMA((8,)), DMA((6,)), DMA((16, 2)), DMA((16, 2)), DMA((16,)), DMA((8,))],
+        + [DMA((11,)), DMA((6,)), DMA((16, 2)), DMA((16, 2)), DMA((16,)), DMA((8,))],
         compiler_params=params(3, 62),
         name="back",
     )(*operands)
 
 
 def finish_kernel(
-    err, gnorm, final, gx, gqw, gkw, gvw, gout, gup, gdown,
-    loss, one, two, final_out, gx_out, gqw_out, gkw_out, gvw_out, gout_out, gup_out, gdown_out,
+    err_in, gnorm_in, final, gx, gqw, gkw, gvw, gout, gup, gdown,
+    loss_out, one_out, two_out, final_out, gx_out, gqw_out, gkw_out, gvw_out, gout_out, gup_out, gdown_out,
     low_up, low_down, wide_up, wide_down, *rest,
 ):
-    rooms, sem, out_sem = rest[:6], rest[6], rest[7]
-    whole = ((gup, low_up), (gdown, low_down), *zip((final, gx, gqw, gkw, gvw, gout), rooms))
+    rooms, (err, gnorm, loss, one, two, sem, out_sem) = rest[:6], rest[6:]
+    whole = (
+        (gup, low_up), (gdown, low_down), *zip((final, gx, gqw, gkw, gvw, gout), rooms), (err_in, err), (gnorm_in, gnorm)
+    )
     copies = [pltpu.make_async_copy(src, dst, sem.at[i]) for i, (src, dst) in enumerate(whole)]
     for copy in copies:
         copy.start()
-    loss[...] = err[0:1, 0:1]
-    one[...] = gnorm[0:1, :]
-    two[...] = gnorm[1:2, :]
     outs = (final_out, gx_out, gqw_out, gkw_out, gvw_out, gout_out)
     last = []
     for i in range(6):
@@ -1784,6 +1815,14 @@
         wide_down[e, :, 768:] = wide[24:]
     last.append(pltpu.make_async_copy(wide_down, gdown_out, out_sem.at[7]))
     last[7].start()
+    copies[8].wait()
+    copies[9].wait()
+    loss[...] = err[0:1, 0:1]
+    one[...] = gnorm[0:1, 0:48]
+    two[...] = gnorm[1:2, 0:48]
+    for i, (src, dst) in enumerate(((loss, loss_out), (one, one_out), (two, two_out))):
+        last.append(pltpu.make_async_copy(src, dst, out_sem.at[8 + i]))
+        last[8 + i].start()
     for copy in last:
         copy.wait()
 
@@ -1806,8 +1845,8 @@
             shape(up, F32),
             shape(down, F32),
         ),
-        in_specs=[VMEM] * 2 + [ANY] * 8,
-        out_specs=(VMEM,) * 3 + (ANY,) * 8,
+        in_specs=[ANY] * 10,
+        out_specs=(ANY,) * 11,
         scratch_shapes=[
             pltpu.VMEM(up, BF),
             pltpu.VMEM((8, 48, 768), BF),
@@ -1819,8 +1858,13 @@
             pltpu.VMEM((48, 256), F32),
             pltpu.VMEM((48, 256), F32),
             pltpu.VMEM((48, 1536), F32),
-            DMA((8,)),
-            DMA((8,)),
+            pltpu.VMEM((8, 128), F32),
+            pltpu.VMEM((8, 128), F32),
+            pltpu.VMEM((1, 1), F32),
+            pltpu.VMEM((1, 48), F32),
+            pltpu.VMEM((1, 48), F32),
+            DMA((10,)),
+            DMA((11,)),
         ],
         compiler_params=pltpu.CompilerParams(vmem_limit_bytes=60 << 20),
         name="finish",
@@ -1838,8 +1882,9 @@
     freq = jnp.asarray(np.concatenate([freq, freq])[None, :], F32)
     rows = states.reshape(tokens, width)
     kept = valid.reshape(1, tokens)
-    gq, go, kv, win, wout, h, n2, n1, qs, o, lse, count = run_front(
-        doc_starts, freq, norm_one.reshape(1, -1), norm_two.reshape(1, -1), kept, rows, expert_out,
+    doc = doc_starts.reshape(1, -1)
+    gq, go, kv, win, wout, h, n2, n1, qs, o, lse, count, gains = run_front(
+        doc, freq, norm_one.reshape(1, -1), norm_two.reshape(1, -1), kept, rows, expert_out,
         w_query, key_weight, value_weight, w_output, expert_in,
     )
     error, final, dn2, dy, dwin, dwout = run_experts(
@@ -1847,7 +1892,7 @@
         n2, h, teacher.reshape(tokens, width), win, wout,
     )
     gx, gqw, gkw, gvw, gnorm, gout, gup, gdown = run_back(
-        doc_starts, freq, rows, h, n1, qs, o, lse, dn2, dy, dwin.reshape(16, 48, 768), dwout, gq, go, kv
+        doc, freq, gains, rows, h, n1, qs, o, lse, dn2, dy, dwin.reshape(16, 48, 768), dwout, gq, go, kv
     )
     loss, one, two, final, gx, gqw, gkw, gvw, gout, gup, gdown = run_finish(
         error, gnorm, final, gx, gqw, gkw, gvw, gout, gup, gdown

time: 409 us -> 397 us (0.971)
  Pallas kernels: 408 us -> 396 us
    pallas_call x1, Pallas kernels: 107 us -> 98.5 us  [run_back(): pl.pallas_call(back_kernel, out_shape=(shape((128, 1536), F32), shape((48...]
where the time goes in v5:
time: 397 us
  Pallas kernels  396 us (100%)
    pallas_call x1, Pallas kernels, run_experts(): pl.pallas_call(experts_kernel, out_shape=(shape((8, 128), F32), shape(wid...  182 us
    pallas_call x1, Pallas kernels, run_front(): pl.pallas_call(front_kernel, out_shape=(shape((32, 48, WIDE), BF), shape(...  111 us
    pallas_call x1, Pallas kernels, run_back(): pl.pallas_call(back_kernel, out_shape=(shape((128, 1536), F32), shape((48...  98.5 us

profile of v5, /device:TPU:0, one launch (start us, length us, event | category | flops | bytes accessed | tf_op | source)
XLA Modules:
  0.0 396.6 jit_solution(11787694381426996184)
XLA Ops:
  0.6 111.3 %front.1 = (bf16[32,48,2176]{2,1,0:T(8,128)(2,1)}, bf16[32,48,1536]{2,1,0:T(8,128)(2,1)}, bf16[32,128,512]{2,1,0:T(8,128)(2,1)}, bf16[16,48,768]{2,1,0:T(8,128)(...) custom-call(s32[1,3]{1,0:T(1,128)} %bitcast.26, ...), custom_call_target="tpu_custom_call" | custom-call | tf_op jit(solution)/shard_map/front/pallas_call | solution.py:989
  112.0 181.6 %experts.1 = (f32[8,128]{1,0:T(8,128)}, bf16[128,1536]{1,0:T(8,128)(2,1)}, f32[128,1536]{1,0:T(8,128)}, f32[128,1536]{1,0:T(8,128)}, bf16[768,768]{1,0:T(8,128)(2,1)}, /*index=5*/bf16[16,48,768]{2,1,0:T(8,128)(2,1)}) custom-call(s32[4,128]{1,0:T(4,128)} %bitcast.22, f32[4,128]{1,0:T(4,128)} %bitcast.23, s32[1,128]{1,0:T(1,128)} %bitcast.25, ...), custom_call_target="tpu_custom_call" | custom-call | tf_op jit(solution)/shard_map/experts/pallas_call | solution.py:1437
  293.6 98.5 %back.1 = (f32[128,1536]{1,0:T(8,128)}, f32[48,1536]{1,0:T(8,128)}, f32[48,256]{1,0:T(8,128)}, f32[48,256]{1,0:T(8,128)}, f32[8,128]{1,0:T(8,128)}, /*index=5*/f...) custom-call(s32[1,3]{1,0:T(1,128)} %bitcast.27, f32[1,128]{1,0:T(1,128)} %constant.2.clone.freq_in, ...), custom_call_target="tpu_custom_call" | custom-call | tf_op jit(solution)/shard_map/back/pallas_call | solution.py:1735
  392.2 4.3 %finish.1 = (f32[1,1]{1,0:T(1,128)}, f32[1,48]{1,0:T(1,128)}, f32[1,48]{1,0:T(1,128)}, bf16[128,1536]{1,0:T(8,128)(2,1)}, f32[128,1536]{1,0:T(8,128)}, /*index=5...) custom-call(f32[8,128]{1,0:T(8,128)} %get-tuple-element.54.err_in, ...), custom_call_target="tpu_custom_call" | custom-call | tf_op jit(solution)/shard_map/finish/pallas_call | solution.py:1833

commit v6 on v5

--- a/solution.py
+++ b/solution.py
@@ -444,7 +444,10 @@
         return carry
 
     lax.fori_loop(1, 32, one, 0)
-    pl.semaphore_wait(barrier, 31)
+
+
+def all_greeted():
+    pl.semaphore_wait(pltpu.get_barrier_semaphore(), 31)
 
 
 def remote(src, dst, send, recv, to):
@@ -612,22 +615,26 @@
         own = self.part[self.index(xx, zz, yy, self.me.c), :, self.cols]
         return k, own.astype(F32) + self.rc[k].astype(F32)
 
-    def turn(self, j):
+    def first_leg(self, i):
         me, half, first, second = self.me, self.half, self.first, self.second
         rc, rx, ry, rn, ss, vn = self.rc, self.rx, self.ry, self.rn, self.ss, self.vn
         x, y = me.x, me.y
 
-        @pl.when(self.valid(j))
+        @pl.when(self.valid(i))
         def _():
-            zz = self.place(j)
+            zz = self.place(i)
             k, total = self.with_core(1 - x, zz, 1 - y)
             rc[k] = total.astype(BF)
-            remote(rc.at[k, :, first], rx.at[zz], ss.at[j, 0], vn.at[zz, 0], me.near("x")).start()
-            remote(rc.at[k, :, second], ry.at[zz], ss.at[j, 1], vn.at[zz, 1], me.near("y")).start()
-
-        @pl.when(self.valid(j - 1))
+            remote(rc.at[k, :, first], rx.at[zz], ss.at[i, 0], vn.at[zz, 0], me.near("x")).start()
+            remote(rc.at[k, :, second], ry.at[zz], ss.at[i, 1], vn.at[zz, 1], me.near("y")).start()
+
+    def second_leg(self, i):
+        me, half, first, second = self.me, self.half, self.first, self.second
+        rc, rx, ry, rn, ss, vn = self.rc, self.rx, self.ry, self.rn, self.ss, self.vn
+        x, y = me.x, me.y
+
+        @pl.when(self.valid(i))
         def _():
-            i = j - 1
             zz = self.place(i)
             k, total = self.with_core(x, zz, 1 - y)
             arrived(rx.at[zz], vn.at[zz, 0], me)
@@ -640,9 +647,13 @@
             rc[k, :, second] = (total[:, half:] + ry[zz].astype(F32)).astype(BF)
             remote(rc.at[k], rn.at[1, zz], ss.at[i, 3], vn.at[zz, 3], me.near("x")).start()
 
-        @pl.when(self.valid(j - 2))
+    def third_leg(self, i):
+        me, half, first, second = self.me, self.half, self.first, self.second
+        rc, rx, ry, rn, ss, vn = self.rc, self.rx, self.ry, self.rn, self.ss, self.vn
+        x, y = me.x, me.y
+
+        @pl.when(self.valid(i))
         def _():
-            i = j - 2
             zz = self.place(i)
             k, total = self.with_core(x, zz, y)
             arrived(rn.at[0, zz], vn.at[zz, 2], me)
@@ -653,6 +664,22 @@
             @pl.when(zz == me.z)
             def _():
                 self.out[:, self.cols] = self.acc[...]
+
+    def turn(self, j):
+        self.first_leg(j)
+        self.second_leg(j - 1)
+        self.third_leg(j - 2)
+
+    def first_legs(self):
+        def one(j, carry):
+            self.first_leg(j)
+            return carry
+
+        lax.fori_loop(0, 4, one, 0)
+
+    def rest(self, j):
+        self.second_leg(j)
+        self.third_leg(j - 1)
 
     def close(self):
         me = self.me
@@ -787,6 +814,7 @@
     load_sem, own_sem, qsend, qrecv, gsend, grecv, ksend, krecv, asend, arecv, osend, orecv,
 ):
     me = Place()
+    greet_all(me)
     x, y, z, b, c = me.x, me.y, me.z, me.b, me.c
     here = by_weight(x, z, y, c)
     mine = [
@@ -813,7 +841,7 @@
         jnp.where(lane == 1, as_column(norm_two[...].astype(F32)), jnp.where(lane == 2, kept, 0.0)),
     )
     gq[here, :, pl.ds(QKV, 128)] = extra.astype(BF)
-    greet_all(me)
+    all_greeted()
     for copy in mine:
         copy.wait()
 
@@ -1052,19 +1080,20 @@
 GELU_B = 0.044715
 
 
+PARTS = ((0, 64), (64, 48), (112, 16))
 CUTS = 2
-CUT = 128 // CUTS
 
 
 def experts_kernel(
     routes_in, gates_in, valid_in, count_in, n2, h_in, teacher_in, win, wout,
     err_out, final_out, dn2_out, dy_out, dwin_out, dwout_out,
-    routes, gates, valid, count, err, h, teacher, final, dy, nall, dyall, pairs, zg, dpairs, part, rc, ry, rz, acc, errs, tables, gate,
+    routes, gates, valid, count, err, h, teacher, final, dy, nall, dyall, pairs, zg, dpairs, part, rc, ry, rz, rzt, ryt, tail, acc, errs, tables, gate,
     wfull, slab, wdown, dwin, dwin_in, dwout, dwout_in,
     load_sem, own_sem, gsend, grecv, csend, crecv, ysend, yrecv, zsend, zrecv, esend, erecv,
     tsend, trecv, xsend, xrecv,
 ):
     me = Place()
+    greet_all(me)
     x, y, z, b, c = me.x, me.y, me.z, me.b, me.c
     half = pltpu.make_async_copy(win, wfull.at[x], own_sem.at[0])
     half.start()
@@ -1081,10 +1110,10 @@
         load.start()
     held = pltpu.make_async_copy(wout, slab, own_sem.at[1])
     pl.when(c == x)(held.start)
-    greet_all(me)
+    all_greeted()
 
     def rows_of(p):
-        return pl.ds(p * CUT, CUT)
+        return pl.ds(*PARTS[p])
 
     def over_weights(k):
         cut = pl.ds(k * 4, 4)
@@ -1093,13 +1122,23 @@
     def over_down():
         return remote(wout, slab, xsend.at[4], xrecv.at[4], me.near("x"))
 
+    def put(buf, way, j, p, kind, n, s):
+        ref = buf.at[s, rows_of(p)]
+        remote(ref, ref, gsend.at[way, j, p, n], grecv.at[way, s, p], me.near(kind)).start()
+
+    def along(buf, way, j, p, n, s, zz):
+        pl.when((zz <= z) & (z < NZ - 1))(lambda: put(buf, way, j, p, "up", n, s))
+        pl.when((zz >= z) & (z > 0))(lambda: put(buf, way, j, p, "down", n + 1, s))
+
+    def begin(buf, way, p):
+        along(buf, way, 0, p, 0, b, z)
+        put(buf, way, 0, p, "y", 2, b)
+        put(buf, way, 0, p, "c", 3, b)
+
     def gather(buf, way, between):
-        def put(j, p, kind, n, s):
-            ref = buf.at[s, rows_of(p)]
-            remote(ref, ref, gsend.at[way, j, p, n], grecv.at[way, s, p], me.near(kind)).start()
-
         def turn(j, carry):
-            for p in range(CUTS):
+            between(j, -1)
+            for p in range(CUTS + 1):
                 zz = me.outward(j)
                 own = me.blk(zz, y, c)
 
@@ -1107,19 +1146,22 @@
                 def _():
                     arrived(buf.at[own, rows_of(p)], grecv.at[way, own, p], me)
 
-                @pl.when(j < 4)
+                @pl.when((j > 0) & (j < 4))
                 def _():
-                    pl.when((zz <= z) & (z < NZ - 1))(lambda: put(j, p, "up", 0, own))
-                    pl.when((zz >= z) & (z > 0))(lambda: put(j, p, "down", 1, own))
-                    put(j, p, "y", 2, own)
-                    put(j, p, "c", 3, own)
+                    along(buf, way, j, p, 0, own, zz)
+                    if p < CUTS:
+                        put(buf, way, j, p, "y", 2, own)
+                    put(buf, way, j, p, "c", 3, own)
 
                 @pl.when((j > 0) & (j < 5))
                 def _():
                     i = j - 1
-                    s = me.blk(me.outward(i), 1 - y, c)
+                    zp = me.outward(i)
+                    s = me.blk(zp, 1 - y, c)
                     arrived(buf.at[s, rows_of(p)], grecv.at[way, s, p], me)
-                    put(i, p, "c", 4, s)
+                    if p == CUTS:
+                        along(buf, way, i, p, 5, s, zp)
+                    put(buf, way, i, p, "c", 4, s)
 
                 between(j, p)
             return carry
@@ -1128,11 +1170,17 @@
 
         def close(j, carry):
             zz = me.outward(j)
-            whole = buf.at[b, rows_of(0)]
-            for p in range(CUTS):
-                pl.when((zz <= z) & (z < NZ - 1))(lambda: left(whole, gsend.at[way, j, p, 0], me))
-                pl.when((zz >= z) & (z > 0))(lambda: left(whole, gsend.at[way, j, p, 1], me))
-                for n in (2, 3, 4):
+            for p in range(CUTS + 1):
+                whole = buf.at[b, rows_of(p)]
+                ends = (0, 1) if p < CUTS else (0, 1, 5, 6)
+                for n in ends:
+                    ok = (zz <= z) & (z < NZ - 1) if n in (0, 5) else (zz >= z) & (z > 0)
+                    pl.when(ok)(lambda: left(whole, gsend.at[way, j, p, n], me))
+                if p < CUTS:
+                    left(whole, gsend.at[way, j, p, 2], me)
+                else:
+                    pl.when(j == 0)(lambda: left(whole, gsend.at[way, j, p, 2], me))
+                for n in (3, 4):
                     left(whole, gsend.at[way, j, p, n], me)
             return carry
 
@@ -1140,7 +1188,7 @@
 
     def from_core(buf, way, zz, yy):
         s = me.blk(zz, yy, 1 - c)
-        for p in range(CUTS):
+        for p in range(CUTS + 1):
             arrived(buf.at[s, rows_of(p)], grecv.at[way, s, p], me)
 
     def to_other_core(way, q):
@@ -1157,11 +1205,29 @@
                 part.at[s, rows_of(p)], ry.at[zz, rows_of(p)], ysend.at[way, j, p], yrecv.at[way, zz, p], me.near("y")
             ).start()
 
-    def follow(way, j):
+    def follow(way, j, done=None):
         zz = me.inward(j)
         q = zz * 2 + y
         s = q * 2 + c
         arrived(rc.at[q], crecv.at[way, q], me)
+        cut = rows_of(CUTS)
+        for n, yy in enumerate((1 - y, y)):
+            k = zz * 2 + yy
+            room = part.at[k * 2 + c, cut]
+            if n:
+                tail[...] = room[...].astype(F32) + rc[k, cut].astype(F32)
+            else:
+                tail[...] = room[...].astype(F32)
+            along_z(
+                me, j, zz, tail, room, rzt.at[n], zsend.at[way, :, CUTS + n], 0, zrecv.at[way, :, CUTS + n]
+            )
+            if n == 0:
+
+                @pl.when(zz == z)
+                def _():
+                    room[...] = tail[...].astype(BF)
+                    remote(room, ryt, ysend.at[way, 3, CUTS], yrecv.at[way, 0, CUTS], me.near("y")).start()
+
         for p in range(CUTS):
             cut = rows_of(p)
             arrived(ry.at[zz, cut], yrecv.at[way, zz, p], me)
@@ -1170,15 +1236,28 @@
             along_z(
                 me, j, zz, piece, part.at[s, cut], rz.at[:, cut], zsend.at[way, :, p], 0, zrecv.at[way, :, p]
             )
+            if done is not None:
+                pl.when(zz == z)(functools.partial(done, p))
+
+        @pl.when(zz == z)
+        def _():
+            arrived(ryt, yrecv.at[way, 0, CUTS], me)
+            acc[rows_of(CUTS)] = tail[...] + ryt[...].astype(F32)
+            if done is not None:
+                done(CUTS)
 
     def close_sum(way):
         def close(j, carry):
             zz = me.inward(j)
-            whole, piece = part.at[b], part.at[b, rows_of(0)]
+            whole = part.at[b]
             left(whole, csend.at[way, j], me)
             left(whole, csend.at[way, j + 4], me)
-            for p in range(CUTS):
-                left(piece, ysend.at[way, j, p], me)
+            for p in range(CUTS + 2):
+                piece = part.at[b, rows_of(min(p, CUTS))]
+                if p < CUTS:
+                    left(piece, ysend.at[way, j, p], me)
+                elif p == CUTS:
+                    pl.when(j == 3)(lambda: left(piece, ysend.at[way, j, p], me))
                 pl.when(zz > z)(lambda: left(piece, zsend.at[way, j, p, 0], me))
                 pl.when(zz < z)(lambda: left(piece, zsend.at[way, j, p, 1], me))
             return carry
@@ -1240,6 +1319,8 @@
                 tables[b] = table
                 lax.fori_loop(1, 16, tell_gates, 0)
 
+    for p in range(CUTS + 1):
+        begin(nall, 0, p)
     gather(nall, 0, with_tokens)
 
     def all_cores(buf, way):
@@ -1273,31 +1354,39 @@
     wdown[:, :768] = wide[:, 0].reshape(384, 768).astype(BF)
     wdown[:, 768:] = wide[:, 1].reshape(384, 768).astype(BF)
 
+    keep = as_column(valid[...].astype(F32))
+    factor = keep * (SPAN / count[0:1, 0:1])
+    loads[1].wait()
+    loads[2].wait()
+    me_index = x * 16 + b
+    errs[me_index] = jnp.zeros((8, 128), F32)
+
+    def loss_and_dy(p):
+        cut, at = rows_of(p), slice(PARTS[p][0], PARTS[p][0] + PARTS[p][1])
+        done = h[cut] + acc[cut]
+        final[cut] = done.astype(BF)
+        diff = done - teacher[cut].astype(F32)
+        scaled = factor[at] * diff
+        dy[cut] = scaled
+        dyall[b, cut] = scaled.astype(BF)
+        begin(dyall, 1, p)
+        errs[me_index] += jnp.zeros((8, 128), F32) + jnp.sum(keep[at] * diff * diff)
+
     def outputs(j, carry):
         @pl.when(j < 4)
         def _():
             forward(me.inward(j) * 2 + 1 - y)
 
-        pl.when(j > 0)(lambda: follow(0, j - 1))
-
-        @pl.when(j < 4)
+        @pl.when((j > 0) & (j < 5))
         def _():
-            lead(0, j)
-            forward(me.inward(j) * 2 + y)
-
+            forward(me.inward(j - 1) * 2 + y)
+
+        pl.when(j < 4)(lambda: lead(0, j))
+        pl.when(j > 1)(lambda: follow(0, j - 2, loss_and_dy))
         return carry
 
-    lax.fori_loop(0, 5, outputs, 0)
-
-    keep = as_column(valid[...].astype(F32))
-    loads[1].wait()
-    loads[2].wait()
-    done = h[...] + acc[...]
-    final[...] = done.astype(BF)
-    diff = done - teacher[...].astype(F32)
-    scaled = (keep * (SPAN / count[0:1, 0:1])) * diff
-    dy[...] = scaled
-    dyall[b] = scaled.astype(BF)
+    lax.fori_loop(0, 6, outputs, 0)
+
     saved = [
         pltpu.make_async_copy(final, final_out, load_sem.at[0]),
         pltpu.make_async_copy(dy, dy_out, load_sem.at[1]),
@@ -1306,24 +1395,31 @@
     ]
     for copy in saved[:2]:
         copy.start()
-    kept = jnp.sum(keep * diff * diff)
-    me_index = x * 16 + b
-    errs[me_index] = jnp.zeros((8, 128), F32) + kept
-
     def tell(k, carry):
         to = ((x + k // 16) % 2, (b + k) % 16)
         remote(errs.at[me_index], errs.at[me_index], esend.at[k], erecv.at[me_index], to).start()
         return carry
 
+    def inputs(i, yy):
+        zz = me.outward(i)
+        from_core(dyall, 1, zz, yy)
+        backward(zz * 2 + yy)
+
     def with_dy(j, p):
-        if p == 0:
-
-            @pl.when((j > 0) & (j < 5))
+        if p == -1:
+
+            @pl.when(j == 4)
             def _():
-                zz = me.outward(j - 1)
-                from_core(dyall, 1, zz, y)
-                backward(zz * 2 + y)
-
+                inputs(2, 1 - y)
+                inputs(3, y)
+
+            @pl.when(j == 5)
+            def _():
+                lead(1, 3)
+                inputs(3, 1 - y)
+
+        elif p == 0:
+            pl.when((j > 0) & (j < 4))(lambda: inputs(j - 1, y))
         elif p == CUTS - 1:
 
             @pl.when(j == 0)
@@ -1331,11 +1427,7 @@
                 lax.fori_loop(1, 32, tell, 0)
                 close_sum(0)
 
-            @pl.when(j > 1)
-            def _():
-                zz = me.outward(j - 2)
-                from_core(dyall, 1, zz, 1 - y)
-                backward(zz * 2 + 1 - y)
+            pl.when((j > 1) & (j < 4))(lambda: inputs(j - 2, 1 - y))
 
     gather(dyall, 1, with_dy)
 
@@ -1364,7 +1456,7 @@
         lead(1, j)
         return carry
 
-    lax.fori_loop(0, 4, leads, 0)
+    lax.fori_loop(0, 3, leads, 0)
 
     def sums(j, carry):
         @pl.when(j == 0)
@@ -1465,6 +1557,9 @@
             pltpu.VMEM((8,) + wide, BF),
             pltpu.VMEM((4,) + wide, BF),
             pltpu.VMEM((5,) + wide, BF),
+            pltpu.VMEM((2, 5, PARTS[CUTS][1], 1536), BF),
+            pltpu.VMEM((PARTS[CUTS][1], 1536), BF),
+            pltpu.VMEM((PARTS[CUTS][1], 1536), F32),
             pltpu.VMEM(wide, F32),
             pltpu.VMEM((32, 8, 128), F32),
             pltpu.VMEM((16, 8, 128), F32),
@@ -1478,14 +1573,14 @@
             pltpu.VMEM((16, 48, 768), BF),
             DMA((7,)),
             DMA((2,)),
-            DMA((2, 4, CUTS, 5)),
-            DMA((2, 16, CUTS)),
+            DMA((2, 4, CUTS + 1, 7)),
+            DMA((2, 16, CUTS + 1)),
             DMA((2, 8)),
             DMA((2, 8)),
-            DMA((2, 4, CUTS)),
-            DMA((2, 4, CUTS)),
-            DMA((2, 4, CUTS, 2)),
-            DMA((2, 5, CUTS)),
+            DMA((2, 4, CUTS + 1)),
+            DMA((2, 4, CUTS + 1)),
+            DMA((2, 4, CUTS + 2, 2)),
+            DMA((2, 5, CUTS + 2)),
             DMA((32,)),
             DMA((32,)),
             DMA((16,)),
@@ -1520,6 +1615,7 @@
     sums = [(rest[i * 11 : i * 11 + 6], rest[i * 11 + 6 : i * 11 + 11]) for i in range(5)]
     load_sem, own_sem, asend, arecv, osend, orecv = rest[55:]
     me = Place()
+    greet_all(me)
     x, y, z, b, c = me.x, me.y, me.z, me.b, me.c
     loads = [
         pltpu.make_async_copy(go, wo, own_sem.at[0]),
@@ -1537,7 +1633,7 @@
     ]
     for load in small[:3] + [small[10], loads[0]] + small[3:10] + [loads[1], loads[2]]:
         load.start()
-    greet_all(me)
+    all_greeted()
 
     def own_piece(n):
         col = pl.multiple_of(n * 768 + c * 384, 128)
@@ -1666,10 +1762,10 @@
         lead_all(piece)
 
     def last_turn(j, carry):
+        out_sum.turn(j + 4)
+        pl.when(j < 2)(lambda: key_sum.turn(j + 4))
         for piece in proj:
             piece.turn(j)
-        out_sum.turn(j + 4)
-        pl.when(j < 2)(lambda: key_sum.turn(j + 4))
 
         @pl.when(j == 1)
         def _():
@@ -1687,11 +1783,12 @@
             pw[:, :, pl.ds(QKV, 128)] = tail.astype(BF).reshape(32, 48, 128)
             lead_all(rest_sum)
             gx[...] = dh[...] + in_grad
-
-        rest_sum.turn(j - 2)
+            rest_sum.first_legs()
+
+        rest_sum.rest(j - 2)
         return carry
 
-    lax.fori_loop(0, 8, last_turn, 0)
+    lax.fori_loop(0, 7, last_turn, 0)
     gkv[...] = gqkv[:, 1536:2048]
     stores = [
         pltpu.make_async_copy(gx, gx_out, load_sem.at[0]),

time: 397 us -> 395 us (level); the launches traced: 397 us -> 389 us
  Pallas kernels: 396 us -> 388 us
    pallas_call x1, Pallas kernels: 182 us -> 173 us  [run_experts(): pl.pallas_call(experts_kernel, out_shape=(shape((8, 128), F32), shape(wid...]
where the time goes in v6:
time: 395 us; the launch traced here: 389 us
  Pallas kernels  388 us (98%)
    pallas_call x1, Pallas kernels, run_experts(): pl.pallas_call(experts_kernel, out_shape=(shape((8, 128), F32), shape(wid...  173 us
    pallas_call x1, Pallas kernels, run_front(): pl.pallas_call(front_kernel, out_shape=(shape((32, 48, WIDE), BF), shape(...  110 us
    pallas_call x1, Pallas kernels, run_back(): pl.pallas_call(back_kernel, out_shape=(shape((128, 1536), F32), shape((48...  100 us

profile of v6, /device:TPU:0, one launch (start us, length us, event | category | flops | bytes accessed | tf_op | source)
XLA Modules:
  0.0 388.7 jit_solution(12212926637599232092)
XLA Ops:
  0.6 109.9 %front.1 = (bf16[32,48,2176]{2,1,0:T(8,128)(2,1)}, bf16[32,48,1536]{2,1,0:T(8,128)(2,1)}, bf16[32,128,512]{2,1,0:T(8,128)(2,1)}, bf16[16,48,768]{2,1,0:T(8,128)(...) custom-call(s32[1,3]{1,0:T(1,128)} %bitcast.26, ...), custom_call_target="tpu_custom_call" | custom-call | tf_op jit(solution)/shard_map/front/pallas_call | solution.py:1017
  110.6 173.3 %experts.1 = (f32[8,128]{1,0:T(8,128)}, bf16[128,1536]{1,0:T(8,128)(2,1)}, f32[128,1536]{1,0:T(8,128)}, f32[128,1536]{1,0:T(8,128)}, bf16[768,768]{1,0:T(8,128)(2,1)}, /*index=5*/bf16[16,48,768]{2,1,0:T(8,128)(2,1)}) custom-call(s32[4,128]{1,0:T(4,128)} %bitcast.22, f32[4,128]{1,0:T(4,128)} %bitcast.23, s32[1,128]{1,0:T(1,128)} %bitcast.25, ...), custom_call_target="tpu_custom_call" | custom-call | tf_op jit(solution)/shard_map/experts/pallas_call | solution.py:1529
  283.9 100.0 %back.1 = (f32[128,1536]{1,0:T(8,128)}, f32[48,1536]{1,0:T(8,128)}, f32[48,256]{1,0:T(8,128)}, f32[48,256]{1,0:T(8,128)}, f32[8,128]{1,0:T(8,128)}, /*index=5*/f...) custom-call(s32[1,3]{1,0:T(1,128)} %bitcast.27, f32[1,128]{1,0:T(1,128)} %constant.2.clone.freq_in, ...), custom_call_target="tpu_custom_call" | custom-call | tf_op jit(solution)/shard_map/back/pallas_call | solution.py:1832
  383.9 4.3 %finish.1 = (f32[1,1]{1,0:T(1,128)}, f32[1,48]{1,0:T(1,128)}, f32[1,48]{1,0:T(1,128)}, bf16[128,1536]{1,0:T(8,128)(2,1)}, f32[128,1536]{1,0:T(8,128)}, /*index=5...) custom-call(f32[8,128]{1,0:T(8,128)} %get-tuple-element.54.err_in, ...), custom_call_target="tpu_custom_call" | custom-call | tf_op jit(solution)/shard_map/finish/pallas_call | solution.py:1930

commit v7 on v6

--- a/solution.py
+++ b/solution.py
@@ -539,7 +539,14 @@
             for yy in (me.y, 1 - me.y):
                 self.wait(self.index(xx, self.place(j), yy, 1 - me.c))
 
-    def close(self, cores=True):
+    def from_cores(self):
+        def one(j, carry):
+            self.from_core(j)
+            return carry
+
+        lax.fori_loop(0, 4, one, 0)
+
+    def close(self):
         me = self.me
 
         def one(j, carry):
@@ -556,8 +563,6 @@
                     left(whole, self.send.at[j, n], me)
                 left(first, self.send.at[j, 4], me)
                 left(second, self.send.at[j, 5], me)
-                if cores:
-                    self.from_core(j)
 
             return carry
 
@@ -855,7 +860,7 @@
         return pltpu.make_async_copy(down.at[b // 2], wout.at[b], own_sem.at[6])
 
     def deal(k, carry):
-        t = (b + k) % 16
+        t = (b + (k * 13) % 16) % 16
         for n in range(2):
             col = pl.multiple_of(n * 768 + (t % 2) * 384, 128)
             remote(
@@ -898,7 +903,7 @@
     rows = low_rows[...].astype(F32)
     level = rows * lax.rsqrt(jnp.mean(rows * rows, axis=-1, keepdims=True) + 1e-06)
     for piece in weights:
-        piece.close()
+        piece.from_cores()
     keep = pltpu.make_async_copy(gq, gq_out, own_sem.at[0])
     keep.start()
 
@@ -946,9 +951,30 @@
             total[i] = total[i] * factor + jnp.sum(p, axis=0, keepdims=True)
             acc[i] = acc[i] * factor + lax.dot_general(v, p.astype(BF), TN, preferred_element_type=F32)
 
+    def close_deal(k, carry):
+        piece = win.at[b, :, pl.ds(0, 384)]
+        f = (b + 16 - k) % 16
+        for n in range(2):
+            left(piece, asend.at[k, n], me)
+            arrived(win.at[f, :, pl.ds(n * 384, 384)], arecv.at[f, n], me)
+        pl.when((b + k) % 2 == x)(lambda: left(wout.at[b], osend.at[k], me))
+        pl.when(c == x)(lambda: arrived(wout.at[f], orecv.at[f], me))
+        return carry
+
     def turn(j, carry):
         pl.when(j > 0)(lambda: keys.turn(j))
         output.turn(j - 2)
+
+        @pl.when(j == 1)
+        def _():
+            for piece in weights:
+                piece.close()
+
+        @pl.when(j == 6)
+        def _():
+            lax.fori_loop(1, 16, close_deal, 0)
+            keys.close()
+
 
         @pl.when(keys.valid(j - 2))
         def _():
@@ -966,9 +992,6 @@
         return carry
 
     lax.fori_loop(0, 8, turn, 0)
-    output.close()
-    keep_o = pltpu.make_async_copy(go, go_out, own_sem.at[1])
-    keep_o.start()
     keep_k = pltpu.make_async_copy(kv, kv_out, own_sem.at[2])
     keep_k.start()
     for i in range(2):
@@ -980,6 +1003,9 @@
     more = [pltpu.make_async_copy(o, o_out, load_sem.at[2]), pltpu.make_async_copy(lse, lse_out, load_sem.at[7])]
     for copy in more:
         copy.start()
+    output.from_cores()
+    keep_o = pltpu.make_async_copy(go, go_out, own_sem.at[1])
+    keep_o.start()
     res = low_rows[...].astype(F32) + jnp.dot(
         o[...].astype(BF), go[...].reshape(1536, 1536), preferred_element_type=F32
     )
@@ -992,19 +1018,7 @@
     more[2].start()
     more[3].start()
 
-    keys.close(False)
-
-    def close(k, carry):
-        piece = win.at[b, :, pl.ds(0, 384)]
-        f = (b + 16 - k) % 16
-        for n in range(2):
-            left(piece, asend.at[k, n], me)
-            arrived(win.at[f, :, pl.ds(n * 384, 384)], arecv.at[f, n], me)
-        pl.when((b + k) % 2 == x)(lambda: left(wout.at[b], osend.at[k], me))
-        pl.when(c == x)(lambda: arrived(wout.at[f], orecv.at[f], me))
-        return carry
-
-    lax.fori_loop(1, 16, close, 0)
+    output.close()
     for n in range(2):
         own_piece(n).wait()
     pl.when(c == x)(lambda: own_down().wait())
@@ -1168,6 +1182,7 @@
 
         lax.fori_loop(0, 6, turn, 0)
 
+    def close_gather(buf, way):
         def close(j, carry):
             zz = me.outward(j)
             for p in range(CUTS + 1):
@@ -1382,6 +1397,7 @@
             forward(me.inward(j - 1) * 2 + y)
 
         pl.when(j < 4)(lambda: lead(0, j))
+        pl.when(j == 1)(lambda: close_gather(nall, 0))
         pl.when(j > 1)(lambda: follow(0, j - 2, loss_and_dy))
         return carry
 
@@ -1458,7 +1474,22 @@
 
     lax.fori_loop(0, 3, leads, 0)
 
+    def hear(k, carry):
+        left(errs.at[0], esend.at[k], me)
+        s = ((x + k // 16) % 2) * 16 + (b + k) % 16
+        arrived(errs.at[s], erecv.at[s], me)
+        return carry
+
     def sums(j, carry):
+        @pl.when(j == 3)
+        def _():
+            close_gather(dyall, 1)
+            lax.fori_loop(1, 32, hear, 0)
+            total = errs[0]
+            for s in range(1, 32):
+                total = total + errs[s]
+            err[...] = total / (1536.0 * count[...])
+
         @pl.when(j == 0)
         def _():
             for k in range(3):
@@ -1485,20 +1516,8 @@
     pl.when(c == x)(lambda: over_down().wait_send())
     lax.fori_loop(0, 4, sums, 0)
     saved[2].start()
+    saved[3].start()
     close_sum(1)
-
-    def hear(k, carry):
-        left(errs.at[0], esend.at[k], me)
-        s = ((x + k // 16) % 2) * 16 + (b + k) % 16
-        arrived(errs.at[s], erecv.at[s], me)
-        return carry
-
-    lax.fori_loop(1, 32, hear, 0)
-    total = errs[0]
-    for s in range(1, 32):
-        total = total + errs[s]
-    err[...] = total / (1536.0 * count[...])
-    saved[3].start()
 
     for k in range(3):
         over_in(k).wait_send()
@@ -1645,7 +1664,7 @@
         return pltpu.make_async_copy(dwout.at[b], gdown.at[b // 2], own_sem.at[5])
 
     def deal(k, carry):
-        t = (b + k) % 16
+        t = (b + (k * 9) % 16) % 16
         for n in range(2):
             col = pl.multiple_of(n * 768 + c * 384, 128)
             remote(
@@ -1761,6 +1780,25 @@
     for piece in proj:
         lead_all(piece)
 
+    stores = [
+        pltpu.make_async_copy(gx, gx_out, load_sem.at[0]),
+        pltpu.make_async_copy(gout, gout_out, load_sem.at[1]),
+        pltpu.make_async_copy(gqkv.at[:, pl.ds(0, 1536)], gqw, load_sem.at[2]),
+        pltpu.make_async_copy(gkv.at[:, pl.ds(0, 256)], gkw, load_sem.at[3]),
+        pltpu.make_async_copy(gkv.at[:, pl.ds(256, 256)], gvw, load_sem.at[4]),
+        pltpu.make_async_copy(gnorm, gnorm_out, load_sem.at[5]),
+    ]
+
+    def close_deal(k, carry):
+        f = (b + 16 - k) % 16
+        for n in range(2):
+            left(dwin.at[0, :, pl.ds(0, 384)], asend.at[k, n], me)
+            col = pl.multiple_of(n * 768 + (f % 2) * 384, 128)
+            arrived(gup.at[f // 2, :, pl.ds(col, 384)], arecv.at[f, n], me)
+        pl.when(c == x)(lambda: left(dwout.at[0], osend.at[k], me))
+        pl.when(f % 2 == x)(lambda: arrived(gdown.at[f // 2], orecv.at[f // 2], me))
+        return carry
+
     def last_turn(j, carry):
         out_sum.turn(j + 4)
         pl.when(j < 2)(lambda: key_sum.turn(j + 4))
@@ -1786,40 +1824,35 @@
             rest_sum.first_legs()
 
         rest_sum.rest(j - 2)
+
+        @pl.when(j == 2)
+        def _():
+            stores[0].start()
+            stores[1].start()
+            out_sum.close()
+
+        @pl.when(j == 3)
+        def _():
+            key_sum.close()
+            lax.fori_loop(1, 16, close_deal, 0)
+
+        @pl.when(j == 5)
+        def _():
+            stores[2].start()
+            for piece in proj:
+                piece.close()
+
         return carry
 
     lax.fori_loop(0, 7, last_turn, 0)
     gkv[...] = gqkv[:, 1536:2048]
-    stores = [
-        pltpu.make_async_copy(gx, gx_out, load_sem.at[0]),
-        pltpu.make_async_copy(gout, gout_out, load_sem.at[1]),
-        pltpu.make_async_copy(gqkv.at[:, pl.ds(0, 1536)], gqw, load_sem.at[2]),
-        pltpu.make_async_copy(gkv.at[:, pl.ds(0, 256)], gkw, load_sem.at[3]),
-        pltpu.make_async_copy(gkv.at[:, pl.ds(256, 256)], gvw, load_sem.at[4]),
-    ]
-    for store in stores:
+    for store in stores[3:5]:
         store.start()
     gnorm[0:1, 0:48] = as_row(gqkv[:, 2048:2049])
     gnorm[1:2, 0:48] = as_row(gqkv[:, 2049:2050])
-    stores.append(pltpu.make_async_copy(gnorm, gnorm_out, load_sem.at[5]))
     stores[5].start()
-    out_sum.close()
-    key_sum.close()
     rest_sum.close()
-    for piece in proj:
-        piece.close()
-
-    def close(k, carry):
-        f = (b + 16 - k) % 16
-        for n in range(2):
-            left(dwin.at[0, :, pl.ds(0, 384)], asend.at[k, n], me)
-            col = pl.multiple_of(n * 768 + (f % 2) * 384, 128)
-            arrived(gup.at[f // 2, :, pl.ds(col, 384)], arecv.at[f, n], me)
-        pl.when(c == x)(lambda: left(dwout.at[0], osend.at[k], me))
-        pl.when(f % 2 == x)(lambda: arrived(gdown.at[f // 2], orecv.at[f // 2], me))
-        return carry
-
-    lax.fori_loop(1, 16, close, 0)
+
     for n in range(2):
         own_piece(n).wait()
     pl.when(c == x)(lambda: own_down().wait())

time: 395 us -> 389 us (0.985)
  Pallas kernels: 388 us -> 381 us
    pallas_call x1, Pallas kernels: 110 us -> 104 us  [run_front(): pl.pallas_call(front_kernel, out_shape=(shape((32, 48, WIDE), BF), shape(...]
where the time goes in v7:
time: 389 us; the launch traced here: 382 us
  Pallas kernels  381 us (98%)
    pallas_call x1, Pallas kernels, run_experts(): pl.pallas_call(experts_kernel, out_shape=(shape((8, 128), F32), shape(wid...  175 us
    pallas_call x1, Pallas kernels, run_front(): pl.pallas_call(front_kernel, out_shape=(shape((32, 48, WIDE), BF), shape(...  104 us
    pallas_call x1, Pallas kernels, run_back(): pl.pallas_call(back_kernel, out_shape=(shape((128, 1536), F32), shape((48...  98.3 us

profile of v7, /device:TPU:0, one launch (start us, length us, event | category | flops | bytes accessed | tf_op | source)
XLA Modules:
  0.0 382.4 jit_solution(4823175000845012436)
XLA Ops:
  0.6 103.9 %front.1 = (bf16[32,48,2176]{2,1,0:T(8,128)(2,1)}, bf16[32,48,1536]{2,1,0:T(8,128)(2,1)}, bf16[32,128,512]{2,1,0:T(8,128)(2,1)}, bf16[16,48,768]{2,1,0:T(8,128)(...) custom-call(s32[1,3]{1,0:T(1,128)} %bitcast.26, ...), custom_call_target="tpu_custom_call" | custom-call | tf_op jit(solution)/shard_map/front/pallas_call | solution.py:1031
  104.5 174.8 %experts.1 = (f32[8,128]{1,0:T(8,128)}, bf16[128,1536]{1,0:T(8,128)(2,1)}, f32[128,1536]{1,0:T(8,128)}, f32[128,1536]{1,0:T(8,128)}, bf16[768,768]{1,0:T(8,128)(2,1)}, /*index=5*/bf16[16,48,768]{2,1,0:T(8,128)(2,1)}) custom-call(s32[4,128]{1,0:T(4,128)} %bitcast.22, f32[4,128]{1,0:T(4,128)} %bitcast.23, s32[1,128]{1,0:T(1,128)} %bitcast.25, ...), custom_call_target="tpu_custom_call" | custom-call | tf_op jit(solution)/shard_map/experts/pallas_call | solution.py:1548
  279.3 98.3 %back.1 = (f32[128,1536]{1,0:T(8,128)}, f32[48,1536]{1,0:T(8,128)}, f32[48,256]{1,0:T(8,128)}, f32[48,256]{1,0:T(8,128)}, f32[8,128]{1,0:T(8,128)}, /*index=5*/f...) custom-call(s32[1,3]{1,0:T(1,128)} %bitcast.27, f32[1,128]{1,0:T(1,128)} %constant.2.clone.freq_in, ...), custom_call_target="tpu_custom_call" | custom-call | tf_op jit(solution)/shard_map/back/pallas_call | solution.py:1865
  377.7 4.3 %finish.1 = (f32[1,1]{1,0:T(1,128)}, f32[1,48]{1,0:T(1,128)}, f32[1,48]{1,0:T(1,128)}, bf16[128,1536]{1,0:T(8,128)(2,1)}, f32[128,1536]{1,0:T(8,128)}, /*index=5...) custom-call(f32[8,128]{1,0:T(8,128)} %get-tuple-element.54.err_in, ...), custom_call_target="tpu_custom_call" | custom-call | tf_op jit(solution)/shard_map/finish/pallas_call | solution.py:1963

commit v8 on v7

--- a/solution.py
+++ b/solution.py
@@ -1094,6 +1094,7 @@
 GELU_B = 0.044715
 
 
+READY_AT = 4
 PARTS = ((0, 64), (64, 48), (112, 16))
 CUTS = 2
 
@@ -1316,6 +1317,25 @@
         remote(tables.at[b], tables.at[b], tsend.at[k], trecv.at[b], (x, to)).start()
         return carry
 
+    def hear_gates(k, carry):
+        left(tables.at[0], tsend.at[k], me)
+        arrived(tables.at[(b + 16 - k) % 16], trecv.at[(b + 16 - k) % 16], me)
+        return carry
+
+    def gate_of(s, carry):
+        row = lax.broadcasted_iota(jnp.int32, (8, 128), 0)
+        picked = jnp.sum(jnp.where(row == b // 2, tables[s], 0.0), axis=0, keepdims=True)
+        gate[s] = as_column(picked)
+        return carry
+
+    def ready():
+        lax.fori_loop(1, 16, hear_gates, 0)
+        lax.fori_loop(0, 16, gate_of, 0)
+        pl.when(c != x)(lambda: arrived(slab, xrecv.at[4], me))
+        wide = slab[...].astype(F32).reshape(16, 2, 24, 768)
+        wdown[:, :768] = wide[:, 0].reshape(384, 768).astype(BF)
+        wdown[:, 768:] = wide[:, 1].reshape(384, 768).astype(BF)
+
     def with_tokens(j, p):
         if p == 0:
             pl.when((j == 0) & (c == x))(lambda: over_down().start())
@@ -1334,6 +1354,8 @@
                 tables[b] = table
                 lax.fori_loop(1, 16, tell_gates, 0)
 
+            pl.when(j == READY_AT)(ready)
+
     for p in range(CUTS + 1):
         begin(nall, 0, p)
     gather(nall, 0, with_tokens)
@@ -1347,28 +1369,9 @@
         lax.fori_loop(0, 4, one, 0)
 
     all_cores(nall, 0)
-    def hear_gates(k, carry):
-        left(tables.at[0], tsend.at[k], me)
-        arrived(tables.at[(b + 16 - k) % 16], trecv.at[(b + 16 - k) % 16], me)
-        return carry
-
-    lax.fori_loop(1, 16, hear_gates, 0)
-
-    def gate_of(s, carry):
-        row = lax.broadcasted_iota(jnp.int32, (8, 128), 0)
-        picked = jnp.sum(jnp.where(row == b // 2, tables[s], 0.0), axis=0, keepdims=True)
-        gate[s] = as_column(picked)
-        return carry
-
-    lax.fori_loop(0, 16, gate_of, 0)
     half.wait()
     for k in range(4):
         arrived(wfull.at[1 - x, pl.ds(k * 4, 4)], xrecv.at[k], me)
-    pl.when(c != x)(lambda: arrived(slab, xrecv.at[4], me))
-    wide = slab[...].astype(F32).reshape(16, 2, 24, 768)
-    wdown[:, :768] = wide[:, 0].reshape(384, 768).astype(BF)
-    wdown[:, 768:] = wide[:, 1].reshape(384, 768).astype(BF)
-
     keep = as_column(valid[...].astype(F32))
     factor = keep * (SPAN / count[0:1, 0:1])
     loads[1].wait()
@@ -1424,15 +1427,15 @@
     def with_dy(j, p):
         if p == -1:
 
-            @pl.when(j == 4)
+            pl.when(j == 5)(lambda: lead(1, 3))
+
+            def late(n, carry):
+                inputs(jnp.where(n == 0, 2, 3), jnp.where(n == 1, y, 1 - y))
+                return carry
+
+            @pl.when(j > 3)
             def _():
-                inputs(2, 1 - y)
-                inputs(3, y)
-
-            @pl.when(j == 5)
-            def _():
-                lead(1, 3)
-                inputs(3, 1 - y)
+                lax.fori_loop((j - 4) * 2, j - 2, late, 0)
 
         elif p == 0:
             pl.when((j > 0) & (j < 4))(lambda: inputs(j - 1, y))
@@ -1454,16 +1457,17 @@
             rows, dpairs[...].reshape(2048, 768), TN, preferred_element_type=F32
         ).astype(BF)
 
-    def out_grad(i):
-        col = pl.ds(i * 256, 256)
+    def out_grad(k, there):
+        i = there // 24 * 3 + k
+        col = pl.ds(pl.multiple_of(i * 256, 256), 256)
         right = dyall[:, :, col].reshape(2048, 256)
         value = lax.dot_general(zg[...].reshape(2048, 384), right, TN, preferred_element_type=F32)
-        there = i // 3 * 24
-        dwout[:, there : there + 24, (i % 3) * 256 : (i % 3) * 256 + 256] = value.reshape(16, 24, 256)
+        part_col = pl.ds(pl.multiple_of(k * 256, 256), 256)
+        dwout[:, there : there + 24, part_col] = value.reshape(16, 24, 256)
 
     def over_in(k):
         src = dwin.at[pl.ds(pl.multiple_of((1 - x) * 768 + k * 256, 256), 256)]
-        return remote(src, dwin_in.at[pl.ds(k * 256, 256)], xsend.at[5 + k], xrecv.at[5 + k], me.near("x"))
+        return remote(src, dwin_in.at[pl.ds(pl.multiple_of(k * 256, 256), 256)], xsend.at[5 + k], xrecv.at[5 + k], me.near("x"))
 
     def over_out():
         return remote(slab, dwout_in, xsend.at[8], xrecv.at[8], me.near("x"))
@@ -1492,21 +1496,31 @@
 
         @pl.when(j == 0)
         def _():
-            for k in range(3):
+            def one(k, carry):
                 in_grad((1 - x) * 3 + k)
                 over_in(k).start()
+                return carry
+
+            lax.fori_loop(0, 3, one, 0)
 
         @pl.when(j == 1)
         def _():
-            for k in range(6):
-                out_grad(k)
+            def one(k, carry):
+                out_grad(k, 0)
+                out_grad(k, 24)
+                return carry
+
+            lax.fori_loop(0, 3, one, 0)
             slab[...] = dwout[...].astype(BF)
             pl.when(c != x)(lambda: over_out().start())
 
         @pl.when(j == 2)
         def _():
-            for k in range(3):
+            def one(k, carry):
                 in_grad(x * 3 + k)
+                return carry
+
+            lax.fori_loop(0, 3, one, 0)
 
         follow(1, j)
         return carry

time: 389 us -> 382 us (0.982); the launches traced: 382 us -> 382 us
  no operation moved by 1% of the time
where the time goes in v8:
time: 382 us
  Pallas kernels  381 us (100%)
    pallas_call x1, Pallas kernels, run_experts(): pl.pallas_call(experts_kernel, out_shape=(shape((8, 128), F32), shape(wid...  175 us
    pallas_call x1, Pallas kernels, run_front(): pl.pallas_call(front_kernel, out_shape=(shape((32, 48, WIDE), BF), shape(...  104 us
    pallas_call x1, Pallas kernels, run_back(): pl.pallas_call(back_kernel, out_shape=(shape((128, 1536), F32), shape((48...  98.3 us

profile of v8, /device:TPU:0, one launch (start us, length us, event | category | flops | bytes accessed | tf_op | source)
XLA Modules:
  0.0 381.9 jit_solution(10141988323741653793)
XLA Ops:
  0.6 103.9 %front.1 = (bf16[32,48,2176]{2,1,0:T(8,128)(2,1)}, bf16[32,48,1536]{2,1,0:T(8,128)(2,1)}, bf16[32,128,512]{2,1,0:T(8,128)(2,1)}, bf16[16,48,768]{2,1,0:T(8,128)(...) custom-call(s32[1,3]{1,0:T(1,128)} %bitcast.26, ...), custom_call_target="tpu_custom_call" | custom-call | tf_op jit(solution)/shard_map/front/pallas_call | solution.py:1031
  104.5 174.6 %experts.1 = (f32[8,128]{1,0:T(8,128)}, bf16[128,1536]{1,0:T(8,128)(2,1)}, f32[128,1536]{1,0:T(8,128)}, f32[128,1536]{1,0:T(8,128)}, bf16[768,768]{1,0:T(8,128)(2,1)}, /*index=5*/bf16[16,48,768]{2,1,0:T(8,128)(2,1)}) custom-call(s32[4,128]{1,0:T(4,128)} %bitcast.22, f32[4,128]{1,0:T(4,128)} %bitcast.23, s32[1,128]{1,0:T(1,128)} %bitcast.25, ...), custom_call_target="tpu_custom_call" | custom-call | tf_op jit(solution)/shard_map/experts/pallas_call | solution.py:1562
  279.1 98.3 %back.1 = (f32[128,1536]{1,0:T(8,128)}, f32[48,1536]{1,0:T(8,128)}, f32[48,256]{1,0:T(8,128)}, f32[48,256]{1,0:T(8,128)}, f32[8,128]{1,0:T(8,128)}, /*index=5*/f...) custom-call(s32[1,3]{1,0:T(1,128)} %bitcast.27, f32[1,128]{1,0:T(1,128)} %constant.2.clone.freq_in, ...), custom_call_target="tpu_custom_call" | custom-call | tf_op jit(solution)/shard_map/back/pallas_call | solution.py:1879
  377.4 4.3 %finish.1 = (f32[1,1]{1,0:T(1,128)}, f32[1,48]{1,0:T(1,128)}, f32[1,48]{1,0:T(1,128)}, bf16[128,1536]{1,0:T(8,128)(2,1)}, f32[128,1536]{1,0:T(8,128)}, /*index=5...) custom-call(f32[8,128]{1,0:T(8,128)} %get-tuple-element.54.err_in, ...), custom_call_target="tpu_custom_call" | custom-call | tf_op jit(solution)/shard_map/finish/pallas_call | solution.py:1977

commit v9 on v8

--- a/solution.py
+++ b/solution.py
@@ -1635,7 +1635,7 @@
     )
 
 
-Q_PIECES = ((0, 768), (768, 768))
+Q_PIECES = ((0, 1536),)
 LAST = (1536, 640)
 
 
@@ -1645,8 +1645,8 @@
     doc, freq, gains, gnorm, states, h, n1, qs, o, lse, dn2, dy, gx, gout, gkv,
     wq, wo, kv, pk, pw, dos, delta, dh, dq, dkv, dqkv, gqkv, *rest,
 ):
-    sums = [(rest[i * 11 : i * 11 + 6], rest[i * 11 + 6 : i * 11 + 11]) for i in range(5)]
-    load_sem, own_sem, asend, arecv, osend, orecv = rest[55:]
+    sums = [(rest[i * 11 : i * 11 + 6], rest[i * 11 + 6 : i * 11 + 11]) for i in range(4)]
+    load_sem, own_sem, asend, arecv, osend, orecv = rest[44:]
     me = Place()
     greet_all(me)
     x, y, z, b, c = me.x, me.y, me.z, me.b, me.c
@@ -1789,8 +1789,8 @@
             pw[i * 8 : i * 8 + 8, :, start : start + width] = part.astype(BF).reshape(8, 48, width)
 
     weight_grad(0, 1536)
-    proj = [Sum(me, pw, by_weight, gqkv, *sums[2 + i], Q_PIECES[i]) for i in range(2)]
-    rest_sum = Sum(me, pw, by_weight, gqkv, *sums[4], LAST)
+    proj = [Sum(me, pw, by_weight, gqkv, *sums[2 + i], Q_PIECES[i]) for i in range(1)]
+    rest_sum = Sum(me, pw, by_weight, gqkv, *sums[3], LAST)
     for piece in proj:
         lead_all(piece)
 
@@ -1921,8 +1921,7 @@
         ]
         + Sum.room(48, 1536)
         + Sum.room(128, 512)
-        + Sum.room(48, 768)
-        + Sum.room(48, 768)
+        + Sum.room(48, 1536)
         + Sum.room(48, LAST[1])
         + [DMA((11,)), DMA((6,)), DMA((16, 2)), DMA((16, 2)), DMA((16,)), DMA((8,))],
         compiler_params=params(3, 62),

time: 382 us -> 382 us (level)
  no operation moved by 1% of the time
where the time goes in v9:
time: 382 us; the launch traced here: 381 us
  Pallas kernels  380 us (99%)
    pallas_call x1, Pallas kernels, run_experts(): pl.pallas_call(experts_kernel, out_shape=(shape((8, 128), F32), shape(wid...  175 us
    pallas_call x1, Pallas kernels, run_front(): pl.pallas_call(front_kernel, out_shape=(shape((32, 48, WIDE), BF), shape(...  104 us
    pallas_call x1, Pallas kernels, run_back(): pl.pallas_call(back_kernel, out_shape=(shape((128, 1536), F32), shape((48...  97.5 us

profile of v9, /device:TPU:0, one launch (start us, length us, event | category | flops | bytes accessed | tf_op | source)
XLA Modules:
  0.0 381.0 jit_solution(7173501519602383635)
XLA Ops:
  0.6 103.9 %front.1 = (bf16[32,48,2176]{2,1,0:T(8,128)(2,1)}, bf16[32,48,1536]{2,1,0:T(8,128)(2,1)}, bf16[32,128,512]{2,1,0:T(8,128)(2,1)}, bf16[16,48,768]{2,1,0:T(8,128)(...) custom-call(s32[1,3]{1,0:T(1,128)} %bitcast.26, ...), custom_call_target="tpu_custom_call" | custom-call | tf_op jit(solution)/shard_map/front/pallas_call | solution.py:1031
  104.5 174.6 %experts.1 = (f32[8,128]{1,0:T(8,128)}, bf16[128,1536]{1,0:T(8,128)(2,1)}, f32[128,1536]{1,0:T(8,128)}, f32[128,1536]{1,0:T(8,128)}, bf16[768,768]{1,0:T(8,128)(2,1)}, /*index=5*/bf16[16,48,768]{2,1,0:T(8,128)(2,1)}) custom-call(s32[4,128]{1,0:T(4,128)} %bitcast.22, f32[4,128]{1,0:T(4,128)} %bitcast.23, s32[1,128]{1,0:T(1,128)} %bitcast.25, ...), custom_call_target="tpu_custom_call" | custom-call | tf_op jit(solution)/shard_map/experts/pallas_call | solution.py:1562
  279.1 97.5 %back.1 = (f32[128,1536]{1,0:T(8,128)}, f32[48,1536]{1,0:T(8,128)}, f32[48,256]{1,0:T(8,128)}, f32[48,256]{1,0:T(8,128)}, f32[8,128]{1,0:T(8,128)}, /*index=5*/f...) custom-call(s32[1,3]{1,0:T(1,128)} %bitcast.27, f32[1,128]{1,0:T(1,128)} %constant.2.clone.freq_in, ...), custom_call_target="tpu_custom_call" | custom-call | tf_op jit(solution)/shard_map/back/pallas_call | solution.py:1879
  376.6 4.3 %finish.1 = (f32[1,1]{1,0:T(1,128)}, f32[1,48]{1,0:T(1,128)}, f32[1,48]{1,0:T(1,128)}, bf16[128,1536]{1,0:T(8,128)(2,1)}, f32[128,1536]{1,0:T(8,128)}, /*index=5...) custom-call(f32[8,128]{1,0:T(8,128)} %get-tuple-element.54.err_in, ...), custom_call_target="tpu_custom_call" | custom-call | tf_op jit(solution)/shard_map/finish/pallas_call | solution.py:1976
